TPU v7x, 32 devices: a whole 2x2x4 slice. The times are simulated.
32 devices in a mesh: seq: 8 (over z, x), head: 4 (over y, core).
Axes of the slice: x: 2, y: 2, z: 4, core: 2. Of those that a mesh axis runs over, the one named last changes fastest.
Arguments:
- stretch_queries: bfloat16 [1024, 8192], P(('seq', 'head')), may hold values from -40 to 40, as said below
- stretch_key_values: bfloat16 [1024, 2048], P(('seq', 'head')), may hold values from -6 to 6
- suffix_queries: bfloat16 [1024, 8192], P(('seq', 'head')), may hold values from -40 to 40, as said below
- suffix_key_values: bfloat16 [1024, 2048], P(('seq', 'head')), may hold values from -6 to 6
- prefix_key_values: bfloat16 [2048, 2048], P('seq', 'head'), may hold values from -40 to 40, as said below
- set_length: int32 [8], P('seq'), may hold values from 1 to 128, as said below
- passage_first_slot: int32 [8, 4], P('seq'), may hold values from 0 to 127, as said below
Outputs:
- stretch_out: bfloat16 [1024, 8192], P(('seq', 'head'))
- suffix_output: bfloat16 [1024, 8192], P(('seq', 'head'))
Inputs may be any that keep to these rules, and one draw needn't show every extreme that they name: `set_length`: each set has from 1 to 128 live slots; at least one set is full. `passage_first_slot`: each row starts with 0 and never falls; in some set the last passage starts at slot 127. `stretch_queries`: entries of order one, some rows larger. `suffix_queries`: entries of order one, some rows larger. `prefix_key_values`: entries of order one, some rows larger.
All inputs are finite; a program needn't handle non-finite values.
Results may differ from a plain program's by a relative error of at most 0.0095.
Values may be sent and summed in bfloat16 or wider, within the bound.
No kernel may reach another device: no remote copies, remote signals or barrier semaphores. Data moves between devices by JAX's collectives and lax.ppermute only.
A program may use at most 64 MiB of HBM per device.

v0:
```python
import jax
import jax.numpy as jnp
from jax import lax
from jax.sharding import PartitionSpec as P

HEAD_SIZE = 128


def state_update(carry, queries, keys_vals, mask):
    kv_heads = queries.shape[1]
    count = keys_vals.shape[0]
    pairs = keys_vals.reshape(count, kv_heads, 2, HEAD_SIZE)
    keys = pairs[:, :, 0]
    vals = pairs[:, :, 1]
    scores = jnp.einsum(
        "rhgd,nhd->hgrn", queries, keys, preferred_element_type=jnp.float32
    ) * HEAD_SIZE ** (-0.5)
    masked = jnp.where(mask, scores, -1e30)
    peak, total, acc = carry
    new_peak = jnp.maximum(peak, jnp.max(masked, axis=-1))
    fade = jnp.exp(peak - new_peak)
    weights = jnp.where(mask, jnp.exp(masked - new_peak[..., None]), 0.0)
    total = total * fade + jnp.sum(weights, axis=-1)
    acc = acc * fade[..., None] + jnp.einsum(
        "hgrn,nhd->hgrd", weights.astype(jnp.bfloat16), vals, preferred_element_type=jnp.float32
    )
    return (new_peak, total, acc)


def finish(state):
    peak, total, acc = state
    outs = acc / total[..., None]
    rows = outs.shape[2]
    return outs.transpose(2, 0, 1, 3).reshape(rows, -1)


def body(
    stretch_queries,
    stretch_key_values,
    suffix_queries,
    suffix_key_values,
    prefix_key_values,
    set_length,
    passage_first_slot,
):
    current_query, current_key_value, suffix_query, suffix_key_value = (
        lax.all_to_all(stretch_queries, "head", split_axis=1, concat_axis=0, tiled=True),
        lax.all_to_all(stretch_key_values, "head", split_axis=1, concat_axis=0, tiled=True),
        lax.all_to_all(suffix_queries, "head", split_axis=1, concat_axis=0, tiled=True),
        lax.all_to_all(suffix_key_values, "head", split_axis=1, concat_axis=0, tiled=True),
    )
    kv_heads = current_key_value.shape[1] // (2 * HEAD_SIZE)
    query_group = current_query.shape[1] // (kv_heads * HEAD_SIZE)
    stretch_rows = current_query.shape[0]
    suffix_rows = suffix_query.shape[0]
    prefix_rows = prefix_key_values.shape[0]
    key_rows = prefix_rows + stretch_rows
    seat = lax.axis_index("seq")
    q_pos = seat * stretch_rows + jnp.arange(stretch_rows, dtype=jnp.int32)
    stretch_heads = current_query.reshape(stretch_rows, kv_heads, query_group, HEAD_SIZE)
    suffix_head_rows = suffix_query.reshape(suffix_rows, kv_heads, query_group, HEAD_SIZE)

    def empty_state(rows):
        return (
            jnp.full((kv_heads, query_group, rows), -1e30, jnp.float32),
            jnp.zeros((kv_heads, query_group, rows), jnp.float32),
            jnp.zeros((kv_heads, query_group, rows, HEAD_SIZE), jnp.float32),
        )

    def stretch_update(carry, piece, key_pos, is_prefix):
        mask = is_prefix[None, :] | (key_pos[None, :] <= q_pos[:, None])
        return state_update(carry, stretch_heads, piece, mask)

    def suffix_update(carry, piece):
        mask = jnp.ones((suffix_rows, piece.shape[0]), dtype=bool)
        return state_update(carry, suffix_head_rows, piece, mask)

    def whole_step(carry, piece, start):
        count = piece.shape[0]
        global_row = start + jnp.arange(count, dtype=jnp.int32)
        owner = global_row // key_rows
        within = global_row % key_rows
        key_pos = owner * stretch_rows + within - prefix_rows
        return (
            stretch_update(carry[0], piece, key_pos, within < prefix_rows),
            suffix_update(carry[1], piece),
        )

    initial = (empty_state(stretch_rows), empty_state(suffix_rows))
    local_keys = jnp.concatenate([prefix_key_values, current_key_value], axis=0)
    carry = initial
    piece = lax.all_gather(local_keys, "seq", axis=0, tiled=True)
    count = piece.shape[0]
    blocks = piece.reshape(count // key_rows, key_rows, piece.shape[1])
    offsets = key_rows * jnp.arange(count // key_rows, dtype=jnp.int32)

    def scan_body(state, inputs):
        return (whole_step(state, inputs[0], inputs[1]), None)

    carry, unused = lax.scan(scan_body, carry, (blocks, offsets))
    stretch_state, suffix_running_state = carry
    slot = suffix_rows // set_length.shape[0]
    row_index = jnp.arange(suffix_rows, dtype=jnp.int32)
    slot_pos = row_index % slot
    set_of = row_index // slot
    set_pick = (
        set_of[:, None] == jnp.arange(set_length.shape[0], dtype=jnp.int32)[None, :]
    ).astype(jnp.int32)
    lengths = jnp.sum(set_pick * set_length[None, :], axis=1)
    starts = jnp.sum(set_pick[:, :, None] * passage_first_slot[None, :, :], axis=1)
    passage = jnp.sum((starts <= slot_pos[:, None]).astype(jnp.int32), axis=1) - 1
    own_rows = (
        (set_of[:, None] == set_of[None, :])
        & (slot_pos[None, :] <= slot_pos[:, None])
        & (passage[None, :] == passage[:, None])
        & (slot_pos[None, :] < lengths[:, None])
    )
    suffix_running_state = state_update(
        suffix_running_state, suffix_head_rows, suffix_key_value, own_rows
    )
    stretch_out = finish(stretch_state).astype(jnp.bfloat16)
    live = slot_pos < lengths
    suffix_output = jnp.where(live[:, None], finish(suffix_running_state), 0.0).astype(jnp.bfloat16)
    return (
        lax.all_to_all(stretch_out, "head", split_axis=0, concat_axis=1, tiled=True),
        lax.all_to_all(suffix_output, "head", split_axis=0, concat_axis=1, tiled=True),
    )


def solution(mesh):
    placed = (
        P(("seq", "head"), None),
        P(("seq", "head"), None),
        P(("seq", "head"), None),
        P(("seq", "head"), None),
        P("seq", "head"),
        P("seq"),
        P("seq", None),
    )
    return jax.shard_map(
        body,
        mesh=mesh,
        in_specs=placed,
        out_specs=(P(("seq", "head"), None), P(("seq", "head"), None)),
        check_vma=False,
    )
```

profile of v0, /device:TPU:0, one launch (start us, length us, event | category | flops | bytes accessed | tf_op | source)
XLA Modules:
  0.0 205.2 jit_solution(399244102212402696)
XLA Ops:
  8.2 8.7 %all_to_all.99 = bf16[32,4,512]{2,0,1:T(8,128)(2,1)S(1)} all-to-all(bf16[32,4,512]{2,0,1:T(8,128)(2,1)S(1)} %bitcast.163), channel_id=1, replica_groups=mesh['seq'=8,'head'=4] {'head'}, dimensions={1} | all-to-all | bytes 262144 | tf_op jit(solution)/shard_map/all_to_all | solution.py:48
  16.9 1.7 pad_maximum_fusion
  18.6 1.6 copy.103
  20.2 3.3 %all-to-all-start.4 = ((bf16[32,4,512]{2,0,1:T(8,128)(2,1)}), bf16[32,4,512]{2,0,1:T(8,128)(2,1)S(1)}, u32[]{:S(2)}, u32[]{:S(2)}) async-start(bf16[32,4,512]{2,0,1:T(8,128)(2,1)} %bitcast.114), calls=%async_computation.4 | async-start | bytes 262144 | tf_op jit(solution)/shard_map/all_to_all | solution.py:50
  23.5 1.9 copy.102
  28.1 3.5 %all-to-all-start.1 = ((bf16[32,4,2048]{2,0,1:T(8,128)(2,1)}), bf16[32,4,2048]{2,0,1:T(8,128)(2,1)S(1)}, u32[]{:S(2)}, u32[]{:S(2)}) async-start(bf16[32,4,2048]{2,0,1:T(8,128)(2,1)} %bitcast.113), calls=%async_computation.1 | async-start | bytes 1048576 | tf_op jit(solution)/shard_map/all_to_all | solution.py:47
  31.7 8.7 %all-to-all-done.1 = bf16[32,4,2048]{2,0,1:T(8,128)(2,1)S(1)} async-done(((bf16[32,4,2048]{2,0,1:T(8,128)(2,1)}), bf16[32,4,2048]{2,0,1:T(8,128)(2,1)S(1)}, u32[]{:S(2)}, u32[]{:S(2)}) %all-to-all-start.1) | async-done | bytes 524320 | tf_op jit(solution)/shard_map/all_to_all | solution.py:47
  40.4 3.5 %all-to-all-start.2 = ((bf16[32,4,2048]{2,0,1:T(8,128)(2,1)}), bf16[32,4,2048]{2,0,1:T(8,128)(2,1)S(1)}, u32[]{:S(2)}, u32[]{:S(2)}) async-start(bf16[32,4,2048]{2,0,1:T(8,128)(2,1)} %bitcast.112), calls=%async_computation.2 | async-start | bytes 1048576 | tf_op jit(solution)/shard_map/all_to_all | solution.py:49
  46.9 5.8 %all-to-all-done.2 = bf16[32,4,2048]{2,0,1:T(8,128)(2,1)S(1)} async-done(((bf16[32,4,2048]{2,0,1:T(8,128)(2,1)}), bf16[32,4,2048]{2,0,1:T(8,128)(2,1)S(1)}, u32[]{:S(2)}, u32[]{:S(2)}) %all-to-all-start.2) | async-done | bytes 524320 | tf_op jit(solution)/shard_map/all_to_all | solution.py:49
  53.7 1.9 fusion.55
  55.6 23.9 %all-gather.2.cloned.1.call-done = bf16[3072,512]{1,0:T(8,128)(2,1)} async-done(((bf16[384,512]{1,0:T(8,128)(2,1)}), bf16[3072,512]{1,0:T(8,128)(2,1)}) %all-gather.2.cloned.1.call-update) | async-done | bytes 3145744 | tf_op jit(solution)/shard_map/all_gather | solution.py:92
  79.5 90.3 %while.23 = (s32[]{:T(128)}, f32[2,8,128]{2,1,0:T(8,128)}, f32[2,8,128]{2,1,0:T(8,128)}, f32[2,8,128,128]{3,2,1,0:T(8,128)}, f32[2,8,128]{2,1,0:T(8,128)S(1)}, /...) while((s32[]{:T(128)}, f32[2,8,128]{2,1,0:T(8,128)}, ...), condition=%wide.region_5.6_spmd.clone, body=%wide.region_0.5_spmd.clone.sunk | while | flops 823522432 | bytes 45978984 | solution.py:100
  80.8 1.7 bitcast_reduce_fusion.2
  92.0 1.7 bitcast_reduce_fusion.2
  98.5 1.4 fusion.76
  103.3 1.7 bitcast_reduce_fusion.2
  109.8 1.4 fusion.76
  114.6 1.7 bitcast_reduce_fusion.2
  121.1 1.4 fusion.76
  125.9 1.7 bitcast_reduce_fusion.2
  132.4 1.4 fusion.76
  137.2 1.7 bitcast_reduce_fusion.2
  143.7 1.4 fusion.76
  148.5 1.7 bitcast_reduce_fusion.2
  154.9 1.4 fusion.76
  159.8 1.7 bitcast_reduce_fusion.2
  166.2 1.4 fusion.76
  169.9 1.7 fusion.43
  173.0 3.5 %all-to-all-start.3 = ((bf16[4,32,2048]{2,1,0:T(8,128)(2,1)}), bf16[4,32,2048]{2,1,0:T(8,128)(2,1)S(1)}, u32[]{:S(2)}, u32[]{:S(2)}) async-start(bf16[4,32,2048]{2,1,0:T(8,128)(2,1)} %convert_element_type.43), calls=%async_computation.3 | async-start | bytes 1048576 | tf_op jit(solution)/shard_map/all_to_all | solution.py:125
  179.3 6.0 %all-to-all-done.3 = bf16[4,32,2048]{2,1,0:T(8,128)(2,1)S(1)} async-done(((bf16[4,32,2048]{2,1,0:T(8,128)(2,1)}), bf16[4,32,2048]{2,1,0:T(8,128)(2,1)S(1)}, u32[]{:S(2)}, u32[]{:S(2)}) %all-to-all-start.3) | async-done | bytes 524320 | tf_op jit(solution)/shard_map/all_to_all | solution.py:125
  185.3 3.5 %all-to-all-start.5 = ((bf16[4,32,2048]{2,1,0:T(8,128)(2,1)}), bf16[4,32,2048]{2,1,0:T(8,128)(2,1)S(1)}, u32[]{:S(2)}, u32[]{:S(2)}) async-start(bf16[4,32,2048]{2,1,0:T(8,128)(2,1)} %select_convert_fusion), calls=%async_computation.5 | async-start | bytes 1048576 | tf_op jit(solution)/shard_map/all_to_all | solution.py:126
  189.6 8.0 %all-to-all-done.5 = bf16[4,32,2048]{2,1,0:T(8,128)(2,1)S(1)} async-done(((bf16[4,32,2048]{2,1,0:T(8,128)(2,1)}), bf16[4,32,2048]{2,1,0:T(8,128)(2,1)S(1)}, u32[]{:S(2)}, u32[]{:S(2)}) %all-to-all-start.5) | async-done | bytes 524320 | tf_op jit(solution)/shard_map/all_to_all | solution.py:126
  (361 shorter events, 78.1 us)
Async XLA Ops:
  7.2 18.2 %copy-start.8 = (bf16[32,8192]{1,0:T(8,128)(2,1)S(1)}, bf16[32,8192]{1,0:T(8,128)(2,1)}, u32[]{:S(2)}) copy-start(bf16[32,8192]{1,0:T(8,128)(2,1)} %param.11) | copy-start | bytes 1572868
  7.2 19.7 %copy-start.19 = (s32[1,4]{1,0:T(1,128)S(1)}, s32[1,4]{1,0:T(1,128)}, u32[]{:S(2)}) copy-start(s32[1,4]{1,0:T(1,128)} %param.15) | copy-start | bytes 52
  7.2 72.3 %all-gather.2.cloned.1.call-start = ((), (), s32[]{:S(2)}) async-start(), calls=%async_computation.6 | async-start | bytes 3538944 | tf_op jit(solution)/shard_map/all_gather | solution.py:92
  20.2 7.9 %all-to-all-start.4 = ((bf16[32,4,512]{2,0,1:T(8,128)(2,1)}), bf16[32,4,512]{2,0,1:T(8,128)(2,1)S(1)}, u32[]{:S(2)}, u32[]{:S(2)}) async-start(bf16[32,4,512]{2,0,1:T(8,128)(2,1)} %bitcast.114), calls=%async_computation.4 | async-start | bytes 262144 | tf_op jit(solution)/shard_map/all_to_all | solution.py:50
  28.1 12.3 %all-to-all-start.1 = ((bf16[32,4,2048]{2,0,1:T(8,128)(2,1)}), bf16[32,4,2048]{2,0,1:T(8,128)(2,1)S(1)}, u32[]{:S(2)}, u32[]{:S(2)}) async-start(bf16[32,4,2048]{2,0,1:T(8,128)(2,1)} %bitcast.113), calls=%async_computation.1 | async-start | bytes 1048576 | tf_op jit(solution)/shard_map/all_to_all | solution.py:47
  31.7 23.9 %copy-start.14 = (pred[128,128]{0,1:T(8,128)(4,1)}, pred[128,128]{0,1:T(8,128)(4,1)S(1)}, u32[]{:S(2)}) copy-start(pred[128,128]{0,1:T(8,128)(4,1)S(1)} %compare_and_fusion) | copy-start | bytes 49156
  40.4 12.3 %all-to-all-start.2 = ((bf16[32,4,2048]{2,0,1:T(8,128)(2,1)}), bf16[32,4,2048]{2,0,1:T(8,128)(2,1)S(1)}, u32[]{:S(2)}, u32[]{:S(2)}) async-start(bf16[32,4,2048]{2,0,1:T(8,128)(2,1)} %bitcast.112), calls=%async_computation.2 | async-start | bytes 1048576 | tf_op jit(solution)/shard_map/all_to_all | solution.py:49
  82.4 2.6 %copy-start.3 = (bf16[128,2,8,128]{3,0,2,1:T(8,128)(2,1)S(1)}, bf16[128,2,8,128]{3,0,2,1:T(8,128)(2,1)}, u32[]{:S(2)}) copy-start(bf16[128,2,8,128]{3,0,2,1:T(8,128)(2,1)} %get-tuple-element.410) | copy-start | bytes 1572868 | tf_op jit(solution)/shard_map/while
  82.5 3.3 %copy-start.7 = (f32[2,8,128]{2,1,0:T(8,128)S(1)}, f32[2,8,128]{2,1,0:T(8,128)}, u32[]{:S(2)}) copy-start(f32[2,8,128]{2,1,0:T(8,128)} %get-tuple-element.388) | copy-start | bytes 24580 | tf_op jit(solution)/shard_map/while
  93.7 2.6 %copy-start.3 = (bf16[128,2,8,128]{3,0,2,1:T(8,128)(2,1)S(1)}, bf16[128,2,8,128]{3,0,2,1:T(8,128)(2,1)}, u32[]{:S(2)}) copy-start(bf16[128,2,8,128]{3,0,2,1:T(8,128)(2,1)} %get-tuple-element.410) | copy-start | bytes 1572868 | tf_op jit(solution)/shard_map/while
  93.8 3.3 %copy-start.7 = (f32[2,8,128]{2,1,0:T(8,128)S(1)}, f32[2,8,128]{2,1,0:T(8,128)}, u32[]{:S(2)}) copy-start(f32[2,8,128]{2,1,0:T(8,128)} %get-tuple-element.388) | copy-start | bytes 24580 | tf_op jit(solution)/shard_map/while
  105.0 2.6 %copy-start.3 = (bf16[128,2,8,128]{3,0,2,1:T(8,128)(2,1)S(1)}, bf16[128,2,8,128]{3,0,2,1:T(8,128)(2,1)}, u32[]{:S(2)}) copy-start(bf16[128,2,8,128]{3,0,2,1:T(8,128)(2,1)} %get-tuple-element.410) | copy-start | bytes 1572868 | tf_op jit(solution)/shard_map/while
  105.1 3.3 %copy-start.7 = (f32[2,8,128]{2,1,0:T(8,128)S(1)}, f32[2,8,128]{2,1,0:T(8,128)}, u32[]{:S(2)}) copy-start(f32[2,8,128]{2,1,0:T(8,128)} %get-tuple-element.388) | copy-start | bytes 24580 | tf_op jit(solution)/shard_map/while
  116.3 2.6 %copy-start.3 = (bf16[128,2,8,128]{3,0,2,1:T(8,128)(2,1)S(1)}, bf16[128,2,8,128]{3,0,2,1:T(8,128)(2,1)}, u32[]{:S(2)}) copy-start(bf16[128,2,8,128]{3,0,2,1:T(8,128)(2,1)} %get-tuple-element.410) | copy-start | bytes 1572868 | tf_op jit(solution)/shard_map/while
  116.3 3.3 %copy-start.7 = (f32[2,8,128]{2,1,0:T(8,128)S(1)}, f32[2,8,128]{2,1,0:T(8,128)}, u32[]{:S(2)}) copy-start(f32[2,8,128]{2,1,0:T(8,128)} %get-tuple-element.388) | copy-start | bytes 24580 | tf_op jit(solution)/shard_map/while
  118.9 2.1 %copy-start.5 = (f32[2,8,128,128]{3,2,1,0:T(8,128)S(1)}, f32[2,8,128,128]{3,2,1,0:T(8,128)}, u32[]{:S(2)}) copy-start(f32[2,8,128,128]{3,2,1,0:T(8,128)} %get-tuple-element.390) | copy-start | bytes 3145732 | tf_op jit(solution)/shard_map/while
  127.6 2.6 %copy-start.3 = (bf16[128,2,8,128]{3,0,2,1:T(8,128)(2,1)S(1)}, bf16[128,2,8,128]{3,0,2,1:T(8,128)(2,1)}, u32[]{:S(2)}) copy-start(bf16[128,2,8,128]{3,0,2,1:T(8,128)(2,1)} %get-tuple-element.410) | copy-start | bytes 1572868 | tf_op jit(solution)/shard_map/while
  127.6 3.3 %copy-start.7 = (f32[2,8,128]{2,1,0:T(8,128)S(1)}, f32[2,8,128]{2,1,0:T(8,128)}, u32[]{:S(2)}) copy-start(f32[2,8,128]{2,1,0:T(8,128)} %get-tuple-element.388) | copy-start | bytes 24580 | tf_op jit(solution)/shard_map/while
  138.9 2.6 %copy-start.3 = (bf16[128,2,8,128]{3,0,2,1:T(8,128)(2,1)S(1)}, bf16[128,2,8,128]{3,0,2,1:T(8,128)(2,1)}, u32[]{:S(2)}) copy-start(bf16[128,2,8,128]{3,0,2,1:T(8,128)(2,1)} %get-tuple-element.410) | copy-start | bytes 1572868 | tf_op jit(solution)/shard_map/while
  138.9 3.3 %copy-start.7 = (f32[2,8,128]{2,1,0:T(8,128)S(1)}, f32[2,8,128]{2,1,0:T(8,128)}, u32[]{:S(2)}) copy-start(f32[2,8,128]{2,1,0:T(8,128)} %get-tuple-element.388) | copy-start | bytes 24580 | tf_op jit(solution)/shard_map/while
  150.2 2.6 %copy-start.3 = (bf16[128,2,8,128]{3,0,2,1:T(8,128)(2,1)S(1)}, bf16[128,2,8,128]{3,0,2,1:T(8,128)(2,1)}, u32[]{:S(2)}) copy-start(bf16[128,2,8,128]{3,0,2,1:T(8,128)(2,1)} %get-tuple-element.410) | copy-start | bytes 1572868 | tf_op jit(solution)/shard_map/while
  150.2 3.3 %copy-start.7 = (f32[2,8,128]{2,1,0:T(8,128)S(1)}, f32[2,8,128]{2,1,0:T(8,128)}, u32[]{:S(2)}) copy-start(f32[2,8,128]{2,1,0:T(8,128)} %get-tuple-element.388) | copy-start | bytes 24580 | tf_op jit(solution)/shard_map/while
  161.5 2.6 %copy-start.3 = (bf16[128,2,8,128]{3,0,2,1:T(8,128)(2,1)S(1)}, bf16[128,2,8,128]{3,0,2,1:T(8,128)(2,1)}, u32[]{:S(2)}) copy-start(bf16[128,2,8,128]{3,0,2,1:T(8,128)(2,1)} %get-tuple-element.410) | copy-start | bytes 1572868 | tf_op jit(solution)/shard_map/while
  161.5 3.3 %copy-start.7 = (f32[2,8,128]{2,1,0:T(8,128)S(1)}, f32[2,8,128]{2,1,0:T(8,128)}, u32[]{:S(2)}) copy-start(f32[2,8,128]{2,1,0:T(8,128)} %get-tuple-element.388) | copy-start | bytes 24580 | tf_op jit(solution)/shard_map/while
  169.8 6.6 %copy-start.17 = (f32[2,8,128]{2,1,0:T(8,128)S(1)}, f32[2,8,128]{2,1,0:T(8,128)}, u32[]{:S(2)}) copy-start(f32[2,8,128]{2,1,0:T(8,128)} %get-tuple-element.280) | copy-start | bytes 24580
  169.8 6.6 %copy-start.4 = (f32[2,8,128,128]{2,3,1,0:T(8,128)S(1)}, f32[2,8,128,128]{2,3,1,0:T(8,128)}, u32[]{:S(2)}) copy-start(f32[2,8,128,128]{2,3,1,0:T(8,128)} %get-tuple-element.281) | copy-start | bytes 3145732
  169.8 6.6 %copy-start.15 = (pred[128,128]{0,1:T(8,128)(4,1)S(1)}, pred[128,128]{0,1:T(8,128)(4,1)}, u32[]{:S(2)}) copy-start(pred[128,128]{0,1:T(8,128)(4,1)} %copy-done.14) | copy-start | bytes 49156
  169.9 6.8 %copy-start.13 = (f32[2,8,128]{2,1,0:T(8,128)S(1)}, f32[2,8,128]{2,1,0:T(8,128)}, u32[]{:S(2)}) copy-start(f32[2,8,128]{2,1,0:T(8,128)} %get-tuple-element.163) | copy-start | bytes 24580
  169.9 6.9 %copy-start.2 = (f32[2,8,128,128]{3,2,1,0:T(8,128)S(1)}, f32[2,8,128,128]{3,2,1,0:T(8,128)}, u32[]{:S(2)}) copy-start(f32[2,8,128,128]{3,2,1,0:T(8,128)} %get-tuple-element.161) | copy-start | bytes 3145732
  169.9 6.9 %copy-start.16 = (bf16[128,2,1,128]{3,2,1,0:T(2,128)(2,1)S(1)}, bf16[128,2,1,128]{3,2,1,0:T(2,128)(2,1)}, u32[]{:S(2)}) copy-start(bf16[128,2,1,128]{3,2,1,0:T(2,128)(2,1)} %get-tuple-element.278) | copy-start | bytes 196612
  173.0 12.3 %all-to-all-start.3 = ((bf16[4,32,2048]{2,1,0:T(8,128)(2,1)}), bf16[4,32,2048]{2,1,0:T(8,128)(2,1)S(1)}, u32[]{:S(2)}, u32[]{:S(2)}) async-start(bf16[4,32,2048]{2,1,0:T(8,128)(2,1)} %convert_element_type.43), calls=%async_computation.3 | async-start | bytes 1048576 | tf_op jit(solution)/shard_map/all_to_all | solution.py:125
  185.3 12.3 %all-to-all-start.5 = ((bf16[4,32,2048]{2,1,0:T(8,128)(2,1)}), bf16[4,32,2048]{2,1,0:T(8,128)(2,1)S(1)}, u32[]{:S(2)}, u32[]{:S(2)}) async-start(bf16[4,32,2048]{2,1,0:T(8,128)(2,1)} %select_convert_fusion), calls=%async_computation.5 | async-start | bytes 1048576 | tf_op jit(solution)/shard_map/all_to_all | solution.py:126
  (72 other events, 107.6 us)
Sparse Core Ops, SparseCore 0:
  18.7 60.7 all-gather.1
where the time goes:
time: 207 us; the launch traced here: 205 us
  waiting for transfers between devices  53.4 us (26%)
  matrix products  42.1 us (20%)
  local copies, waits for them, and re-layouts  39.6 us (19%)
  other arithmetic  27.2 us (13%)
  starting transfers between devices  17.2 us (8%)
  between operations  15 us (7%)
  blocking collectives  8.67 us (4%)
    all_gather x1, waiting for transfers between devices, body(): piece = lax.all_gather(local_keys, 'seq', axis=0, tiled=True)  23.9 us
    dot_general x17, matrix products, state_update(): jnp.einsum('hgrn,nhd->hgrd', weights.astype(jnp.bfloat16), vals, preferre...  21.4 us
    dot_general x17, matrix products, state_update(): jnp.einsum('rhgd,nhd->hgrn', queries, keys, preferred_element_type=jnp.fl...  20.7 us
    dynamic_slice x24, local copies, waits for them, and re-layouts, body(): carry, unused = lax.scan(scan_body, carry, (blocks, offsets))  14.4 us
    while x192, local copies, waits for them, and re-layouts  13.4 us
    reduce_sum x17, other arithmetic, state_update(): total = total * fade + jnp.sum(weights, axis=-1)  10.6 us
    all_to_all x1, blocking collectives, body(): lax.all_to_all(stretch_key_values, 'head', split_axis=1, concat_axis=0, t...  8.67 us
    all_to_all x1, waiting for transfers between devices, body(): lax.all_to_all(stretch_queries, 'head', split_axis=1, concat_axis=0, tile...  8.66 us
  transfers between devices with their start and end apart: 6, of which 6 were waited for; matrix products, arithmetic and copies ran while one was open for 7% of the time, Pallas kernels for 0%

commit v1 on v0

v1 whole, which is shorter than its diff:
```python
import functools
import math

import jax
import jax.numpy as jnp
import numpy as np
from jax import lax
from jax.experimental import pallas as pl
from jax.experimental.pallas import tpu as pltpu
from jax.sharding import PartitionSpec as P

HEAD_SIZE = 128
GROUP = 8
PAIR = 2 * HEAD_SIZE
RATE = HEAD_SIZE ** (-0.5) * math.log2(math.e)
LOW = -1e30
VMEM_LIMIT = 40 * 1024 * 1024


def ring_order(count):
    wide = max(1, math.isqrt(count // 2))
    if count % wide or wide % 2 or wide < 2:
        return list(range(count))
    tall = count // wide
    order = [z * wide for z in range(tall)]
    for step, z in enumerate(reversed(range(tall))):
        row = [z * wide + x for x in range(1, wide)]
        order += row if step % 2 == 0 else row[::-1]
    return order


def split_columns(me, arrays, peers):
    rows = [a.shape[0] for a in arrays]
    cols = arrays[0].shape[1] // peers
    total = sum(rows)

    def kernel(me_ref, *refs):
        ins, outs = refs[: len(arrays)], refs[len(arrays) :]
        for r in range(peers):
            start = pl.multiple_of((me_ref[0] ^ r) * cols, HEAD_SIZE)
            top = 0
            for ref, count in zip(ins, rows):
                outs[r][top : top + count, :] = ref[:, pl.ds(start, cols)]
                top += count

    return pl.pallas_call(
        kernel,
        out_shape=[jax.ShapeDtypeStruct((total, cols), arrays[0].dtype)] * peers,
        in_specs=[pl.BlockSpec(memory_space=pltpu.SMEM)] + [pl.BlockSpec(memory_space=pltpu.VMEM)] * len(arrays),
        out_specs=[pl.BlockSpec(memory_space=pltpu.VMEM)] * peers,
        name="split_columns",
    )(me, *arrays)


def join_columns(me, chunks, rows):
    parts, peers = len(chunks), len(chunks[0])
    cols = chunks[0][0].shape[1]
    outs_count = chunks[0][0].shape[0] // rows
    flat = [c for part in chunks for c in part]

    def kernel(me_ref, *refs):
        ins, outs = refs[: len(flat)], refs[len(flat) :]
        for part in range(parts):
            for r in range(peers):
                start = pl.multiple_of((me_ref[0] ^ r) * (cols * parts) + part * cols, HEAD_SIZE)
                for o in range(outs_count):
                    outs[o][:, pl.ds(start, cols)] = ins[part * peers + r][o * rows : (o + 1) * rows, :]

    return pl.pallas_call(
        kernel,
        out_shape=[jax.ShapeDtypeStruct((rows, cols * parts * peers), flat[0].dtype)] * outs_count,
        in_specs=[pl.BlockSpec(memory_space=pltpu.SMEM)] + [pl.BlockSpec(memory_space=pltpu.VMEM)] * len(flat),
        out_specs=[pl.BlockSpec(memory_space=pltpu.VMEM)] * outs_count,
        name="join_columns",
    )(me, *flat)


def attend(info, queries, carry, prefixes, stretches, flags, own, last, split=4):
    peers = len(queries)
    tokens = queries[0].shape[0] // 2
    seat_tokens = peers * tokens
    heads = prefixes[0].shape[1] // PAIR
    groups = GROUP // split
    block = groups * seat_tokens
    pieces = list(prefixes) + list(stretches) + (list(own) if own else [])
    sizes = [p.shape[0] for p in pieces]
    keys = sum(sizes)
    n_prefix = sum(p.shape[0] for p in prefixes)
    n_common = n_prefix + sum(p.shape[0] for p in stretches)
    n_in = 1 + peers + len(pieces) + (2 if carry else 0)

    def kernel(*refs):
        info_ref = refs[0]
        q_refs = refs[1 : 1 + peers]
        piece_refs = refs[1 + peers : 1 + peers + len(pieces)]
        carry_refs = refs[1 + peers + len(pieces) : n_in]
        out_refs = refs[n_in:-2]
        k_ref, v_ref = refs[-2:]
        me = info_ref[0]

        @pl.when(pl.program_id(1) == 0)
        def _():
            top = 0
            for ref, size in zip(piece_refs, sizes):
                k_ref[top : top + size, :] = ref[:, :HEAD_SIZE]
                v_ref[top : top + size, :HEAD_SIZE] = ref[:, HEAD_SIZE:]
                top += size
            v_ref[:, HEAD_SIZE:] = jnp.ones((keys, HEAD_SIZE), jnp.bfloat16)

        def positions(axis):
            index = lax.broadcasted_iota(jnp.int32, (seat_tokens, seat_tokens), axis)
            return (me ^ (index // tokens)) * tokens + index % tokens

        row_pos = col_pos = None
        if own or last:
            row_pos = positions(0)
        if own:
            col_pos = positions(1)

        def scores(q, low, high):
            return lax.dot_general(
                q, k_ref[low:high, :], (((1,), (1,)), ((), ())), preferred_element_type=jnp.float32
            )

        for kind in range(2):
            q = jnp.concatenate(
                [
                    q_refs[r][kind * tokens : (kind + 1) * tokens, g * HEAD_SIZE : (g + 1) * HEAD_SIZE]
                    for g in range(groups)
                    for r in range(peers)
                ],
                axis=0,
            )
            spans = [(0, n_prefix, None)]
            top = n_prefix
            if kind == 0:
                for piece, flag in zip(stretches, flags):
                    spans.append((top, top + piece.shape[0], info_ref[flag] > 0))
                    top += piece.shape[0]
            else:
                spans = [(0, n_common + (seat_tokens if own else 0), None)]
            if own:
                if kind == 0:
                    allowed = col_pos <= row_pos
                    low, high = n_common, n_common + seat_tokens
                else:
                    row_set = col_set = jnp.zeros((seat_tokens, seat_tokens), jnp.int32)
                    for slot in range(4):
                        row_set += (info_ref[2 + slot] <= row_pos).astype(jnp.int32)
                        col_set += (info_ref[2 + slot] <= col_pos).astype(jnp.int32)
                    allowed = (col_pos <= row_pos) & (row_set == col_set) & (col_pos < info_ref[1])
                    low, high = n_common + seat_tokens, n_common + 2 * seat_tokens
                spans.append((low, high, allowed))
            parts = []
            for low, high, allowed in spans:
                if low == high:
                    continue
                s = scores(q, low, high)
                if allowed is not None:
                    if allowed.ndim == 2:
                        s = jnp.where(allowed[None], s.reshape(groups, seat_tokens, high - low), LOW)
                        s = s.reshape(block, high - low)
                    else:
                        s = jnp.where(allowed, s, LOW)
                parts.append((low, high, s))
            peak = functools.reduce(jnp.maximum, [jnp.max(s, axis=1, keepdims=True) for _, _, s in parts])
            if carry:
                stats = carry_refs[1][0, kind]
                old = stats[:, :1]
                peak = jnp.maximum(old, peak)
                fade = jnp.exp2((old - peak) * RATE)
                acc = carry_refs[0][0, kind] * fade
                total = stats[:, HEAD_SIZE // 2 : HEAD_SIZE // 2 + 1] * fade
            else:
                acc = total = None
            for low, high, s in parts:
                weights = jnp.exp2((s - peak) * RATE).astype(jnp.bfloat16)
                both = jnp.dot(weights, v_ref[low:high, :], preferred_element_type=jnp.float32)
                if acc is None:
                    acc, total = both[:, :HEAD_SIZE], both[:, HEAD_SIZE:]
                else:
                    acc = acc + both[:, :HEAD_SIZE]
                    total = total + both[:, HEAD_SIZE:]
            if last:
                result = acc / total
                if kind == 1:
                    live = (row_pos < info_ref[1])[:, :HEAD_SIZE]
                    result = jnp.where(
                        live[None], result.reshape(groups, seat_tokens, HEAD_SIZE), 0.0
                    ).reshape(block, HEAD_SIZE)
                result = result.astype(jnp.bfloat16)
                for g in range(groups):
                    for r in range(peers):
                        row = g * seat_tokens + r * tokens
                        out_refs[r][kind * tokens : (kind + 1) * tokens, g * HEAD_SIZE : (g + 1) * HEAD_SIZE] = (
                            result[row : row + tokens]
                        )
            else:
                out_refs[0][0, kind] = acc
                lane = lax.broadcasted_iota(jnp.int32, (block, HEAD_SIZE), 1)
                out_refs[1][0, kind] = jnp.where(lane < HEAD_SIZE // 2, peak, total)

    state_spec = pl.BlockSpec((1, 2, block, HEAD_SIZE), lambda h, b: (h, 0, b, 0))
    state_shape = jax.ShapeDtypeStruct((heads, 2, GROUP * seat_tokens, HEAD_SIZE), jnp.float32)
    q_spec = pl.BlockSpec((2 * tokens, groups * HEAD_SIZE), lambda h, b: (0, h * split + b))
    in_specs = (
        [pl.BlockSpec(memory_space=pltpu.SMEM)]
        + [q_spec] * peers
        + [pl.BlockSpec((size, PAIR), lambda h, b: (0, h)) for size in sizes]
        + ([state_spec] * 2 if carry else [])
    )
    if last:
        out_shape = [jax.ShapeDtypeStruct(q.shape, jnp.bfloat16) for q in queries]
        out_specs = [q_spec] * peers
    else:
        out_shape = [state_shape] * 2
        out_specs = [state_spec] * 2
    rows = heads * GROUP * seat_tokens * 2
    return pl.pallas_call(
        kernel,
        grid=(heads, split),
        in_specs=in_specs,
        out_specs=out_specs,
        out_shape=out_shape,
        scratch_shapes=[
            pltpu.VMEM((keys, HEAD_SIZE), jnp.bfloat16),
            pltpu.VMEM((keys, PAIR), jnp.bfloat16),
        ],
        compiler_params=pltpu.CompilerParams(vmem_limit_bytes=VMEM_LIMIT),
        cost_estimate=pl.CostEstimate(
            flops=rows * keys * HEAD_SIZE * 8, bytes_accessed=rows * HEAD_SIZE * 8, transcendentals=rows * keys
        ),
        name="attend",
    )(info, *queries, *pieces, *(carry if carry else ()))


def body(
    stretch_queries,
    stretch_key_values,
    suffix_queries,
    suffix_key_values,
    prefix_key_values,
    set_length,
    passage_first_slot,
    *,
    peers,
    seats,
):
    tokens = stretch_queries.shape[0]
    me = lax.axis_index("head").astype(jnp.int32)
    seat = lax.axis_index("seq").astype(jnp.int32)
    order = ring_order(seats)
    place = {s: i for i, s in enumerate(order)}
    right = [(order[i], order[(i + 1) % seats]) for i in range(seats)]
    left = [(b, a) for a, b in right]
    across = [[(h, h ^ r) for h in range(peers)] for r in range(peers)]
    half = seats // 2

    table = np.zeros((seats, 2 * half), np.int32)
    for s in range(seats):
        for k in range(1, half + 1):
            table[s, 2 * k - 2] = order[(place[s] - k) % seats] < s
            table[s, 2 * k - 1] = order[(place[s] + k) % seats] < s
    sees = lax.dynamic_slice_in_dim(jnp.asarray(table), seat, 1, 0)[0]
    me = me[None]
    info = jnp.concatenate([me, set_length, passage_first_slot[0], sees])
    first_flag = 2 + passage_first_slot.shape[1]

    def around(first):
        from_left, from_right = first, first
        arrived = []
        for step in range(1, half + 1):
            if step == half:
                cut = first.shape[0] // 2
                from_left, from_right = from_left[:cut], from_right[cut:]
            from_left = lax.ppermute(from_left, "seq", right)
            from_right = lax.ppermute(from_right, "seq", left)
            arrived.append((from_left, from_right))
        return arrived

    key_value_chunks = split_columns(me, [stretch_key_values, suffix_key_values], peers)
    key_value_chunks = [key_value_chunks[0]] + [
        lax.ppermute(key_value_chunks[r], "head", across[r]) for r in range(1, peers)
    ]
    queries = split_columns(me, [stretch_queries, suffix_queries], peers)
    queries = [queries[0]] + [lax.ppermute(queries[r], "head", across[r]) for r in range(1, peers)]
    own_stretch = jnp.concatenate([c[:tokens] for c in key_value_chunks], axis=0)
    own_suffix = jnp.concatenate([c[tokens:] for c in key_value_chunks], axis=0)

    prefix = around(prefix_key_values)
    stretch = around(own_stretch)

    def update(carry, first, stop, own, last):
        prefixes = [p for k in range(first, stop) for p in prefix[k]]
        stretches = [p for k in range(first, stop) for p in stretch[k]]
        flags = [first_flag + 2 * k + side for k in range(first, stop) for side in range(2)]
        if own:
            prefixes = [prefix_key_values] + prefixes
        return attend(info, queries, carry, prefixes, stretches, flags, own, last)

    early = max(1, half - 2)
    carry = update(None, 0, early, (own_stretch, own_suffix), False)
    if half - 1 > early:
        carry = update(carry, early, half - 1, None, False)
    outs = update(carry, half - 1, half, None, True)
    outs = [outs[0]] + [lax.ppermute(outs[r], "head", across[r]) for r in range(1, peers)]
    return tuple(join_columns(me, [outs], tokens))


def solution(mesh):
    placed = (
        P(("seq", "head"), None),
        P(("seq", "head"), None),
        P(("seq", "head"), None),
        P(("seq", "head"), None),
        P("seq", "head"),
        P("seq"),
        P("seq", None),
    )
    return jax.shard_map(
        functools.partial(body, peers=mesh.shape["head"], seats=mesh.shape["seq"]),
        mesh=mesh,
        in_specs=placed,
        out_specs=(P(("seq", "head"), None), P(("seq", "head"), None)),
        check_vma=False,
    )
```

time: 207 us -> 99.7 us (0.48)
  Pallas kernels: 0 us -> 42.7 us
  matrix products: 42.1 us -> 0 us
  local copies, waits for them, and re-layouts: 39.6 us -> 3.88 us
  other arithmetic: 27.2 us -> 0.1 us
  waiting for transfers between devices: 53.4 us -> 26.9 us
  between operations: 15 us -> 1.47 us
  blocking collectives: 8.67 us -> 0 us
  starting transfers between devices: 17.2 us -> 24.3 us
    pallas_call x0 -> x6, Pallas kernels: none -> 42.7 us  [the longest x3 36.6 us: attend(): pl.pallas_call(kernel, grid=(heads, split), in_specs=in_specs, out_specs=...]
    dot_general x34 -> x0, matrix products: 42.1 us -> none  [the longest x17 21.4 us: state_update(): jnp.einsum('hgrn,nhd->hgrd', weights.astype(jnp.bfloat16), vals, preferre...]
    all_to_all x5 -> x0, waiting for transfers between devices: 29.5 us -> none  [the longest x1 8.66 us: body(): lax.all_to_all(stretch_queries, 'head', split_axis=1, concat_axis=0, tile...]
    ppermute x0 -> x25, waiting for transfers between devices: none -> 26.9 us  [the longest x3 12.1 us: body(): lax.ppermute(outs[r], 'head', across[r])]
    ppermute x0 -> x25, starting transfers between devices: none -> 24.3 us  [the longest x8 11.7 us: around(): from_left = lax.ppermute(from_left, 'seq', right)]
    all_gather x1 -> x0, waiting for transfers between devices: 23.9 us -> none  [body(): piece = lax.all_gather(local_keys, 'seq', axis=0, tiled=True)]
    all_to_all x5 -> x0, starting transfers between devices: 17.2 us -> none  [the longest x1 3.47 us: body(): lax.all_to_all(stretch_queries, 'head', split_axis=1, concat_axis=0, tile...]
    dynamic_slice x24 -> x0, local copies, waits for them, and re-layouts: 14.4 us -> none  [body(): carry, unused = lax.scan(scan_body, carry, (blocks, offsets))]
  transfers between devices with their start and end apart: 6 -> 25, of which waited for: 6 -> 9; matrix products, arithmetic and copies ran while one was open for 7% -> 2% of each run, Pallas kernels for 0% -> 27%
where the time goes in v1:
time: 99.7 us; the launch traced here: 99.3 us
  Pallas kernels  42.7 us (43%)
  waiting for transfers between devices  26.9 us (27%)
  starting transfers between devices  24.3 us (24%)
  local copies, waits for them, and re-layouts  3.88 us (4%)
  between operations  1.47 us (1%)
    pallas_call x3, Pallas kernels, attend(): pl.pallas_call(kernel, grid=(heads, split), in_specs=in_specs, out_specs=...  36.6 us
    ppermute x3, waiting for transfers between devices, body(): lax.ppermute(outs[r], 'head', across[r])  12.1 us
    ppermute x8, starting transfers between devices, around(): from_left = lax.ppermute(from_left, 'seq', right)  11.7 us
    ppermute x8, waiting for transfers between devices, around(): from_left = lax.ppermute(from_left, 'seq', right)  7.97 us
    ppermute x8, starting transfers between devices, around(): from_right = lax.ppermute(from_right, 'seq', left)  5.73 us
    pallas_call x2, Pallas kernels, split_columns(): pl.pallas_call(kernel, out_shape=[jax.ShapeDtypeStruct((total, cols), arr...  3.92 us
    ppermute x3, waiting for transfers between devices, body(): lax.ppermute(queries[r], 'head', across[r])  3.44 us
    ppermute x3, waiting for transfers between devices, body(): lax.ppermute(key_value_chunks[r], 'head', across[r])  3.34 us
  transfers between devices with their start and end apart: 25, of which 9 were waited for; matrix products, arithmetic and copies ran while one was open for 2% of the time, Pallas kernels for 27%

profile of v1, /device:TPU:0, one launch (start us, length us, event | category | flops | bytes accessed | tf_op | source)
XLA Modules:
  0.0 99.3 jit_solution(7614143559866613342)
XLA Ops:
  0.7 1.7 %split_columns.3 = (bf16[64,512]{1,0:T(8,128)(2,1)}, bf16[64,512]{1,0:T(8,128)(2,1)}, bf16[64,512]{1,0:T(8,128)(2,1)}, bf16[64,512]{1,0:T(8,128)(2,1)}) custom-call(s32[1]{0:T(128)} %bitcast.me_ref, bf16[32,2048]{1,0:T(8,128)(2,1)} %refs_0_.3, bf16[32,2048]{1,0:T(8,128)(2,1)} %refs_1_.3), custom_call_target="tpu_custom_call" | custom-call | tf_op jit(solution)/shard_map/split_columns/pallas_call | solution.py:46
  2.8 2.5 %collective-permute-start.12 = (bf16[64,512]{1,0:T(8,128)(2,1)}, bf16[64,512]{1,0:T(8,128)(2,1)S(1)}, u32[]{:S(2)}, u32[]{:S(2)}) collective-permute-start(bf16[64,512]{1,0:T(8,128)(2,1)} %get-tuple-element.24), channel_id=1, source_target_pairs={{0,2},{1,3},{2,0},{3,1},{4,6},{5,7},{6,4},{7,5},{8,10},{9,11},{10,... | collective-permute-start | bytes 196616 | tf_op jit(solution)/shard_map/ppermute | solution.py:283
  5.5 0.8 fusion
  6.3 2.0 %collective-permute-done.12 = bf16[64,512]{1,0:T(8,128)(2,1)S(1)} collective-permute-done((bf16[64,512]{1,0:T(8,128)(2,1)}, bf16[64,512]{1,0:T(8,128)(2,1)S(1)}, u32[]{:S(2)}, u32[]{:S(2)}) %collective-permute-start.12) | collective-permute-done | bytes 65568 | tf_op jit(solution)/shard_map/ppermute | solution.py:283
  8.3 1.3 %collective-permute-done.13 = bf16[64,512]{1,0:T(8,128)(2,1)S(1)} collective-permute-done((bf16[64,512]{1,0:T(8,128)(2,1)}, bf16[64,512]{1,0:T(8,128)(2,1)S(1)}, u32[]{:S(2)}, u32[]{:S(2)}) %collective-permute-start.13) | collective-permute-done | bytes 65568 | tf_op jit(solution)/shard_map/ppermute | solution.py:283
  9.6 1.6 %collective-permute-start.14 = (bf16[128,512]{1,0:T(8,128)(2,1)S(1)}, bf16[128,512]{1,0:T(8,128)(2,1)S(1)}, u32[]{:S(2)}, u32[]{:S(2)}) collective-permute-start(bf16[128,512]{1,0:T(8,128)(2,1)S(1)} %pad_maximum_fusion.refs_14_), channel_id=1, source_target_pairs={{0,8},{8,16},{16,24},{24,28},{28,20},{20,12},{12,4},{4,0},{1,9},{9... | collective-permute-start | bytes 393224 | tf_op jit(solution)/shard_map/ppermute | solution.py:276
  11.7 1.6 %collective-permute-start.3 = (bf16[256,512]{1,0:T(8,128)(2,1)}, bf16[256,512]{1,0:T(8,128)(2,1)S(1)}, u32[]{:S(2)}, u32[]{:S(2)}) collective-permute-start(bf16[256,512]{1,0:T(8,128)(2,1)} %refs_5_.1), channel_id=1, source_target_pairs={{0,8},{8,16},{16,24},{24,28},{28,20},{20,12},{12,4},{4,0},{1,9},{9... | collective-permute-start | bytes 786440 | tf_op jit(solution)/shard_map/ppermute | solution.py:276
  13.7 2.3 %collective-permute-done.14.refs_10_ = bf16[128,512]{1,0:T(8,128)(2,1)S(1)} collective-permute-done((bf16[128,512]{1,0:T(8,128)(2,1)S(1)}, bf16[128,512]{1,0:T(8,128)(2,1)S(1)}, u32[]{:S(2)}, u32[]{:S(2)}) %collective-permute-start.14) | collective-permute-done | bytes 131104 | tf_op jit(solution)/shard_map/ppermute | solution.py:276
  16.0 1.6 %collective-permute-start.15 = (bf16[128,512]{1,0:T(8,128)(2,1)S(1)}, bf16[128,512]{1,0:T(8,128)(2,1)S(1)}, u32[]{:S(2)}, u32[]{:S(2)}) collective-permute-start(bf16[128,512]{1,0:T(8,128)(2,1)S(1)} %collective-permute-done.14.refs_10_), channel_id=1, source_target_pairs={{0,8},{8,16},{16,24},{24,28},{28,20},{20,12},{12,4},{4,0},{1,9},{9... | collective-permute-start | bytes 393224 | tf_op jit(solution)/shard_map/ppermute | solution.py:276
  18.1 5.6 %collective-permute-done.15.refs_12_ = bf16[128,512]{1,0:T(8,128)(2,1)S(1)} collective-permute-done((bf16[128,512]{1,0:T(8,128)(2,1)S(1)}, bf16[128,512]{1,0:T(8,128)(2,1)S(1)}, u32[]{:S(2)}, u32[]{:S(2)}) %collective-permute-start.15) | collective-permute-done | bytes 131104 | tf_op jit(solution)/shard_map/ppermute | solution.py:276
  23.7 1.6 %collective-permute-start.16 = (bf16[128,512]{1,0:T(8,128)(2,1)S(1)}, bf16[128,512]{1,0:T(8,128)(2,1)S(1)}, u32[]{:S(2)}, u32[]{:S(2)}) collective-permute-start(bf16[128,512]{1,0:T(8,128)(2,1)S(1)} %collective-permute-done.15.refs_12_), channel_id=1, source_target_pairs={{0,8},{8,16},{16,24},{24,28},{28,20},{20,12},{12,4},{4,0},{1,9},{9... | collective-permute-start | bytes 393224 | tf_op jit(solution)/shard_map/ppermute | solution.py:276
  25.7 2.2 %split_columns.2 = (bf16[64,2048]{1,0:T(8,128)(2,1)}, bf16[64,2048]{1,0:T(8,128)(2,1)}, bf16[64,2048]{1,0:T(8,128)(2,1)}, bf16[64,2048]{1,0:T(8,128)(2,1)}) custom-call(s32[1]{0:T(128)} %bitcast.me_ref, bf16[32,8192]{1,0:T(8,128)(2,1)} %refs_0_.2, bf16[32,8192]{1,0:T(8,128)(2,1)} %refs_1_.2), custom_call_target="tpu_custom_call" | custom-call | tf_op jit(solution)/shard_map/split_columns/pallas_call | solution.py:46
  27.9 1.6 %collective-permute-start.1 = (bf16[64,2048]{1,0:T(8,128)(2,1)}, bf16[64,2048]{1,0:T(8,128)(2,1)S(1)}, u32[]{:S(2)}, u32[]{:S(2)}) collective-permute-start(bf16[64,2048]{1,0:T(8,128)(2,1)} %get-tuple-element.20), channel_id=1, source_target_pairs={{0,2},{1,3},{2,0},{3,1},{4,6},{5,7},{6,4},{7,5},{8,10},{9,11},{10,... | collective-permute-start | bytes 786440 | tf_op jit(solution)/shard_map/ppermute | solution.py:286
  29.8 1.6 %collective-permute-start.4 = (bf16[256,512]{1,0:T(8,128)(2,1)S(1)}, bf16[256,512]{1,0:T(8,128)(2,1)S(1)}, u32[]{:S(2)}, u32[]{:S(2)}) collective-permute-start(bf16[256,512]{1,0:T(8,128)(2,1)S(1)} %collective-permute-done.3.refs_6_), channel_id=1, source_target_pairs={{0,8},{8,16},{16,24},{24,28},{28,20},{20,12},{12,4},{4,0},{1,9},{9... | collective-permute-start | bytes 786440 | tf_op jit(solution)/shard_map/ppermute | solution.py:276
  31.8 0.7 dynamic-slice_bitcast_fusion
  33.3 1.6 %collective-permute-start.17 = (bf16[64,512]{1,0:T(8,128)(2,1)S(1)}, bf16[64,512]{1,0:T(8,128)(2,1)S(1)}, u32[]{:S(2)}, u32[]{:S(2)}) collective-permute-start(bf16[64,512]{1,0:T(8,128)(2,1)S(1)} %slice.53), channel_id=1, source_target_pairs={{0,8},{8,16},{16,24},{24,28},{28,20},{20,12},{12,4},{4,0},{1,9},{9... | collective-permute-start | bytes 196616 | tf_op jit(solution)/shard_map/ppermute | solution.py:276
  34.9 2.4 %collective-permute-done.1.refs_3_ = bf16[64,2048]{1,0:T(8,128)(2,1)S(1)} collective-permute-done((bf16[64,2048]{1,0:T(8,128)(2,1)}, bf16[64,2048]{1,0:T(8,128)(2,1)S(1)}, u32[]{:S(2)}, u32[]{:S(2)}) %collective-permute-start.1) | collective-permute-done | bytes 262176 | tf_op jit(solution)/shard_map/ppermute | solution.py:286
  37.3 1.5 %collective-permute-start.21 = (bf16[64,512]{1,0:T(8,128)(2,1)S(1)}, bf16[64,512]{1,0:T(8,128)(2,1)S(1)}, u32[]{:S(2)}, u32[]{:S(2)}) collective-permute-start(bf16[64,512]{1,0:T(8,128)(2,1)S(1)} %slice.54), channel_id=1, source_target_pairs={{8,0},{16,8},{24,16},{28,24},{20,28},{12,20},{4,12},{0,4},{9,1},{1... | collective-permute-start | bytes 196616 | tf_op jit(solution)/shard_map/ppermute | solution.py:277
  38.9 1.6 %collective-permute-start.5 = (bf16[256,512]{1,0:T(8,128)(2,1)S(1)}, bf16[256,512]{1,0:T(8,128)(2,1)S(1)}, u32[]{:S(2)}, u32[]{:S(2)}) collective-permute-start(bf16[256,512]{1,0:T(8,128)(2,1)S(1)} %collective-permute-done.4.refs_8_), channel_id=1, source_target_pairs={{0,8},{8,16},{16,24},{24,28},{28,20},{20,12},{12,4},{4,0},{1,9},{9... | collective-permute-start | bytes 786440 | tf_op jit(solution)/shard_map/ppermute | solution.py:276
  40.9 1.1 %collective-permute-done.2.refs_4_ = bf16[64,2048]{1,0:T(8,128)(2,1)S(1)} collective-permute-done((bf16[64,2048]{1,0:T(8,128)(2,1)}, bf16[64,2048]{1,0:T(8,128)(2,1)S(1)}, u32[]{:S(2)}, u32[]{:S(2)}) %collective-permute-start.2) | collective-permute-done | bytes 262176 | tf_op jit(solution)/shard_map/ppermute | solution.py:286
  42.0 0.9 copy-done.2
  43.0 14.7 %attend.3 = (f32[2,2,1024,128]{3,2,1,0:T(8,128)S(1)}, f32[2,2,1024,128]{3,2,1,0:T(8,128)S(1)}) custom-call(s32[14]{0:T(128)S(1)} %pad_add_fusion.refs_0_, bf16[64,2048]{1,0:T(8,128)(2,1)S(1)} %copy-done.2, bf16[64,2048]{1,0:T(8,128)(2,1)S(1)} %collective-permute-done.refs_2_, bf16[64,2048]{1,0:T(8,128)(2,1)S(1)} %collective-permute-done.1.refs_3_, ...), custom_call_target="tpu_custom_call" | custom-call | flops 8589934592 | bytes 4194304 | tf_op jit(solution)/shard_map/attend/pallas_call | solution.py:219
  57.7 1.5 %collective-permute-start.10 = (bf16[128,512]{1,0:T(8,128)(2,1)S(1)}, bf16[128,512]{1,0:T(8,128)(2,1)S(1)}, u32[]{:S(2)}, u32[]{:S(2)}) collective-permute-start(bf16[128,512]{1,0:T(8,128)(2,1)S(1)} %slice.49), channel_id=1, source_target_pairs={{8,0},{16,8},{24,16},{28,24},{20,28},{12,20},{4,12},{0,4},{9,1},{1... | collective-permute-start | bytes 393224 | tf_op jit(solution)/shard_map/ppermute | solution.py:277
  59.2 0.6 collective-permute-start.6
  59.8 10.2 %attend.4 = (f32[2,2,1024,128]{3,2,1,0:T(8,128)S(1)}, f32[2,2,1024,128]{3,2,1,0:T(8,128)S(1)}) custom-call(s32[14]{0:T(128)S(1)} %pad_add_fusion.refs_0_, bf16[64,2048]{1,0:T(8,128)(2,1)S(1)} %copy-done.3, bf16[64,2048]{1,0:T(8,128)(2,1)S(1)} %collective-permute-done.refs_2_, bf16[64,2048]{1,0:T(8,128)(2,1)S(1)} %collective-permute-done.1.refs_3_, ...), custom_call_target="tpu_custom_call" | custom-call | flops 3221225472 | bytes 4194304 | tf_op jit(solution)/shard_map/attend/pallas_call | solution.py:219
  70.1 11.7 %attend.5 = (bf16[64,2048]{1,0:T(8,128)(2,1)S(1)}, bf16[64,2048]{1,0:T(8,128)(2,1)S(1)}, bf16[64,2048]{1,0:T(8,128)(2,1)S(1)}, bf16[64,2048]{1,0:T(8,128)(2,1)S(1)}) custom-call(s32[14]{0:T(128)S(1)} %pad_add_fusion.refs_0_, bf16[64,2048]{1,0:T(8,128)(2,1)S(1)} %copy-done.3, bf16[64,2048]{1,0:T(8,128)(2,1)S(1)} %collective-permute-done.refs_2_, ...), custom_call_target="tpu_custom_call" | custom-call | flops 1610612736 | bytes 4194304 | tf_op jit(solution)/shard_map/attend/pallas_call | solution.py:219
  81.8 0.7 copy-done
  82.5 1.5 %collective-permute-start.23 = (bf16[64,2048]{1,0:T(8,128)(2,1)S(1)}, bf16[64,2048]{1,0:T(8,128)(2,1)S(1)}, u32[]{:S(2)}, u32[]{:S(2)}) collective-permute-start(bf16[64,2048]{1,0:T(8,128)(2,1)S(1)} %get-tuple-element.32), channel_id=1, source_target_pairs={{0,2},{1,3},{2,0},{3,1},{4,6},{5,7},{6,4},{7,5},{8,10},{9,11},{10,... | collective-permute-start | bytes 786440 | tf_op jit(solution)/shard_map/ppermute | solution.py:306
  84.3 7.2 %collective-permute-done.23.refs_2_ = bf16[64,2048]{1,0:T(8,128)(2,1)S(1)} collective-permute-done((bf16[64,2048]{1,0:T(8,128)(2,1)S(1)}, bf16[64,2048]{1,0:T(8,128)(2,1)S(1)}, u32[]{:S(2)}, u32[]{:S(2)}) %collective-permute-start.23) | collective-permute-done | bytes 262176 | tf_op jit(solution)/shard_map/ppermute | solution.py:306
  91.6 4.8 %collective-permute-done.24.refs_3_ = bf16[64,2048]{1,0:T(8,128)(2,1)S(1)} collective-permute-done((bf16[64,2048]{1,0:T(8,128)(2,1)S(1)}, bf16[64,2048]{1,0:T(8,128)(2,1)S(1)}, u32[]{:S(2)}, u32[]{:S(2)}) %collective-permute-start.24) | collective-permute-done | bytes 262176 | tf_op jit(solution)/shard_map/ppermute | solution.py:306
  96.4 0.7 copy-done.6
  97.1 2.2 %join_columns.1 = (bf16[32,8192]{1,0:T(8,128)(2,1)}, bf16[32,8192]{1,0:T(8,128)(2,1)}) custom-call(s32[1]{0:T(128)} %bitcast.me_ref, bf16[64,2048]{1,0:T(8,128)(2,1)} %copy-done, bf16[64,2048]{1,0:T(8,128)(2,1)} %copy-done.4, bf16[64,2048]{1,0:T(8,128)(2,1)} %copy-done.5, bf16[64,2048]{1,0:T(8,128)(2,1)} %copy-done.6), custom_call_target="tpu_custom_call" | custom-call | tf_op jit(solution)/shard_map/join_columns/pallas_call | solution.py:69
  (52 shorter events, 4.3 us)
Async XLA Ops:
  0.6 41.4 %copy-start.1 = (bf16[256,512]{1,0:T(8,128)(2,1)S(1)}, bf16[256,512]{1,0:T(8,128)(2,1)}, u32[]{:S(2)}) copy-start(bf16[256,512]{1,0:T(8,128)(2,1)} %refs_5_.1) | copy-start | bytes 786436
  0.6 32.5 %copy-start.7 = (s32[1,4]{1,0:T(1,128)S(1)}, s32[1,4]{1,0:T(1,128)}, u32[]{:S(2)}) copy-start(s32[1,4]{1,0:T(1,128)} %param.14) | copy-start | bytes 52
  2.4 3.9 %collective-permute-start.11 = (bf16[64,512]{1,0:T(8,128)(2,1)}, bf16[64,512]{1,0:T(8,128)(2,1)S(1)}, u32[]{:S(2)}, u32[]{:S(2)}) collective-permute-start(bf16[64,512]{1,0:T(8,128)(2,1)} %get-tuple-element.23), channel_id=1, source_target_pairs={{0,1},{1,0},{2,3},{3,2},{4,5},{5,4},{6,7},{7,6},{8,9},{9,8},{10,11... | collective-permute-start | bytes 196616 | tf_op jit(solution)/shard_map/ppermute | solution.py:283
  2.8 5.5 %collective-permute-start.12 = (bf16[64,512]{1,0:T(8,128)(2,1)}, bf16[64,512]{1,0:T(8,128)(2,1)S(1)}, u32[]{:S(2)}, u32[]{:S(2)}) collective-permute-start(bf16[64,512]{1,0:T(8,128)(2,1)} %get-tuple-element.24), channel_id=1, source_target_pairs={{0,2},{1,3},{2,0},{3,1},{4,6},{5,7},{6,4},{7,5},{8,10},{9,11},{10,... | collective-permute-start | bytes 196616 | tf_op jit(solution)/shard_map/ppermute | solution.py:283
  5.3 4.3 %collective-permute-start.13 = (bf16[64,512]{1,0:T(8,128)(2,1)}, bf16[64,512]{1,0:T(8,128)(2,1)S(1)}, u32[]{:S(2)}, u32[]{:S(2)}) collective-permute-start(bf16[64,512]{1,0:T(8,128)(2,1)} %get-tuple-element.25), channel_id=1, source_target_pairs={{0,3},{1,2},{2,1},{3,0},{4,7},{5,6},{6,5},{7,4},{8,11},{9,10},{10,... | collective-permute-start | bytes 196616 | tf_op jit(solution)/shard_map/ppermute | solution.py:283
  9.6 6.4 %collective-permute-start.14 = (bf16[128,512]{1,0:T(8,128)(2,1)S(1)}, bf16[128,512]{1,0:T(8,128)(2,1)S(1)}, u32[]{:S(2)}, u32[]{:S(2)}) collective-permute-start(bf16[128,512]{1,0:T(8,128)(2,1)S(1)} %pad_maximum_fusion.refs_14_), channel_id=1, source_target_pairs={{0,8},{8,16},{16,24},{24,28},{28,20},{20,12},{12,4},{4,0},{1,9},{9... | collective-permute-start | bytes 393224 | tf_op jit(solution)/shard_map/ppermute | solution.py:276
  11.3 6.4 %collective-permute-start.18 = (bf16[128,512]{1,0:T(8,128)(2,1)S(1)}, bf16[128,512]{1,0:T(8,128)(2,1)S(1)}, u32[]{:S(2)}, u32[]{:S(2)}) collective-permute-start(bf16[128,512]{1,0:T(8,128)(2,1)S(1)} %pad_maximum_fusion.refs_14_), channel_id=1, source_target_pairs={{8,0},{16,8},{24,16},{28,24},{20,28},{12,20},{4,12},{0,4},{9,1},{1... | collective-permute-start | bytes 393224 | tf_op jit(solution)/shard_map/ppermute | solution.py:277
  11.7 16.2 %collective-permute-start.3 = (bf16[256,512]{1,0:T(8,128)(2,1)}, bf16[256,512]{1,0:T(8,128)(2,1)S(1)}, u32[]{:S(2)}, u32[]{:S(2)}) collective-permute-start(bf16[256,512]{1,0:T(8,128)(2,1)} %refs_5_.1), channel_id=1, source_target_pairs={{0,8},{8,16},{16,24},{24,28},{28,20},{20,12},{12,4},{4,0},{1,9},{9... | collective-permute-start | bytes 786440 | tf_op jit(solution)/shard_map/ppermute | solution.py:276
  13.3 16.2 %collective-permute-start.7 = (bf16[256,512]{1,0:T(8,128)(2,1)}, bf16[256,512]{1,0:T(8,128)(2,1)S(1)}, u32[]{:S(2)}, u32[]{:S(2)}) collective-permute-start(bf16[256,512]{1,0:T(8,128)(2,1)} %refs_5_.1), channel_id=1, source_target_pairs={{8,0},{16,8},{24,16},{28,24},{20,28},{12,20},{4,12},{0,4},{9,1},{1... | collective-permute-start | bytes 786440 | tf_op jit(solution)/shard_map/ppermute | solution.py:277
  16.0 7.6 %collective-permute-start.15 = (bf16[128,512]{1,0:T(8,128)(2,1)S(1)}, bf16[128,512]{1,0:T(8,128)(2,1)S(1)}, u32[]{:S(2)}, u32[]{:S(2)}) collective-permute-start(bf16[128,512]{1,0:T(8,128)(2,1)S(1)} %collective-permute-done.14.refs_10_), channel_id=1, source_target_pairs={{0,8},{8,16},{16,24},{24,28},{28,20},{20,12},{12,4},{4,0},{1,9},{9... | collective-permute-start | bytes 393224 | tf_op jit(solution)/shard_map/ppermute | solution.py:276
  17.6 7.6 %collective-permute-start.19 = (bf16[128,512]{1,0:T(8,128)(2,1)S(1)}, bf16[128,512]{1,0:T(8,128)(2,1)S(1)}, u32[]{:S(2)}, u32[]{:S(2)}) collective-permute-start(bf16[128,512]{1,0:T(8,128)(2,1)S(1)} %collective-permute-done.18.refs_11_), channel_id=1, source_target_pairs={{8,0},{16,8},{24,16},{28,24},{20,28},{12,20},{4,12},{0,4},{9,1},{1... | collective-permute-start | bytes 393224 | tf_op jit(solution)/shard_map/ppermute | solution.py:277
  23.7 6.1 %collective-permute-start.16 = (bf16[128,512]{1,0:T(8,128)(2,1)S(1)}, bf16[128,512]{1,0:T(8,128)(2,1)S(1)}, u32[]{:S(2)}, u32[]{:S(2)}) collective-permute-start(bf16[128,512]{1,0:T(8,128)(2,1)S(1)} %collective-permute-done.15.refs_12_), channel_id=1, source_target_pairs={{0,8},{8,16},{16,24},{24,28},{28,20},{20,12},{12,4},{4,0},{1,9},{9... | collective-permute-start | bytes 393224 | tf_op jit(solution)/shard_map/ppermute | solution.py:276
  25.2 6.1 %collective-permute-start.20 = (bf16[128,512]{1,0:T(8,128)(2,1)S(1)}, bf16[128,512]{1,0:T(8,128)(2,1)S(1)}, u32[]{:S(2)}, u32[]{:S(2)}) collective-permute-start(bf16[128,512]{1,0:T(8,128)(2,1)S(1)} %collective-permute-done.19.refs_13_), channel_id=1, source_target_pairs={{8,0},{16,8},{24,16},{28,24},{20,28},{12,20},{4,12},{0,4},{9,1},{1... | collective-permute-start | bytes 393224 | tf_op jit(solution)/shard_map/ppermute | solution.py:277
  27.9 5.4 %collective-permute-start = (bf16[64,2048]{1,0:T(8,128)(2,1)}, bf16[64,2048]{1,0:T(8,128)(2,1)S(1)}, u32[]{:S(2)}, u32[]{:S(2)}) collective-permute-start(bf16[64,2048]{1,0:T(8,128)(2,1)} %get-tuple-element.19), channel_id=1, source_target_pairs={{0,1},{1,0},{2,3},{3,2},{4,5},{5,4},{6,7},{7,6},{8,9},{9,8},{10,11... | collective-permute-start | bytes 786440 | tf_op jit(solution)/shard_map/ppermute | solution.py:286
  27.9 9.4 %collective-permute-start.1 = (bf16[64,2048]{1,0:T(8,128)(2,1)}, bf16[64,2048]{1,0:T(8,128)(2,1)S(1)}, u32[]{:S(2)}, u32[]{:S(2)}) collective-permute-start(bf16[64,2048]{1,0:T(8,128)(2,1)} %get-tuple-element.20), channel_id=1, source_target_pairs={{0,2},{1,3},{2,0},{3,1},{4,6},{5,7},{6,4},{7,5},{8,10},{9,11},{10,... | collective-permute-start | bytes 786440 | tf_op jit(solution)/shard_map/ppermute | solution.py:286
  29.5 12.5 %collective-permute-start.2 = (bf16[64,2048]{1,0:T(8,128)(2,1)}, bf16[64,2048]{1,0:T(8,128)(2,1)S(1)}, u32[]{:S(2)}, u32[]{:S(2)}) collective-permute-start(bf16[64,2048]{1,0:T(8,128)(2,1)} %get-tuple-element.21), channel_id=1, source_target_pairs={{0,3},{1,2},{2,1},{3,0},{4,7},{5,6},{6,5},{7,4},{8,11},{9,10},{10,... | collective-permute-start | bytes 786440 | tf_op jit(solution)/shard_map/ppermute | solution.py:286
  29.8 9.1 %collective-permute-start.4 = (bf16[256,512]{1,0:T(8,128)(2,1)S(1)}, bf16[256,512]{1,0:T(8,128)(2,1)S(1)}, u32[]{:S(2)}, u32[]{:S(2)}) collective-permute-start(bf16[256,512]{1,0:T(8,128)(2,1)S(1)} %collective-permute-done.3.refs_6_), channel_id=1, source_target_pairs={{0,8},{8,16},{16,24},{24,28},{28,20},{20,12},{12,4},{4,0},{1,9},{9... | collective-permute-start | bytes 786440 | tf_op jit(solution)/shard_map/ppermute | solution.py:276
  31.4 9.1 %collective-permute-start.8 = (bf16[256,512]{1,0:T(8,128)(2,1)S(1)}, bf16[256,512]{1,0:T(8,128)(2,1)S(1)}, u32[]{:S(2)}, u32[]{:S(2)}) collective-permute-start(bf16[256,512]{1,0:T(8,128)(2,1)S(1)} %collective-permute-done.7.refs_7_), channel_id=1, source_target_pairs={{8,0},{16,8},{24,16},{28,24},{20,28},{12,20},{4,12},{0,4},{9,1},{1... | collective-permute-start | bytes 786440 | tf_op jit(solution)/shard_map/ppermute | solution.py:277
  33.3 36.7 %collective-permute-start.17 = (bf16[64,512]{1,0:T(8,128)(2,1)S(1)}, bf16[64,512]{1,0:T(8,128)(2,1)S(1)}, u32[]{:S(2)}, u32[]{:S(2)}) collective-permute-start(bf16[64,512]{1,0:T(8,128)(2,1)S(1)} %slice.53), channel_id=1, source_target_pairs={{0,8},{8,16},{16,24},{24,28},{28,20},{20,12},{12,4},{4,0},{1,9},{9... | collective-permute-start | bytes 196616 | tf_op jit(solution)/shard_map/ppermute | solution.py:276
  37.3 32.7 %collective-permute-start.21 = (bf16[64,512]{1,0:T(8,128)(2,1)S(1)}, bf16[64,512]{1,0:T(8,128)(2,1)S(1)}, u32[]{:S(2)}, u32[]{:S(2)}) collective-permute-start(bf16[64,512]{1,0:T(8,128)(2,1)S(1)} %slice.54), channel_id=1, source_target_pairs={{8,0},{16,8},{24,16},{28,24},{20,28},{12,20},{4,12},{0,4},{9,1},{1... | collective-permute-start | bytes 196616 | tf_op jit(solution)/shard_map/ppermute | solution.py:277
  38.9 20.3 %collective-permute-start.5 = (bf16[256,512]{1,0:T(8,128)(2,1)S(1)}, bf16[256,512]{1,0:T(8,128)(2,1)S(1)}, u32[]{:S(2)}, u32[]{:S(2)}) collective-permute-start(bf16[256,512]{1,0:T(8,128)(2,1)S(1)} %collective-permute-done.4.refs_8_), channel_id=1, source_target_pairs={{0,8},{8,16},{16,24},{24,28},{28,20},{20,12},{12,4},{4,0},{1,9},{9... | collective-permute-start | bytes 786440 | tf_op jit(solution)/shard_map/ppermute | solution.py:276
  40.5 17.2 %collective-permute-start.9 = (bf16[256,512]{1,0:T(8,128)(2,1)S(1)}, bf16[256,512]{1,0:T(8,128)(2,1)S(1)}, u32[]{:S(2)}, u32[]{:S(2)}) collective-permute-start(bf16[256,512]{1,0:T(8,128)(2,1)S(1)} %collective-permute-done.8.refs_9_), channel_id=1, source_target_pairs={{8,0},{16,8},{24,16},{28,24},{20,28},{12,20},{4,12},{0,4},{9,1},{1... | collective-permute-start | bytes 786440 | tf_op jit(solution)/shard_map/ppermute | solution.py:277
  42.0 1.0 copy-start.2
  42.9 16.9 %copy-start.3 = (bf16[64,2048]{1,0:T(8,128)(2,1)S(1)}, bf16[64,2048]{1,0:T(8,128)(2,1)}, u32[]{:S(2)}) copy-start(bf16[64,2048]{1,0:T(8,128)(2,1)} %get-tuple-element.18.refs_1_) | copy-start | bytes 786436
  57.7 12.4 %collective-permute-start.10 = (bf16[128,512]{1,0:T(8,128)(2,1)S(1)}, bf16[128,512]{1,0:T(8,128)(2,1)S(1)}, u32[]{:S(2)}, u32[]{:S(2)}) collective-permute-start(bf16[128,512]{1,0:T(8,128)(2,1)S(1)} %slice.49), channel_id=1, source_target_pairs={{8,0},{16,8},{24,16},{28,24},{20,28},{12,20},{4,12},{0,4},{9,1},{1... | collective-permute-start | bytes 393224 | tf_op jit(solution)/shard_map/ppermute | solution.py:277
  59.2 10.8 %collective-permute-start.6 = (bf16[128,512]{1,0:T(8,128)(2,1)S(1)}, bf16[128,512]{1,0:T(8,128)(2,1)S(1)}, u32[]{:S(2)}, u32[]{:S(2)}) collective-permute-start(bf16[128,512]{1,0:T(8,128)(2,1)S(1)} %slice.48), channel_id=1, source_target_pairs={{0,8},{8,16},{16,24},{24,28},{28,20},{20,12},{12,4},{4,0},{1,9},{9... | collective-permute-start | bytes 393224 | tf_op jit(solution)/shard_map/ppermute | solution.py:276
  81.8 0.7 copy-start
  82.5 1.9 %collective-permute-start.22 = (bf16[64,2048]{1,0:T(8,128)(2,1)S(1)}, bf16[64,2048]{1,0:T(8,128)(2,1)S(1)}, u32[]{:S(2)}, u32[]{:S(2)}) collective-permute-start(bf16[64,2048]{1,0:T(8,128)(2,1)S(1)} %get-tuple-element.31), channel_id=1, source_target_pairs={{0,1},{1,0},{2,3},{3,2},{4,5},{5,4},{6,7},{7,6},{8,9},{9,8},{10,11... | collective-permute-start | bytes 786440 | tf_op jit(solution)/shard_map/ppermute | solution.py:306
  82.5 9.1 %collective-permute-start.23 = (bf16[64,2048]{1,0:T(8,128)(2,1)S(1)}, bf16[64,2048]{1,0:T(8,128)(2,1)S(1)}, u32[]{:S(2)}, u32[]{:S(2)}) collective-permute-start(bf16[64,2048]{1,0:T(8,128)(2,1)S(1)} %get-tuple-element.32), channel_id=1, source_target_pairs={{0,2},{1,3},{2,0},{3,1},{4,6},{5,7},{6,4},{7,5},{8,10},{9,11},{10,... | collective-permute-start | bytes 786440 | tf_op jit(solution)/shard_map/ppermute | solution.py:306
  84.0 12.4 %collective-permute-start.24 = (bf16[64,2048]{1,0:T(8,128)(2,1)S(1)}, bf16[64,2048]{1,0:T(8,128)(2,1)S(1)}, u32[]{:S(2)}, u32[]{:S(2)}) collective-permute-start(bf16[64,2048]{1,0:T(8,128)(2,1)S(1)} %get-tuple-element.33), channel_id=1, source_target_pairs={{0,3},{1,2},{2,1},{3,0},{4,7},{5,6},{6,5},{7,4},{8,11},{9,10},{10,... | collective-permute-start | bytes 786440 | tf_op jit(solution)/shard_map/ppermute | solution.py:306
  84.3 12.1 %copy-start.4 = (bf16[64,2048]{1,0:T(8,128)(2,1)}, bf16[64,2048]{1,0:T(8,128)(2,1)S(1)}, u32[]{:S(2)}) copy-start(bf16[64,2048]{1,0:T(8,128)(2,1)S(1)} %collective-permute-done.22.refs_1_) | copy-start | bytes 786436
  91.6 4.9 %copy-start.5 = (bf16[64,2048]{1,0:T(8,128)(2,1)}, bf16[64,2048]{1,0:T(8,128)(2,1)S(1)}, u32[]{:S(2)}) copy-start(bf16[64,2048]{1,0:T(8,128)(2,1)S(1)} %collective-permute-done.23.refs_2_) | copy-start | bytes 786436
  (1 other events, 0.7 us)

commit v2 on v0

v2 whole, which is shorter than its diff:
```python
import functools
import math

import jax
import jax.numpy as jnp
import numpy as np
from jax import lax
from jax.experimental import pallas as pl
from jax.experimental.pallas import tpu as pltpu
from jax.sharding import PartitionSpec as P

HEAD_SIZE = 128
GROUP = 8
PAIR = 2 * HEAD_SIZE
RATE = HEAD_SIZE ** (-0.5) * math.log2(math.e)
LOW = -1e30
PASSAGES = 4
MERGE = 2
TIE_P = True
TIE_Q = True
VMEM_LIMIT = 40 * 1024 * 1024


def ring_order(count):
    wide = max(1, math.isqrt(count // 2))
    if count % wide or wide % 2 or wide < 2:
        return list(range(count))
    tall = count // wide
    order = [z * wide for z in range(tall)]
    for step, z in enumerate(reversed(range(tall))):
        row = [z * wide + x for x in range(1, wide)]
        order += row if step % 2 == 0 else row[::-1]
    return order


def is_one_of(index, members):
    found = jnp.int32(0)
    for base in range(0, max(members, default=0) + 1, 16):
        bits = sum(1 << (m - base) for m in members if base <= m < base + 16)
        found += jnp.where(index // 16 == base // 16, (jnp.int32(bits) >> (index % 16)) & 1, 0)
    return found > 0


def split_columns(arrays, peers):
    rows = [a.shape[0] for a in arrays]
    cols = arrays[0].shape[1] // peers
    total = sum(rows)

    def kernel(*refs):
        ins, outs = refs[: len(arrays)], refs[len(arrays) :]
        me = lax.axis_index("head")
        for r in range(peers):
            start = pl.multiple_of((me ^ r) * cols, HEAD_SIZE)
            top = 0
            for ref, count in zip(ins, rows):
                outs[r][top : top + count, :] = ref[:, pl.ds(start, cols)]
                top += count

    return pl.pallas_call(
        kernel,
        out_shape=[jax.ShapeDtypeStruct((total, cols), arrays[0].dtype)] * peers,
        in_specs=[pl.BlockSpec(memory_space=pltpu.VMEM)] * len(arrays),
        out_specs=[pl.BlockSpec(memory_space=pltpu.VMEM)] * peers,
        name="split_columns",
    )(*arrays)


def join_columns(chunks, rows):
    parts, peers = len(chunks), len(chunks[0])
    cols = chunks[0][0].shape[1]
    outs_count = chunks[0][0].shape[0] // rows
    flat = [c for part in chunks for c in part]

    def kernel(*refs):
        ins, outs = refs[: len(flat)], refs[len(flat) :]
        me = lax.axis_index("head")
        for part in range(parts):
            for r in range(peers):
                start = pl.multiple_of((me ^ r) * (cols * parts) + part * cols, HEAD_SIZE)
                for o in range(outs_count):
                    outs[o][:, pl.ds(start, cols)] = ins[part * peers + r][o * rows : (o + 1) * rows, :]

    return pl.pallas_call(
        kernel,
        out_shape=[jax.ShapeDtypeStruct((rows, cols * parts * peers), flat[0].dtype)] * outs_count,
        in_specs=[pl.BlockSpec(memory_space=pltpu.VMEM)] * len(flat),
        out_specs=[pl.BlockSpec(memory_space=pltpu.VMEM)] * outs_count,
        name="join_columns",
    )(*flat)


def stack_rows(groups):
    flat = []
    for group in groups:
        for array, _, _ in group:
            if not any(array is other for other in flat):
                flat.append(array)

    def kernel(*refs):
        ins, outs = refs[: len(flat)], refs[len(flat) :]
        for group, out in zip(groups, outs):
            top = 0
            for array, low, count in group:
                source = [ref for ref, other in zip(ins, flat) if other is array][0]
                out[top : top + count, :] = source[low : low + count, :]
                top += count

    return pl.pallas_call(
        kernel,
        out_shape=[
            jax.ShapeDtypeStruct((sum(count for _, _, count in group), group[0][0].shape[1]), group[0][0].dtype)
            for group in groups
        ],
        in_specs=[pl.BlockSpec(memory_space=pltpu.VMEM)] * len(flat),
        out_specs=[pl.BlockSpec(memory_space=pltpu.VMEM)] * len(groups),
        name="stack_rows",
    )(*flat)


def attend(length, starts, peers, sets, pieces, own, last):
    first = [state is None for _, _, state in sets]
    tokens = sets[0][1][0].shape[0] // 2 if first[0] else sets[0][1].shape[3] // (len(sets[0][0]) * GROUP)
    seat_tokens = peers * tokens
    heads = pieces[0][0].shape[1] // PAIR
    arrays = [p[0] for p in pieces] + list(own or ())
    prefix_rows = [p[1] for p in pieces]
    stretch_rows = [p[0].shape[0] - p[1] for p in pieces]
    seen_by = [p[2] for p in pieces]
    n_prefix = sum(prefix_rows)
    n_common = n_prefix + sum(stretch_rows)
    keys = n_common + (2 * seat_tokens if own else 0)

    flat = [length, starts] + arrays
    q_at, state_at = [], []
    for (ranks, queries, state), fresh in zip(sets, first):
        q_at.append(len(flat))
        flat += list(queries) if fresh else [queries]
        state_at.append(len(flat))
        flat += [] if fresh else list(state)

    mine = [len(ranks) * tokens for ranks, _, _ in sets]
    blocks = [GROUP * m for m in mine]
    out_shape, out_at = [], []
    for (ranks, _, _), fresh, block in zip(sets, first, blocks):
        out_at.append(len(out_shape))
        if last:
            out_shape += [jax.ShapeDtypeStruct((2 * tokens, heads * GROUP * HEAD_SIZE), jnp.bfloat16)] * len(ranks)
        else:
            out_shape.append(jax.ShapeDtypeStruct((heads, 2, HEAD_SIZE, block), jnp.float32))
            out_shape.append(jax.ShapeDtypeStruct((heads, 2, 8, block), jnp.float32))
            if fresh:
                out_shape.append(jax.ShapeDtypeStruct((heads, 2, HEAD_SIZE, block), jnp.bfloat16))

    def kernel(*refs):
        length_ref, starts_ref, array_refs = refs[0], refs[1], refs[2 : 2 + len(arrays)]
        in_refs, out_refs = refs[: len(flat)], refs[len(flat) : -2]
        k_ref, v_ref = refs[-2:]
        me = lax.axis_index("head")
        seat = lax.axis_index("seq")

        def query_positions(n, rows):
            index = lax.broadcasted_iota(jnp.int32, (rows, mine[n]), 1)
            rank = jnp.full_like(index, sets[n][0][0])
            for i, r in enumerate(sets[n][0][1:]):
                rank = jnp.where(index // tokens == i + 1, r, rank)
            return (me ^ rank) * tokens + index % tokens

        def tiled(allowed):
            return jnp.concatenate([jnp.where(allowed, 0.0, LOW)] * GROUP, axis=1)

        masks, live = [], []
        for n in range(len(sets)):
            if own:
                q_pos = query_positions(n, seat_tokens)
                index = lax.broadcasted_iota(jnp.int32, (seat_tokens, mine[n]), 0)
                k_pos = (me ^ (index // tokens)) * tokens + index % tokens
                before = k_pos <= q_pos
                q_set = k_set = jnp.zeros((seat_tokens, mine[n]), jnp.int32)
                for slot in range(PASSAGES):
                    q_set += (starts_ref[0, slot] <= q_pos).astype(jnp.int32)
                    k_set += (starts_ref[0, slot] <= k_pos).astype(jnp.int32)
                masks.append((tiled(before), tiled(before & (q_set == k_set) & (k_pos < length_ref[0]))))
            if last:
                live.append(tiled(query_positions(n, 1) < length_ref[0]) == 0.0)

        def load(h):
            base = h * PAIR

            def put(ref, low, count, top):
                k_ref[h, top : top + count, :] = ref[low : low + count, base : base + HEAD_SIZE]
                v_ref[h, :HEAD_SIZE, top : top + count] = jnp.transpose(
                    ref[low : low + count, base + HEAD_SIZE : base + PAIR]
                )

            top, low = 0, n_prefix
            for ref, in_prefix, in_stretch in zip(array_refs, prefix_rows, stretch_rows):
                if in_prefix:
                    put(ref, 0, in_prefix, top)
                if in_stretch:
                    put(ref, in_prefix, in_stretch, low)
                top += in_prefix
                low += in_stretch
            for ref in array_refs[len(pieces) :]:
                put(ref, 0, seat_tokens, low)
                low += seat_tokens
            v_ref[h, HEAD_SIZE:, :] = jnp.ones((16, keys), jnp.bfloat16)

        def look(n, h, kind):
            if first[n]:
                q = jnp.concatenate(
                    [
                        ref[kind * tokens : (kind + 1) * tokens, col * HEAD_SIZE : (col + 1) * HEAD_SIZE]
                        for col in range(h * GROUP, (h + 1) * GROUP)
                        for ref in in_refs[q_at[n] : state_at[n]]
                    ],
                    axis=0,
                )
                q = jnp.transpose(q)
                if not last:
                    out_refs[out_at[n] + 2][h, kind] = q
            else:
                q = in_refs[q_at[n]][h, kind]
            if kind == 0:
                spans = [(0, n_prefix, None)]
                top = n_prefix
                for count, seen in zip(stretch_rows, seen_by):
                    if count:
                        spans.append((top, top + count, is_one_of(seat, seen)))
                    top += count
                if own:
                    spans.append((n_common, n_common + seat_tokens, masks[n][0]))
            else:
                spans = [(0, n_common + (seat_tokens if own else 0), None)]
                if own:
                    spans.append((n_common + seat_tokens, n_common + 2 * seat_tokens, masks[n][1]))
            parts = []
            for low, high, allowed in spans:
                if low == high:
                    continue
                s = jnp.dot(k_ref[h, low:high, :], q, preferred_element_type=jnp.float32)
                if allowed is not None:
                    s = s + allowed if allowed.ndim == 2 else jnp.where(allowed, s, LOW)
                parts.append(s)
            return parts, functools.reduce(jnp.maximum, [jnp.max(s, axis=0, keepdims=True) for s in parts])

        def weigh(n, h, kind, parts, peak):
            if not first[n]:
                acc_ref, stats_ref = in_refs[state_at[n]], in_refs[state_at[n] + 1]
                old = stats_ref[h, kind, 0:1, :]
                peak = jnp.maximum(old, peak)
                fade = jnp.exp2((old - peak) * RATE)
            weights = jnp.concatenate([jnp.exp2((s - peak) * RATE).astype(jnp.bfloat16) for s in parts], axis=0)
            both = jnp.dot(v_ref[h, :, : weights.shape[0]], weights, preferred_element_type=jnp.float32)
            acc, total = both[:HEAD_SIZE], both[HEAD_SIZE : HEAD_SIZE + 1]
            if not first[n]:
                acc = acc + acc_ref[h, kind] * fade
                total = total + stats_ref[h, kind, 1:2, :] * fade
            if not last:
                out_refs[out_at[n]][h, kind] = acc
                out_refs[out_at[n] + 1][h, kind, 0:1, :] = peak
                out_refs[out_at[n] + 1][h, kind, 1:2, :] = total
                return
            result = acc * (1.0 / total)
            if kind == 1:
                result = jnp.where(live[n], result, 0.0)
            result = jnp.transpose(result.astype(jnp.bfloat16))
            for g in range(GROUP):
                col = (h * GROUP + g) * HEAD_SIZE
                for i in range(len(sets[n][0])):
                    row = g * mine[n] + i * tokens
                    out_refs[out_at[n] + i][kind * tokens : (kind + 1) * tokens, col : col + HEAD_SIZE] = result[
                        row : row + tokens
                    ]

        items = [(n, h, kind) for h in range(heads) for n in range(len(sets)) for kind in range(2)]
        for h in range(heads):
            load(h)
        ahead = look(*items[0])
        for i, item in enumerate(items):
            now = ahead
            if i + 1 < len(items):
                ahead = look(*items[i + 1])
            weigh(*item, *now)

    vmem = pl.BlockSpec(memory_space=pltpu.VMEM)
    rows = heads * 2 * sum(blocks)
    outs = pl.pallas_call(
        kernel,
        in_specs=[pl.BlockSpec(memory_space=pltpu.SMEM)] * 2 + [vmem] * (len(flat) - 2),
        out_specs=[vmem] * len(out_shape),
        out_shape=out_shape,
        scratch_shapes=[
            pltpu.VMEM((heads, keys, HEAD_SIZE), jnp.bfloat16),
            pltpu.VMEM((heads, HEAD_SIZE + 16, keys), jnp.bfloat16),
        ],
        compiler_params=pltpu.CompilerParams(vmem_limit_bytes=VMEM_LIMIT),
        cost_estimate=pl.CostEstimate(
            flops=rows * keys * HEAD_SIZE * 8, bytes_accessed=rows * HEAD_SIZE * 8, transcendentals=rows * keys
        ),
        name="attend",
    )(*flat)
    after = []
    for n, (ranks, queries, _) in enumerate(sets):
        got = outs[out_at[n] :]
        if last:
            after.append(got[: len(ranks)])
        else:
            after.append((ranks, got[2] if first[n] else queries, (got[0], got[1])))
    return after


def body(
    stretch_queries,
    stretch_key_values,
    suffix_queries,
    suffix_key_values,
    prefix_key_values,
    set_length,
    passage_first_slot,
    *,
    peers,
    seats,
):
    tokens = stretch_queries.shape[0]
    prefix_tokens = prefix_key_values.shape[0]
    seat_tokens = peers * tokens
    me = lax.axis_index("head").astype(jnp.int32)
    seat = lax.axis_index("seq").astype(jnp.int32)
    order = ring_order(seats)
    place = {s: i for i, s in enumerate(order)}
    right = [(order[i], order[(i + 1) % seats]) for i in range(seats)]
    left = [(b, a) for a, b in right]
    half = seats // 2

    def across(chunk, r):
        return lax.ppermute(chunk, "head", [(h, h ^ r) for h in range(peers)])

    def step(from_left, from_right):
        return lax.ppermute(from_left, "seq", right), lax.ppermute(from_right, "seq", left)

    def seers(k, side):
        return [s for s in range(seats) if order[(place[s] + (k if side else -k)) % seats] < s]

    near = tuple(r for r in range(peers) if r < 2)
    far = tuple(r for r in range(peers) if r >= 2)

    prefix = {1: step(prefix_key_values, prefix_key_values)}
    chunks = split_columns([stretch_key_values, suffix_key_values], peers)
    chunks = [chunks[0]] + [across(chunks[r], r) for r in range(1, peers)]
    queries = split_columns([stretch_queries, suffix_queries], peers)
    own = stack_rows([[(c, 0, tokens) for c in chunks], [(c, tokens, tokens) for c in chunks]])
    own_stretch = own[0]
    if TIE_P:
        own_stretch, prefix[1] = lax.optimization_barrier((own_stretch, prefix[1]))
    if TIE_Q:
        own_stretch, queries = lax.optimization_barrier((own_stretch, queries))
    queries = [queries[0]] + [across(queries[r], r) for r in range(1, peers)]
    stretch = {1: step(own_stretch, own_stretch)}

    pieces = {0: [(prefix_key_values, prefix_tokens, [])]}
    for k in range(1, min(MERGE, half + 1)):
        if k > 1:
            pair = [prefix[k - 1], stretch[k - 1]]
            if k == half:
                pair = [(p[0][: p[0].shape[0] // 2], p[1][p[1].shape[0] // 2 :]) for p in pair]
            prefix[k] = step(*pair[0])
            stretch[k] = step(*pair[1])
        pieces[k] = [(p, p.shape[0], []) for p in prefix[k]]
        pieces[k] += [(s, 0, seers(k, side)) for side, s in enumerate(stretch[k])]
    k = MERGE - 1
    if k < half:
        whole = stack_rows(
            [[(prefix[k][side], 0, prefix_tokens), (stretch[k][side], 0, seat_tokens)] for side in range(2)]
        )
    for k in range(MERGE, half + 1):
        counts = [prefix_tokens, prefix_tokens]
        if k == half:
            cut = (prefix_tokens + seat_tokens) // 2
            whole = whole[0][:cut], whole[1][cut:]
            counts = [min(cut, prefix_tokens), max(0, prefix_tokens - cut)]
        whole = step(*whole)
        pieces[k] = [(whole[side], counts[side], seers(k, side)) for side in range(2)]

    near_set, far_set = (near, [queries[r] for r in near], None), (far, [queries[r] for r in far], None)
    (near_set,) = attend(set_length, passage_first_slot, peers, [near_set], pieces[0], own, False)
    (near_set,) = attend(set_length, passage_first_slot, peers, [near_set], pieces[1], None, False)
    (far_set,) = attend(set_length, passage_first_slot, peers, [far_set], pieces[0] + pieces[1], own, False)
    for k in range(2, half):
        near_set, far_set = attend(set_length, passage_first_slot, peers, [near_set, far_set], pieces[k], None, False)
    (far_out,) = attend(set_length, passage_first_slot, peers, [far_set], pieces[half], None, True)
    (near_out,) = attend(set_length, passage_first_slot, peers, [near_set], pieces[half], None, True)
    outs = list(near_out) + list(far_out)
    outs = [outs[0]] + [across(outs[r], r) for r in range(1, peers)]
    return tuple(join_columns([outs], tokens))


def solution(mesh):
    placed = (
        P(("seq", "head"), None),
        P(("seq", "head"), None),
        P(("seq", "head"), None),
        P(("seq", "head"), None),
        P("seq", "head"),
        P("seq"),
        P("seq", None),
    )
    return jax.shard_map(
        functools.partial(body, peers=mesh.shape["head"], seats=mesh.shape["seq"]),
        mesh=mesh,
        in_specs=placed,
        out_specs=(P(("seq", "head"), None), P(("seq", "head"), None)),
        check_vma=False,
    )
```

time: 207 us -> 69.8 us (0.34)
  matrix products: 42.1 us -> 0 us
  waiting for transfers between devices: 53.4 us -> 13.5 us
  local copies, waits for them, and re-layouts: 39.6 us -> 3.44 us
  Pallas kernels: 0 us -> 33.1 us
  other arithmetic: 27.2 us -> 0 us
  between operations: 15 us -> 1.54 us
  blocking collectives: 8.67 us -> 0 us
    dot_general x34 -> x0, matrix products: 42.1 us -> none  [the longest x17 21.4 us: state_update(): jnp.einsum('hgrn,nhd->hgrd', weights.astype(jnp.bfloat16), vals, preferre...]
    pallas_call x0 -> x12, Pallas kernels: none -> 33.1 us  [the longest x7 23.3 us: attend(): pl.pallas_call(kernel, in_specs=[pl.BlockSpec(memory_space=pltpu.SMEM)] *...]
    all_to_all x5 -> x0, waiting for transfers between devices: 29.5 us -> none  [the longest x1 8.66 us: body(): lax.all_to_all(stretch_queries, 'head', split_axis=1, concat_axis=0, tile...]
    all_gather x1 -> x0, waiting for transfers between devices: 23.9 us -> none  [body(): piece = lax.all_gather(local_keys, 'seq', axis=0, tiled=True)]
    ppermute x0 -> x19, starting transfers between devices: none -> 17.6 us  [the longest x5 7.49 us: step(): lax.ppermute(from_left, 'seq', right)]
    all_to_all x5 -> x0, starting transfers between devices: 17.2 us -> none  [the longest x1 3.47 us: body(): lax.all_to_all(stretch_queries, 'head', split_axis=1, concat_axis=0, tile...]
    dynamic_slice x24 -> x0, local copies, waits for them, and re-layouts: 14.4 us -> none  [body(): carry, unused = lax.scan(scan_body, carry, (blocks, offsets))]
    ppermute x0 -> x19, waiting for transfers between devices: none -> 13.5 us  [the longest x9 8.07 us: across(): return lax.ppermute(chunk, 'head', [(h, h ^ r) for h in range(peers)])]
  transfers between devices with their start and end apart: 6 -> 19, of which waited for: 6 -> 9; matrix products, arithmetic and copies ran while one was open for 7% -> 0% of each run, Pallas kernels for 0% -> 42%
where the time goes in v2:
time: 69.8 us; the launch traced here: 69.2 us
  Pallas kernels  33.1 us (47%)
  starting transfers between devices  17.6 us (25%)
  waiting for transfers between devices  13.5 us (19%)
  local copies, waits for them, and re-layouts  3.44 us (5%)
  between operations  1.54 us (2%)
    pallas_call x7, Pallas kernels, attend(): pl.pallas_call(kernel, in_specs=[pl.BlockSpec(memory_space=pltpu.SMEM)] *...  23.3 us
    ppermute x9, waiting for transfers between devices, across(): return lax.ppermute(chunk, 'head', [(h, h ^ r) for h in range(peers)])  8.07 us
    ppermute x5, starting transfers between devices, step(): lax.ppermute(from_left, 'seq', right)  7.49 us
    ppermute x9, starting transfers between devices, across(): return lax.ppermute(chunk, 'head', [(h, h ^ r) for h in range(peers)])  6.07 us
    ppermute x5, starting transfers between devices, step(): lax.ppermute(from_right, 'seq', left)  4.01 us
    pallas_call x2, Pallas kernels, split_columns(): pl.pallas_call(kernel, out_shape=[jax.ShapeDtypeStruct((total, cols), arr...  3.9 us
    pallas_call x2, Pallas kernels, stack_rows(): pl.pallas_call(kernel, out_shape=[jax.ShapeDtypeStruct((sum((count for _,...  3.7 us
    unnamed x42, local copies, waits for them, and re-layouts  3.41 us
  transfers between devices with their start and end apart: 19, of which 9 were waited for; matrix products, arithmetic and copies ran while one was open for 0% of the time, Pallas kernels for 42%

profile of v2, /device:TPU:0, one launch (start us, length us, event | category | flops | bytes accessed | tf_op | source)
XLA Modules:
  0.0 69.2 jit_solution(13714981901161520669)
XLA Ops:
  0.6 3.1 %collective-permute-start.3 = (bf16[256,512]{1,0:T(8,128)(2,1)}, bf16[256,512]{1,0:T(8,128)(2,1)S(1)}, u32[]{:S(2)}, u32[]{:S(2)}) collective-permute-start(bf16[256,512]{1,0:T(8,128)(2,1)} %refs_2_.3), channel_id=1, source_target_pairs={{0,8},{8,16},{16,24},{24,28},{28,20},{20,12},{12,4},{4,0},{1,9},{9... | collective-permute-start | bytes 786440 | tf_op jit(solution)/shard_map/ppermute | solution.py:339
  3.7 1.7 %split_columns.2 = (bf16[64,512]{1,0:T(8,128)(2,1)}, bf16[64,512]{1,0:T(8,128)(2,1)}, bf16[64,512]{1,0:T(8,128)(2,1)}, bf16[64,512]{1,0:T(8,128)(2,1)}) custom-call(bf16[32,2048]{1,0:T(8,128)(2,1)} %refs_0_.9, bf16[32,2048]{1,0:T(8,128)(2,1)} %refs_1_.9), custom_call_target="tpu_custom_call" | custom-call | tf_op jit(solution)/shard_map/split_columns/pallas_call | solution.py:59
  5.4 2.0 %collective-permute-start.1 = (bf16[64,512]{1,0:T(8,128)(2,1)}, bf16[64,512]{1,0:T(8,128)(2,1)S(1)}, u32[]{:S(2)}, u32[]{:S(2)}) collective-permute-start(bf16[64,512]{1,0:T(8,128)(2,1)} %get-tuple-element.44), channel_id=1, source_target_pairs={{0,2},{1,3},{2,0},{3,1},{4,6},{5,7},{6,4},{7,5},{8,10},{9,11},{10,... | collective-permute-start | bytes 196616 | tf_op jit(solution)/shard_map/ppermute | solution.py:336
  7.5 2.2 %split_columns.3 = (bf16[64,2048]{1,0:T(8,128)(2,1)}, bf16[64,2048]{1,0:T(8,128)(2,1)}, bf16[64,2048]{1,0:T(8,128)(2,1)}, bf16[64,2048]{1,0:T(8,128)(2,1)}) custom-call(bf16[32,8192]{1,0:T(8,128)(2,1)} %refs_0_.10, bf16[32,8192]{1,0:T(8,128)(2,1)} %refs_1_.10), custom_call_target="tpu_custom_call" | custom-call | tf_op jit(solution)/shard_map/split_columns/pallas_call | solution.py:59
  10.3 1.3 %collective-permute-done.2.refs_3_ = bf16[64,512]{1,0:T(8,128)(2,1)S(1)} collective-permute-done((bf16[64,512]{1,0:T(8,128)(2,1)}, bf16[64,512]{1,0:T(8,128)(2,1)S(1)}, u32[]{:S(2)}, u32[]{:S(2)}) %collective-permute-start.2) | collective-permute-done | bytes 65568 | tf_op jit(solution)/shard_map/ppermute | solution.py:336
  12.3 1.7 %stack_rows.2 = (bf16[128,512]{1,0:T(8,128)(2,1)}, bf16[128,512]{1,0:T(8,128)(2,1)}) custom-call(bf16[64,512]{1,0:T(8,128)(2,1)} %get-tuple-element.42.refs_0_, bf16[64,512]{1,0:T(8,128)(2,1)} %copy-done.17, bf16[64,512]{1,0:T(8,128)(2,1)} %copy-done.18, bf16[64,512]{1,0:T(8,128)(2,1)} %copy-done.19), custom_call_target="tpu_custom_call" | custom-call | tf_op jit(solution)/shard_map/stack_rows/pallas_call | solution.py:108
  14.2 1.6 %collective-permute-start.5 = (bf16[128,512]{1,0:T(8,128)(2,1)}, bf16[128,512]{1,0:T(8,128)(2,1)S(1)}, u32[]{:S(2)}, u32[]{:S(2)}) collective-permute-start(bf16[128,512]{1,0:T(8,128)(2,1)} %get-tuple-element.53.refs_3_.refs_7_), channel_id=1, source_target_pairs={{0,8},{8,16},{16,24},{24,28},{28,20},{20,12},{12,4},{4,0},{1,9},{9... | collective-permute-start | bytes 393224 | tf_op jit(solution)/shard_map/ppermute | solution.py:339
  16.2 1.5 %collective-permute-start.14 = (bf16[64,2048]{1,0:T(8,128)(2,1)}, bf16[64,2048]{1,0:T(8,128)(2,1)S(1)}, u32[]{:S(2)}, u32[]{:S(2)}) collective-permute-start(bf16[64,2048]{1,0:T(8,128)(2,1)} %get-tuple-element.65), channel_id=1, source_target_pairs={{0,2},{1,3},{2,0},{3,1},{4,6},{5,7},{6,4},{7,5},{8,10},{9,11},{10,... | collective-permute-start | bytes 786440 | tf_op jit(solution)/shard_map/ppermute | solution.py:336
  17.8 2.4 %collective-permute-done.5.refs_1_.refs_4_.refs_5_ = bf16[128,512]{1,0:T(8,128)(2,1)S(1)} collective-permute-done((bf16[128,512]{1,0:T(8,128)(2,1)}, bf16[128,512]{1,0:T(8,128)(2,1)S(1)}, u32[]{:S(2)}, u32[]{:S(2)}) %collective-permute-start.5) | collective-permute-done | bytes 131104 | tf_op jit(solution)/shard_map/ppermute | solution.py:339
  20.2 1.3 %collective-permute-done.6.refs_3_.refs_5_.refs_6_ = bf16[128,512]{1,0:T(8,128)(2,1)S(1)} collective-permute-done((bf16[128,512]{1,0:T(8,128)(2,1)}, bf16[128,512]{1,0:T(8,128)(2,1)S(1)}, u32[]{:S(2)}, u32[]{:S(2)}) %collective-permute-start.6) | collective-permute-done | bytes 131104 | tf_op jit(solution)/shard_map/ppermute | solution.py:339
  22.1 2.0 %stack_rows.3 = (bf16[384,512]{1,0:T(8,128)(2,1)}, bf16[384,512]{1,0:T(8,128)(2,1)}) custom-call(bf16[256,512]{1,0:T(8,128)(2,1)} %copy-done, bf16[128,512]{1,0:T(8,128)(2,1)} %copy-done.5, bf16[256,512]{1,0:T(8,128)(2,1)} %copy-done.2, bf16[128,512]{1,0:T(8,128)(2,1)} %copy-done.7), custom_call_target="tpu_custom_call" | custom-call | tf_op jit(solution)/shard_map/stack_rows/pallas_call | solution.py:108
  24.2 0.8 %collective-permute-start.10 = (bf16[384,512]{1,0:T(8,128)(2,1)}, bf16[384,512]{1,0:T(8,128)(2,1)S(1)}, u32[]{:S(2)}, u32[]{:S(2)}) collective-permute-start(bf16[384,512]{1,0:T(8,128)(2,1)} %get-tuple-element.56), channel_id=1, source_target_pairs={{8,0},{16,8},{24,16},{28,24},{20,28},{12,20},{4,12},{0,4},{9,1},{1... | collective-permute-start | bytes 1179656 | tf_op jit(solution)/shard_map/ppermute | solution.py:339
  25.0 1.2 %collective-permute-start.7 = (bf16[384,512]{1,0:T(8,128)(2,1)}, bf16[384,512]{1,0:T(8,128)(2,1)S(1)}, u32[]{:S(2)}, u32[]{:S(2)}) collective-permute-start(bf16[384,512]{1,0:T(8,128)(2,1)} %get-tuple-element.55), channel_id=1, source_target_pairs={{0,8},{8,16},{16,24},{24,28},{28,20},{20,12},{12,4},{4,0},{1,9},{9... | collective-permute-start | bytes 1179656 | tf_op jit(solution)/shard_map/ppermute | solution.py:339
  27.5 2.2 %attend.7 = (f32[2,2,128,512]{3,2,1,0:T(8,128)S(1)}, f32[2,2,8,512]{3,2,1,0:T(8,128)S(1)}, bf16[2,2,128,512]{3,2,1,0:T(8,128)(2,1)S(1)}) custom-call(s32[1]{0:T(128)S(6)} %copy.9.refs_0_, s32[1,4]{1,0:T(1,128)S(1)} %copy-done.13, bf16[256,512]{1,0:T(8,128)(2,1)S(1)} %copy-done.9, bf16[128,512]{1,0:T(8,128)(2,1)S(1)} %copy-done.11, ...), custom_call_target="tpu_custom_call" | custom-call | flops 1073741824 | bytes 2097152 | tf_op jit(solution)/shard_map/attend/pallas_call | solution.py:287
  29.8 4.0 %attend.9 = (f32[2,2,128,512]{3,2,1,0:T(8,128)S(1)}, f32[2,2,8,512]{3,2,1,0:T(8,128)S(1)}, bf16[2,2,128,512]{3,2,1,0:T(8,128)(2,1)S(1)}) custom-call(s32[1]{0:T(128)S(6)} %copy.9.refs_0_, s32[1,4]{1,0:T(1,128)S(1)} %copy-done.13, bf16[256,512]{1,0:T(8,128)(2,1)S(1)} %copy-done.9, bf16[256,512]{1,0:T(8,128)(2,1)S(1)} %copy-done.1, ...), custom_call_target="tpu_custom_call" | custom-call | flops 2684354560 | bytes 2097152 | tf_op jit(solution)/shard_map/attend/pallas_call | solution.py:287
  33.8 0.8 %collective-permute-done.10.refs_3_ = bf16[384,512]{1,0:T(8,128)(2,1)S(1)} collective-permute-done((bf16[384,512]{1,0:T(8,128)(2,1)}, bf16[384,512]{1,0:T(8,128)(2,1)S(1)}, u32[]{:S(2)}, u32[]{:S(2)}) %collective-permute-start.10) | collective-permute-done | bytes 393248 | tf_op jit(solution)/shard_map/ppermute | solution.py:339
  34.6 1.2 %collective-permute-start.11 = (bf16[384,512]{1,0:T(8,128)(2,1)S(1)}, bf16[384,512]{1,0:T(8,128)(2,1)S(1)}, u32[]{:S(2)}, u32[]{:S(2)}) collective-permute-start(bf16[384,512]{1,0:T(8,128)(2,1)S(1)} %collective-permute-done.10.refs_3_), channel_id=1, source_target_pairs={{8,0},{16,8},{24,16},{28,24},{20,28},{12,20},{4,12},{0,4},{9,1},{1... | collective-permute-start | bytes 1179656 | tf_op jit(solution)/shard_map/ppermute | solution.py:339
  35.8 0.9 %collective-permute-start.8 = (bf16[384,512]{1,0:T(8,128)(2,1)S(1)}, bf16[384,512]{1,0:T(8,128)(2,1)S(1)}, u32[]{:S(2)}, u32[]{:S(2)}) collective-permute-start(bf16[384,512]{1,0:T(8,128)(2,1)S(1)} %collective-permute-done.7.refs_2_), channel_id=1, source_target_pairs={{0,8},{8,16},{16,24},{24,28},{28,20},{20,12},{12,4},{4,0},{1,9},{9... | collective-permute-start | bytes 1179656 | tf_op jit(solution)/shard_map/ppermute | solution.py:339
  36.7 2.9 %attend.8 = (f32[2,2,128,512]{3,2,1,0:T(8,128)S(1)}, f32[2,2,8,512]{3,2,1,0:T(8,128)S(1)}) custom-call(s32[1]{0:T(128)S(6)} %copy.9.refs_0_, s32[1,4]{1,0:T(1,128)S(1)} %copy-done.13, bf16[256,512]{1,0:T(8,128)(2,1)S(1)} %copy-done.1, bf16[256,512]{1,0:T(8,128)(2,1)S(1)} %copy-done.3, bf16[128,512]{1,0:T(8,128)(2,1)S(1)} %copy-done.6, ...), custom_call_target="tpu_custom_call" | custom-call | flops 1610612736 | bytes 2097152 | tf_op jit(solution)/shard_map/attend/pallas_call | solution.py:287
  39.5 5.0 %attend.10 = (f32[2,2,128,512]{3,2,1,0:T(8,128)S(1)}, f32[2,2,8,512]{3,2,1,0:T(8,128)S(1)}, f32[2,2,128,512]{3,2,1,0:T(8,128)S(1)}, f32[2,2,8,512]{3,2,1,0:T(8,128)S(1)}) custom-call(s32[1]{0:T(128)S(6)} %copy.9.refs_0_, s32[1,4]{1,0:T(1,128)S(1)} %copy-done.13, bf16[384,512]{1,0:T(8,128)(2,1)S(1)} %collective-permute-done.7.refs_2_, ...), custom_call_target="tpu_custom_call" | custom-call | flops 3221225472 | bytes 4194304 | tf_op jit(solution)/shard_map/attend/pallas_call | solution.py:287
  44.6 0.7 %collective-permute-done.11.refs_3_ = bf16[384,512]{1,0:T(8,128)(2,1)S(1)} collective-permute-done((bf16[384,512]{1,0:T(8,128)(2,1)S(1)}, bf16[384,512]{1,0:T(8,128)(2,1)S(1)}, u32[]{:S(2)}, u32[]{:S(2)}) %collective-permute-start.11) | collective-permute-done | bytes 393248 | tf_op jit(solution)/shard_map/ppermute | solution.py:339
  45.3 1.6 %collective-permute-start.12 = (bf16[192,512]{1,0:T(8,128)(2,1)S(1)}, bf16[192,512]{1,0:T(8,128)(2,1)S(1)}, u32[]{:S(2)}, u32[]{:S(2)}) collective-permute-start(bf16[192,512]{1,0:T(8,128)(2,1)S(1)} %slice.9), channel_id=1, source_target_pairs={{8,0},{16,8},{24,16},{28,24},{20,28},{12,20},{4,12},{0,4},{9,1},{1... | collective-permute-start | bytes 589832 | tf_op jit(solution)/shard_map/ppermute | solution.py:339
  46.9 0.8 %collective-permute-start.9 = (bf16[192,512]{1,0:T(8,128)(2,1)S(1)}, bf16[192,512]{1,0:T(8,128)(2,1)S(1)}, u32[]{:S(2)}, u32[]{:S(2)}) collective-permute-start(bf16[192,512]{1,0:T(8,128)(2,1)S(1)} %slice.8), channel_id=1, source_target_pairs={{0,8},{8,16},{16,24},{24,28},{28,20},{20,12},{12,4},{4,0},{1,9},{9... | collective-permute-start | bytes 589832 | tf_op jit(solution)/shard_map/ppermute | solution.py:339
  47.7 5.0 %attend.11 = (f32[2,2,128,512]{3,2,1,0:T(8,128)S(1)}, f32[2,2,8,512]{3,2,1,0:T(8,128)S(1)}, f32[2,2,128,512]{3,2,1,0:T(8,128)S(1)}, f32[2,2,8,512]{3,2,1,0:T(8,128)S(1)}) custom-call(s32[1]{0:T(128)S(6)} %copy.9.refs_0_, s32[1,4]{1,0:T(1,128)S(1)} %copy-done.13, bf16[384,512]{1,0:T(8,128)(2,1)S(1)} %collective-permute-done.8.refs_2_, ...), custom_call_target="tpu_custom_call" | custom-call | flops 3221225472 | bytes 4194304 | tf_op jit(solution)/shard_map/attend/pallas_call | solution.py:287
  52.9 2.1 %attend.13 = (bf16[64,2048]{1,0:T(8,128)(2,1)S(1)}, bf16[64,2048]{1,0:T(8,128)(2,1)S(1)}) custom-call(s32[1]{0:T(128)S(6)} %copy.9.refs_0_, s32[1,4]{1,0:T(1,128)S(1)} %copy-done.13, bf16[192,512]{1,0:T(8,128)(2,1)S(1)} %collective-permute-done.9.refs_2_, bf16[192,512]{1,0:T(8,128)(2,1)S(1)} %collective-permute-done.12.refs_3_, ...), custom_call_target="tpu_custom_call" | custom-call | flops 805306368 | bytes 2097152 | tf_op jit(solution)/shard_map/attend/pallas_call | solution.py:287
  55.0 1.6 %collective-permute-start.17 = (bf16[64,2048]{1,0:T(8,128)(2,1)S(1)}, bf16[64,2048]{1,0:T(8,128)(2,1)S(1)}, u32[]{:S(2)}, u32[]{:S(2)}) collective-permute-start(bf16[64,2048]{1,0:T(8,128)(2,1)S(1)} %get-tuple-element.80), channel_id=1, source_target_pairs={{0,2},{1,3},{2,0},{3,1},{4,6},{5,7},{6,4},{7,5},{8,10},{9,11},{10,... | collective-permute-start | bytes 786440 | tf_op jit(solution)/shard_map/ppermute | solution.py:336
  56.5 2.1 %attend.12 = (bf16[64,2048]{1,0:T(8,128)(2,1)S(1)}, bf16[64,2048]{1,0:T(8,128)(2,1)S(1)}) custom-call(s32[1]{0:T(128)S(6)} %copy.9.refs_0_, s32[1,4]{1,0:T(1,128)S(1)} %copy-done.13, bf16[192,512]{1,0:T(8,128)(2,1)S(1)} %collective-permute-done.9.refs_2_, bf16[192,512]{1,0:T(8,128)(2,1)S(1)} %collective-permute-done.12.refs_3_, ...), custom_call_target="tpu_custom_call" | custom-call | flops 805306368 | bytes 2097152 | tf_op jit(solution)/shard_map/attend/pallas_call | solution.py:287
  58.6 0.7 copy-done.4
  60.0 3.5 %collective-permute-done.17.refs_2_ = bf16[64,2048]{1,0:T(8,128)(2,1)S(1)} collective-permute-done((bf16[64,2048]{1,0:T(8,128)(2,1)S(1)}, bf16[64,2048]{1,0:T(8,128)(2,1)S(1)}, u32[]{:S(2)}, u32[]{:S(2)}) %collective-permute-start.17) | collective-permute-done | bytes 262176 | tf_op jit(solution)/shard_map/ppermute | solution.py:336
  63.5 2.6 %collective-permute-done.18.refs_3_ = bf16[64,2048]{1,0:T(8,128)(2,1)S(1)} collective-permute-done((bf16[64,2048]{1,0:T(8,128)(2,1)S(1)}, bf16[64,2048]{1,0:T(8,128)(2,1)S(1)}, u32[]{:S(2)}, u32[]{:S(2)}) %collective-permute-start.18) | collective-permute-done | bytes 262176 | tf_op jit(solution)/shard_map/ppermute | solution.py:336
  66.1 0.7 copy-done.15
  66.9 2.2 %join_columns.1 = (bf16[32,8192]{1,0:T(8,128)(2,1)}, bf16[32,8192]{1,0:T(8,128)(2,1)}) custom-call(bf16[64,2048]{1,0:T(8,128)(2,1)} %copy-done.4, bf16[64,2048]{1,0:T(8,128)(2,1)} %copy-done.16, bf16[64,2048]{1,0:T(8,128)(2,1)} %copy-done.14, bf16[64,2048]{1,0:T(8,128)(2,1)} %copy-done.15), custom_call_target="tpu_custom_call" | custom-call | tf_op jit(solution)/shard_map/join_columns/pallas_call | solution.py:83
  (62 shorter events, 4.3 us)
Async XLA Ops:
  0.6 13.3 %collective-permute-start.3 = (bf16[256,512]{1,0:T(8,128)(2,1)}, bf16[256,512]{1,0:T(8,128)(2,1)S(1)}, u32[]{:S(2)}, u32[]{:S(2)}) collective-permute-start(bf16[256,512]{1,0:T(8,128)(2,1)} %refs_2_.3), channel_id=1, source_target_pairs={{0,8},{8,16},{16,24},{24,28},{28,20},{20,12},{12,4},{4,0},{1,9},{9... | collective-permute-start | bytes 786440 | tf_op jit(solution)/shard_map/ppermute | solution.py:339
  3.7 10.2 %collective-permute-start.4 = (bf16[256,512]{1,0:T(8,128)(2,1)}, bf16[256,512]{1,0:T(8,128)(2,1)S(1)}, u32[]{:S(2)}, u32[]{:S(2)}) collective-permute-start(bf16[256,512]{1,0:T(8,128)(2,1)} %refs_2_.3), channel_id=1, source_target_pairs={{8,0},{16,8},{24,16},{28,24},{20,28},{12,20},{4,12},{0,4},{9,1},{1... | collective-permute-start | bytes 786440 | tf_op jit(solution)/shard_map/ppermute | solution.py:339
  5.4 4.3 %collective-permute-start = (bf16[64,512]{1,0:T(8,128)(2,1)}, bf16[64,512]{1,0:T(8,128)(2,1)S(1)}, u32[]{:S(2)}, u32[]{:S(2)}) collective-permute-start(bf16[64,512]{1,0:T(8,128)(2,1)} %get-tuple-element.43), channel_id=1, source_target_pairs={{0,1},{1,0},{2,3},{3,2},{4,5},{5,4},{6,7},{7,6},{8,9},{9,8},{10,11... | collective-permute-start | bytes 196616 | tf_op jit(solution)/shard_map/ppermute | solution.py:336
  5.4 4.9 %collective-permute-start.1 = (bf16[64,512]{1,0:T(8,128)(2,1)}, bf16[64,512]{1,0:T(8,128)(2,1)S(1)}, u32[]{:S(2)}, u32[]{:S(2)}) collective-permute-start(bf16[64,512]{1,0:T(8,128)(2,1)} %get-tuple-element.44), channel_id=1, source_target_pairs={{0,2},{1,3},{2,0},{3,1},{4,6},{5,7},{6,4},{7,5},{8,10},{9,11},{10,... | collective-permute-start | bytes 196616 | tf_op jit(solution)/shard_map/ppermute | solution.py:336
  7.4 4.3 %collective-permute-start.2 = (bf16[64,512]{1,0:T(8,128)(2,1)}, bf16[64,512]{1,0:T(8,128)(2,1)S(1)}, u32[]{:S(2)}, u32[]{:S(2)}) collective-permute-start(bf16[64,512]{1,0:T(8,128)(2,1)} %get-tuple-element.45), channel_id=1, source_target_pairs={{0,3},{1,2},{2,1},{3,0},{4,7},{5,6},{6,5},{7,4},{8,11},{9,10},{10,... | collective-permute-start | bytes 196616 | tf_op jit(solution)/shard_map/ppermute | solution.py:336
  9.7 8.0 %copy-start.20 = (bf16[64,2048]{1,0:T(8,128)(2,1)S(1)}, bf16[64,2048]{1,0:T(8,128)(2,1)}, u32[]{:S(2)}) copy-start(bf16[64,2048]{1,0:T(8,128)(2,1)} %get-tuple-element.66) | copy-start | bytes 786436
  9.7 1.9 %copy-start.17 = (bf16[64,512]{1,0:T(8,128)(2,1)}, bf16[64,512]{1,0:T(8,128)(2,1)S(1)}, u32[]{:S(2)}) copy-start(bf16[64,512]{1,0:T(8,128)(2,1)S(1)} %collective-permute-done.refs_1_) | copy-start | bytes 196612
  13.9 7.5 %copy-start = (bf16[256,512]{1,0:T(8,128)(2,1)}, bf16[256,512]{1,0:T(8,128)(2,1)S(1)}, u32[]{:S(2)}) copy-start(bf16[256,512]{1,0:T(8,128)(2,1)S(1)} %collective-permute-done.3.refs_0_.refs_2_.refs_3_) | copy-start | bytes 786436
  13.9 7.5 %copy-start.2 = (bf16[256,512]{1,0:T(8,128)(2,1)}, bf16[256,512]{1,0:T(8,128)(2,1)S(1)}, u32[]{:S(2)}) copy-start(bf16[256,512]{1,0:T(8,128)(2,1)S(1)} %collective-permute-done.4.refs_2_.refs_3_.refs_4_) | copy-start | bytes 786436
  13.9 12.9 %copy-start.9 = (bf16[256,512]{1,0:T(8,128)(2,1)S(1)}, bf16[256,512]{1,0:T(8,128)(2,1)}, u32[]{:S(2)}) copy-start(bf16[256,512]{1,0:T(8,128)(2,1)} %refs_2_.3) | copy-start | bytes 786436
  14.0 12.9 %copy-start.10 = (bf16[64,2048]{1,0:T(8,128)(2,1)S(1)}, bf16[64,2048]{1,0:T(8,128)(2,1)}, u32[]{:S(2)}) copy-start(bf16[64,2048]{1,0:T(8,128)(2,1)} %get-tuple-element.58.refs_5_) | copy-start | bytes 786436
  14.0 12.9 %copy-start.11 = (bf16[128,512]{1,0:T(8,128)(2,1)S(1)}, bf16[128,512]{1,0:T(8,128)(2,1)}, u32[]{:S(2)}) copy-start(bf16[128,512]{1,0:T(8,128)(2,1)} %get-tuple-element.53.refs_3_.refs_7_) | copy-start | bytes 393220
  14.0 12.9 %copy-start.12 = (bf16[128,512]{1,0:T(8,128)(2,1)S(1)}, bf16[128,512]{1,0:T(8,128)(2,1)}, u32[]{:S(2)}) copy-start(bf16[128,512]{1,0:T(8,128)(2,1)} %get-tuple-element.57.refs_4_.refs_8_) | copy-start | bytes 393220
  14.0 12.9 %collective-permute-start.13 = (bf16[64,2048]{1,0:T(8,128)(2,1)}, bf16[64,2048]{1,0:T(8,128)(2,1)S(1)}, u32[]{:S(2)}, u32[]{:S(2)}) collective-permute-start(bf16[64,2048]{1,0:T(8,128)(2,1)} %get-tuple-element.59), channel_id=1, source_target_pairs={{0,1},{1,0},{2,3},{3,2},{4,5},{5,4},{6,7},{7,6},{8,9},{9,8},{10,11... | collective-permute-start | bytes 786440 | tf_op jit(solution)/shard_map/ppermute | solution.py:336
  14.2 6.0 %collective-permute-start.5 = (bf16[128,512]{1,0:T(8,128)(2,1)}, bf16[128,512]{1,0:T(8,128)(2,1)S(1)}, u32[]{:S(2)}, u32[]{:S(2)}) collective-permute-start(bf16[128,512]{1,0:T(8,128)(2,1)} %get-tuple-element.53.refs_3_.refs_7_), channel_id=1, source_target_pairs={{0,8},{8,16},{16,24},{24,28},{28,20},{20,12},{12,4},{4,0},{1,9},{9... | collective-permute-start | bytes 393224 | tf_op jit(solution)/shard_map/ppermute | solution.py:339
  15.8 5.7 %collective-permute-start.6 = (bf16[128,512]{1,0:T(8,128)(2,1)}, bf16[128,512]{1,0:T(8,128)(2,1)S(1)}, u32[]{:S(2)}, u32[]{:S(2)}) collective-permute-start(bf16[128,512]{1,0:T(8,128)(2,1)} %get-tuple-element.53.refs_3_.refs_7_), channel_id=1, source_target_pairs={{8,0},{16,8},{24,16},{28,24},{20,28},{12,20},{4,12},{0,4},{9,1},{1... | collective-permute-start | bytes 393224 | tf_op jit(solution)/shard_map/ppermute | solution.py:339
  16.2 13.5 %collective-permute-start.14 = (bf16[64,2048]{1,0:T(8,128)(2,1)}, bf16[64,2048]{1,0:T(8,128)(2,1)S(1)}, u32[]{:S(2)}, u32[]{:S(2)}) collective-permute-start(bf16[64,2048]{1,0:T(8,128)(2,1)} %get-tuple-element.65), channel_id=1, source_target_pairs={{0,2},{1,3},{2,0},{3,1},{4,6},{5,7},{6,4},{7,5},{8,10},{9,11},{10,... | collective-permute-start | bytes 786440 | tf_op jit(solution)/shard_map/ppermute | solution.py:336
  17.8 12.0 %collective-permute-start.15 = (bf16[64,2048]{1,0:T(8,128)(2,1)S(1)}, bf16[64,2048]{1,0:T(8,128)(2,1)S(1)}, u32[]{:S(2)}, u32[]{:S(2)}) collective-permute-start(bf16[64,2048]{1,0:T(8,128)(2,1)S(1)} %copy-done.20), channel_id=1, source_target_pairs={{0,3},{1,2},{2,1},{3,0},{4,7},{5,6},{6,5},{7,4},{8,11},{9,10},{10,... | collective-permute-start | bytes 786440 | tf_op jit(solution)/shard_map/ppermute | solution.py:336
  24.2 10.5 %collective-permute-start.10 = (bf16[384,512]{1,0:T(8,128)(2,1)}, bf16[384,512]{1,0:T(8,128)(2,1)S(1)}, u32[]{:S(2)}, u32[]{:S(2)}) collective-permute-start(bf16[384,512]{1,0:T(8,128)(2,1)} %get-tuple-element.56), channel_id=1, source_target_pairs={{8,0},{16,8},{24,16},{28,24},{20,28},{12,20},{4,12},{0,4},{9,1},{1... | collective-permute-start | bytes 1179656 | tf_op jit(solution)/shard_map/ppermute | solution.py:339
  25.0 10.8 %collective-permute-start.7 = (bf16[384,512]{1,0:T(8,128)(2,1)}, bf16[384,512]{1,0:T(8,128)(2,1)S(1)}, u32[]{:S(2)}, u32[]{:S(2)}) collective-permute-start(bf16[384,512]{1,0:T(8,128)(2,1)} %get-tuple-element.55), channel_id=1, source_target_pairs={{0,8},{8,16},{16,24},{24,28},{28,20},{20,12},{12,4},{4,0},{1,9},{9... | collective-permute-start | bytes 1179656 | tf_op jit(solution)/shard_map/ppermute | solution.py:339
  27.5 2.2 %copy-start.1 = (bf16[256,512]{1,0:T(8,128)(2,1)S(1)}, bf16[256,512]{1,0:T(8,128)(2,1)}, u32[]{:S(2)}) copy-start(bf16[256,512]{1,0:T(8,128)(2,1)} %copy-done) | copy-start | bytes 786436
  27.5 2.3 %copy-start.3 = (bf16[256,512]{1,0:T(8,128)(2,1)S(1)}, bf16[256,512]{1,0:T(8,128)(2,1)}, u32[]{:S(2)}) copy-start(bf16[256,512]{1,0:T(8,128)(2,1)} %copy-done.2) | copy-start | bytes 786436
  27.5 2.3 %copy-start.6 = (bf16[128,512]{1,0:T(8,128)(2,1)S(1)}, bf16[128,512]{1,0:T(8,128)(2,1)}, u32[]{:S(2)}) copy-start(bf16[128,512]{1,0:T(8,128)(2,1)} %copy-done.5) | copy-start | bytes 393220
  27.5 2.3 %copy-start.8 = (bf16[128,512]{1,0:T(8,128)(2,1)S(1)}, bf16[128,512]{1,0:T(8,128)(2,1)}, u32[]{:S(2)}) copy-start(bf16[128,512]{1,0:T(8,128)(2,1)} %copy-done.7) | copy-start | bytes 393220
  34.6 10.7 %collective-permute-start.11 = (bf16[384,512]{1,0:T(8,128)(2,1)S(1)}, bf16[384,512]{1,0:T(8,128)(2,1)S(1)}, u32[]{:S(2)}, u32[]{:S(2)}) collective-permute-start(bf16[384,512]{1,0:T(8,128)(2,1)S(1)} %collective-permute-done.10.refs_3_), channel_id=1, source_target_pairs={{8,0},{16,8},{24,16},{28,24},{20,28},{12,20},{4,12},{0,4},{9,1},{1... | collective-permute-start | bytes 1179656 | tf_op jit(solution)/shard_map/ppermute | solution.py:339
  35.8 11.1 %collective-permute-start.8 = (bf16[384,512]{1,0:T(8,128)(2,1)S(1)}, bf16[384,512]{1,0:T(8,128)(2,1)S(1)}, u32[]{:S(2)}, u32[]{:S(2)}) collective-permute-start(bf16[384,512]{1,0:T(8,128)(2,1)S(1)} %collective-permute-done.7.refs_2_), channel_id=1, source_target_pairs={{0,8},{8,16},{16,24},{24,28},{28,20},{20,12},{12,4},{4,0},{1,9},{9... | collective-permute-start | bytes 1179656 | tf_op jit(solution)/shard_map/ppermute | solution.py:339
  45.3 7.4 %collective-permute-start.12 = (bf16[192,512]{1,0:T(8,128)(2,1)S(1)}, bf16[192,512]{1,0:T(8,128)(2,1)S(1)}, u32[]{:S(2)}, u32[]{:S(2)}) collective-permute-start(bf16[192,512]{1,0:T(8,128)(2,1)S(1)} %slice.9), channel_id=1, source_target_pairs={{8,0},{16,8},{24,16},{28,24},{20,28},{12,20},{4,12},{0,4},{9,1},{1... | collective-permute-start | bytes 589832 | tf_op jit(solution)/shard_map/ppermute | solution.py:339
  46.9 6.0 %collective-permute-start.9 = (bf16[192,512]{1,0:T(8,128)(2,1)S(1)}, bf16[192,512]{1,0:T(8,128)(2,1)S(1)}, u32[]{:S(2)}, u32[]{:S(2)}) collective-permute-start(bf16[192,512]{1,0:T(8,128)(2,1)S(1)} %slice.8), channel_id=1, source_target_pairs={{0,8},{8,16},{16,24},{24,28},{28,20},{20,12},{12,4},{4,0},{1,9},{9... | collective-permute-start | bytes 589832 | tf_op jit(solution)/shard_map/ppermute | solution.py:339
  55.0 8.5 %collective-permute-start.17 = (bf16[64,2048]{1,0:T(8,128)(2,1)S(1)}, bf16[64,2048]{1,0:T(8,128)(2,1)S(1)}, u32[]{:S(2)}, u32[]{:S(2)}) collective-permute-start(bf16[64,2048]{1,0:T(8,128)(2,1)S(1)} %get-tuple-element.80), channel_id=1, source_target_pairs={{0,2},{1,3},{2,0},{3,1},{4,6},{5,7},{6,4},{7,5},{8,10},{9,11},{10,... | collective-permute-start | bytes 786440 | tf_op jit(solution)/shard_map/ppermute | solution.py:336
  56.5 9.6 %collective-permute-start.18 = (bf16[64,2048]{1,0:T(8,128)(2,1)S(1)}, bf16[64,2048]{1,0:T(8,128)(2,1)S(1)}, u32[]{:S(2)}, u32[]{:S(2)}) collective-permute-start(bf16[64,2048]{1,0:T(8,128)(2,1)S(1)} %get-tuple-element.81), channel_id=1, source_target_pairs={{0,3},{1,2},{2,1},{3,0},{4,7},{5,6},{6,5},{7,4},{8,11},{9,10},{10,... | collective-permute-start | bytes 786440 | tf_op jit(solution)/shard_map/ppermute | solution.py:336
  59.3 6.8 %collective-permute-start.16 = (bf16[64,2048]{1,0:T(8,128)(2,1)S(1)}, bf16[64,2048]{1,0:T(8,128)(2,1)S(1)}, u32[]{:S(2)}, u32[]{:S(2)}) collective-permute-start(bf16[64,2048]{1,0:T(8,128)(2,1)S(1)} %get-tuple-element.77), channel_id=1, source_target_pairs={{0,1},{1,0},{2,3},{3,2},{4,5},{5,4},{6,7},{7,6},{8,9},{9,8},{10,11... | collective-permute-start | bytes 786440 | tf_op jit(solution)/shard_map/ppermute | solution.py:336
  63.5 2.7 %copy-start.14 = (bf16[64,2048]{1,0:T(8,128)(2,1)}, bf16[64,2048]{1,0:T(8,128)(2,1)S(1)}, u32[]{:S(2)}) copy-start(bf16[64,2048]{1,0:T(8,128)(2,1)S(1)} %collective-permute-done.17.refs_2_) | copy-start | bytes 786436
  (8 other events, 6.7 us)

commit v3 on v2

--- a/solution.py
+++ b/solution.py
@@ -15,9 +15,8 @@
 RATE = HEAD_SIZE ** (-0.5) * math.log2(math.e)
 LOW = -1e30
 PASSAGES = 4
-MERGE = 2
-TIE_P = True
-TIE_Q = True
+AHEAD = 3
+JOIN_VMEM = 8 * 1024 * 1024
 VMEM_LIMIT = 40 * 1024 * 1024
 
 
@@ -42,79 +41,41 @@
 
 
 def split_columns(arrays, peers):
-    rows = [a.shape[0] for a in arrays]
     cols = arrays[0].shape[1] // peers
-    total = sum(rows)
+    me = lax.axis_index("head")
+    return [
+        jnp.concatenate([lax.dynamic_slice_in_dim(a, (me ^ r) * cols, cols, 1) for a in arrays], axis=0)
+        for r in range(peers)
+    ]
+
+
+def join_columns(chunks, peers, rows):
+    cols = chunks[0].shape[1]
+    count = chunks[0].shape[0] // rows
 
     def kernel(*refs):
-        ins, outs = refs[: len(arrays)], refs[len(arrays) :]
+        ins, outs = refs[:peers], refs[peers : peers + count]
         me = lax.axis_index("head")
+        copies = []
         for r in range(peers):
             start = pl.multiple_of((me ^ r) * cols, HEAD_SIZE)
-            top = 0
-            for ref, count in zip(ins, rows):
-                outs[r][top : top + count, :] = ref[:, pl.ds(start, cols)]
-                top += count
+            for o in range(count):
+                source, target = ins[r].at[pl.ds(o * rows, rows)], outs[o].at[:, pl.ds(start, cols)]
+                copies.append(pltpu.make_async_copy(source, target, refs[-1].at[r, o]))
+        for copy in copies:
+            copy.start()
+        for copy in copies:
+            copy.wait()
 
     return pl.pallas_call(
         kernel,
-        out_shape=[jax.ShapeDtypeStruct((total, cols), arrays[0].dtype)] * peers,
-        in_specs=[pl.BlockSpec(memory_space=pltpu.VMEM)] * len(arrays),
-        out_specs=[pl.BlockSpec(memory_space=pltpu.VMEM)] * peers,
-        name="split_columns",
-    )(*arrays)
-
-
-def join_columns(chunks, rows):
-    parts, peers = len(chunks), len(chunks[0])
-    cols = chunks[0][0].shape[1]
-    outs_count = chunks[0][0].shape[0] // rows
-    flat = [c for part in chunks for c in part]
-
-    def kernel(*refs):
-        ins, outs = refs[: len(flat)], refs[len(flat) :]
-        me = lax.axis_index("head")
-        for part in range(parts):
-            for r in range(peers):
-                start = pl.multiple_of((me ^ r) * (cols * parts) + part * cols, HEAD_SIZE)
-                for o in range(outs_count):
-                    outs[o][:, pl.ds(start, cols)] = ins[part * peers + r][o * rows : (o + 1) * rows, :]
-
-    return pl.pallas_call(
-        kernel,
-        out_shape=[jax.ShapeDtypeStruct((rows, cols * parts * peers), flat[0].dtype)] * outs_count,
-        in_specs=[pl.BlockSpec(memory_space=pltpu.VMEM)] * len(flat),
-        out_specs=[pl.BlockSpec(memory_space=pltpu.VMEM)] * outs_count,
+        out_shape=[jax.ShapeDtypeStruct((rows, cols * peers), chunks[0].dtype)] * count,
+        in_specs=[pl.BlockSpec(memory_space=pltpu.VMEM)] * peers,
+        out_specs=[pl.BlockSpec(memory_space=pl.ANY)] * count,
+        scratch_shapes=[pltpu.SemaphoreType.DMA((peers, count))],
+        compiler_params=pltpu.CompilerParams(vmem_limit_bytes=JOIN_VMEM),
         name="join_columns",
-    )(*flat)
-
-
-def stack_rows(groups):
-    flat = []
-    for group in groups:
-        for array, _, _ in group:
-            if not any(array is other for other in flat):
-                flat.append(array)
-
-    def kernel(*refs):
-        ins, outs = refs[: len(flat)], refs[len(flat) :]
-        for group, out in zip(groups, outs):
-            top = 0
-            for array, low, count in group:
-                source = [ref for ref, other in zip(ins, flat) if other is array][0]
-                out[top : top + count, :] = source[low : low + count, :]
-                top += count
-
-    return pl.pallas_call(
-        kernel,
-        out_shape=[
-            jax.ShapeDtypeStruct((sum(count for _, _, count in group), group[0][0].shape[1]), group[0][0].dtype)
-            for group in groups
-        ],
-        in_specs=[pl.BlockSpec(memory_space=pltpu.VMEM)] * len(flat),
-        out_specs=[pl.BlockSpec(memory_space=pltpu.VMEM)] * len(groups),
-        name="stack_rows",
-    )(*flat)
+    )(*chunks)
 
 
 def attend(length, starts, peers, sets, pieces, own, last):
@@ -123,11 +84,10 @@
     seat_tokens = peers * tokens
     heads = pieces[0][0].shape[1] // PAIR
     arrays = [p[0] for p in pieces] + list(own or ())
-    prefix_rows = [p[1] for p in pieces]
-    stretch_rows = [p[0].shape[0] - p[1] for p in pieces]
-    seen_by = [p[2] for p in pieces]
-    n_prefix = sum(prefix_rows)
-    n_common = n_prefix + sum(stretch_rows)
+    spots = [(i,) + span for i, (_, spans) in enumerate(pieces) for span in spans]
+    spots = [s for s in spots if s[3] is None] + [s for s in spots if s[3] is not None]
+    n_prefix = sum(s[2] for s in spots if s[3] is None)
+    n_common = sum(s[2] for s in spots)
     keys = n_common + (2 * seat_tokens if own else 0)
 
     flat = [length, starts] + arrays
@@ -192,17 +152,13 @@
                     ref[low : low + count, base + HEAD_SIZE : base + PAIR]
                 )
 
-            top, low = 0, n_prefix
-            for ref, in_prefix, in_stretch in zip(array_refs, prefix_rows, stretch_rows):
-                if in_prefix:
-                    put(ref, 0, in_prefix, top)
-                if in_stretch:
-                    put(ref, in_prefix, in_stretch, low)
-                top += in_prefix
-                low += in_stretch
+            top = 0
+            for i, low, count, _ in spots:
+                put(array_refs[i], low, count, top)
+                top += count
             for ref in array_refs[len(pieces) :]:
-                put(ref, 0, seat_tokens, low)
-                low += seat_tokens
+                put(ref, 0, seat_tokens, top)
+                top += seat_tokens
             v_ref[h, HEAD_SIZE:, :] = jnp.ones((16, keys), jnp.bfloat16)
 
         def look(n, h, kind):
@@ -223,10 +179,10 @@
             if kind == 0:
                 spans = [(0, n_prefix, None)]
                 top = n_prefix
-                for count, seen in zip(stretch_rows, seen_by):
-                    if count:
+                for _, _, count, seen in spots:
+                    if seen is not None:
                         spans.append((top, top + count, is_one_of(seat, seen)))
-                    top += count
+                        top += count
                 if own:
                     spans.append((n_common, n_common + seat_tokens, masks[n][0]))
             else:
@@ -275,12 +231,11 @@
         items = [(n, h, kind) for h in range(heads) for n in range(len(sets)) for kind in range(2)]
         for h in range(heads):
             load(h)
-        ahead = look(*items[0])
+        queue = [look(*item) for item in items[:AHEAD]]
         for i, item in enumerate(items):
-            now = ahead
-            if i + 1 < len(items):
-                ahead = look(*items[i + 1])
-            weigh(*item, *now)
+            if i + AHEAD < len(items):
+                queue.append(look(*items[i + AHEAD]))
+            weigh(*item, *queue[i])
 
     vmem = pl.BlockSpec(memory_space=pltpu.VMEM)
     rows = heads * 2 * sum(blocks)
@@ -344,54 +299,47 @@
     near = tuple(r for r in range(peers) if r < 2)
     far = tuple(r for r in range(peers) if r >= 2)
 
-    prefix = {1: step(prefix_key_values, prefix_key_values)}
+    first = step(prefix_key_values, prefix_key_values)
     chunks = split_columns([stretch_key_values, suffix_key_values], peers)
     chunks = [chunks[0]] + [across(chunks[r], r) for r in range(1, peers)]
     queries = split_columns([stretch_queries, suffix_queries], peers)
-    own = stack_rows([[(c, 0, tokens) for c in chunks], [(c, tokens, tokens) for c in chunks]])
-    own_stretch = own[0]
-    if TIE_P:
-        own_stretch, prefix[1] = lax.optimization_barrier((own_stretch, prefix[1]))
-    if TIE_Q:
-        own_stretch, queries = lax.optimization_barrier((own_stretch, queries))
+    own = [jnp.concatenate([c[i * tokens : (i + 1) * tokens] for c in chunks], axis=0) for i in range(2)]
+    own, queries = lax.optimization_barrier((own, queries))
     queries = [queries[0]] + [across(queries[r], r) for r in range(1, peers)]
-    stretch = {1: step(own_stretch, own_stretch)}
-
-    pieces = {0: [(prefix_key_values, prefix_tokens, [])]}
-    for k in range(1, min(MERGE, half + 1)):
-        if k > 1:
-            pair = [prefix[k - 1], stretch[k - 1]]
-            if k == half:
-                pair = [(p[0][: p[0].shape[0] // 2], p[1][p[1].shape[0] // 2 :]) for p in pair]
-            prefix[k] = step(*pair[0])
-            stretch[k] = step(*pair[1])
-        pieces[k] = [(p, p.shape[0], []) for p in prefix[k]]
-        pieces[k] += [(s, 0, seers(k, side)) for side, s in enumerate(stretch[k])]
-    k = MERGE - 1
-    if k < half:
-        whole = stack_rows(
-            [[(prefix[k][side], 0, prefix_tokens), (stretch[k][side], 0, seat_tokens)] for side in range(2)]
+
+    pieces = [[(prefix_key_values, [(0, prefix_tokens, None)])] + [(p, [(0, prefix_tokens, None)]) for p in first]]
+    cut = prefix_tokens // 2
+    moving = jnp.concatenate([first[0], own[0]], axis=0), jnp.concatenate([own[0], first[1]], axis=0)
+    for k in range(2, half + 1):
+        count = prefix_tokens
+        if k == half:
+            count = cut
+            moving = moving[0][cut:], moving[1][: seat_tokens + cut]
+        moving = step(*moving)
+        pieces.append(
+            [
+                (moving[0], [(0, count, None), (count, seat_tokens, seers(k - 1, 0))]),
+                (moving[1], [(0, seat_tokens, seers(k - 1, 1)), (seat_tokens, count, None)]),
+            ]
         )
-    for k in range(MERGE, half + 1):
-        counts = [prefix_tokens, prefix_tokens]
-        if k == half:
-            cut = (prefix_tokens + seat_tokens) // 2
-            whole = whole[0][:cut], whole[1][cut:]
-            counts = [min(cut, prefix_tokens), max(0, prefix_tokens - cut)]
-        whole = step(*whole)
-        pieces[k] = [(whole[side], counts[side], seers(k, side)) for side in range(2)]
+    moving = step(moving[0][cut : cut + seat_tokens // 2], moving[1][seat_tokens // 2 : seat_tokens])
+    pieces.append([(m, [(0, seat_tokens // 2, seers(half, side))]) for side, m in enumerate(moving)])
+    pieces[-2:] = [pieces[-2] + pieces[-1]]
+
+    def update(sets, piece, own=None, last=False):
+        return attend(set_length, passage_first_slot, peers, sets, piece, own, last)
 
     near_set, far_set = (near, [queries[r] for r in near], None), (far, [queries[r] for r in far], None)
-    (near_set,) = attend(set_length, passage_first_slot, peers, [near_set], pieces[0], own, False)
-    (near_set,) = attend(set_length, passage_first_slot, peers, [near_set], pieces[1], None, False)
-    (far_set,) = attend(set_length, passage_first_slot, peers, [far_set], pieces[0] + pieces[1], own, False)
-    for k in range(2, half):
-        near_set, far_set = attend(set_length, passage_first_slot, peers, [near_set, far_set], pieces[k], None, False)
-    (far_out,) = attend(set_length, passage_first_slot, peers, [far_set], pieces[half], None, True)
-    (near_out,) = attend(set_length, passage_first_slot, peers, [near_set], pieces[half], None, True)
-    outs = list(near_out) + list(far_out)
-    outs = [outs[0]] + [across(outs[r], r) for r in range(1, peers)]
-    return tuple(join_columns([outs], tokens))
+    (near_set,) = update([near_set], pieces[0], own)
+    far_set = (far, lax.optimization_barrier((far_set[1], pieces[1][0][0]))[0], None)
+    (far_set,) = update([far_set], pieces[0], own)
+    for piece in pieces[1:-1]:
+        near_set, far_set = update([near_set, far_set], piece)
+    (far_out,) = update([far_set], pieces[-1], last=True)
+    (near_out,) = update([near_set], pieces[-1], last=True)
+    far_out = [across(c, r) for c, r in zip(far_out, far)]
+    near_out = [across(c, r) if r else c for c, r in zip(near_out, near)]
+    return tuple(join_columns(near_out + far_out, peers, tokens))
 
 
 def solution(mesh):

time: 69.8 us -> 62.6 us (0.90)
  Pallas kernels: 33.1 us -> 22.7 us
  waiting for transfers between devices: 13.5 us -> 17.3 us
  local copies, waits for them, and re-layouts: 3.44 us -> 2.14 us
    pallas_call x5 -> x1, Pallas kernels: 9.82 us -> 1.02 us  [join_columns(): pl.pallas_call(kernel, out_shape=[jax.ShapeDtypeStruct((rows, cols * peer...]
    ppermute x5, waiting for transfers between devices: 2.56 us -> 7.76 us  [step(): lax.ppermute(from_left, 'seq', right)]
    unnamed x42 -> x6, local copies, waits for them, and re-layouts: 3.41 us -> 0.01 us
    dynamic_slice x0 -> x2, local copies, waits for them, and re-layouts: none -> 2.06 us  [split_columns(): lax.dynamic_slice_in_dim(a, (me ^ r) * cols, cols, 1)]
    ppermute x5, waiting for transfers between devices: 2.84 us -> 0.83 us  [step(): lax.ppermute(from_right, 'seq', left)]
    ppermute x5, starting transfers between devices: 7.49 us -> 9.45 us  [step(): lax.ppermute(from_left, 'seq', right)]
    ppermute x5, starting transfers between devices: 4.01 us -> 2.12 us  [step(): lax.ppermute(from_right, 'seq', left)]
    pallas_call x7 -> x6, Pallas kernels: 23.3 us -> 21.7 us  [attend(): pl.pallas_call(kernel, in_specs=[pl.BlockSpec(memory_space=pltpu.SMEM)] *...]
  transfers between devices with their start and end apart: 19 -> 19, of which waited for: 9 -> 8; matrix products, arithmetic and copies ran while one was open for 0% -> 4% of each run, Pallas kernels for 42% -> 31%
where the time goes in v3:
time: 62.6 us; the launch traced here: 62 us
  Pallas kernels  22.7 us (36%)
  starting transfers between devices  17.9 us (29%)
  waiting for transfers between devices  17.3 us (28%)
  local copies, waits for them, and re-layouts  2.14 us (3%)
  between operations  1.67 us (3%)
    pallas_call x6, Pallas kernels, attend(): pl.pallas_call(kernel, in_specs=[pl.BlockSpec(memory_space=pltpu.SMEM)] *...  21.7 us
    ppermute x5, starting transfers between devices, step(): lax.ppermute(from_left, 'seq', right)  9.45 us
    ppermute x9, waiting for transfers between devices, across(): return lax.ppermute(chunk, 'head', [(h, h ^ r) for h in range(peers)])  8.74 us
    ppermute x5, waiting for transfers between devices, step(): lax.ppermute(from_left, 'seq', right)  7.76 us
    ppermute x9, starting transfers between devices, across(): return lax.ppermute(chunk, 'head', [(h, h ^ r) for h in range(peers)])  6.35 us
    ppermute x5, starting transfers between devices, step(): lax.ppermute(from_right, 'seq', left)  2.12 us
    dynamic_slice x2, local copies, waits for them, and re-layouts, split_columns(): lax.dynamic_slice_in_dim(a, (me ^ r) * cols, cols, 1)  2.06 us
  transfers between devices with their start and end apart: 19, of which 8 were waited for; matrix products, arithmetic and copies ran while one was open for 4% of the time, Pallas kernels for 31%

profile of v3, /device:TPU:0, one launch (start us, length us, event | category | flops | bytes accessed | tf_op | source)
XLA Modules:
  0.0 62.0 jit_solution(11577288783264535735)
XLA Ops:
  0.6 3.1 %collective-permute-start = (bf16[256,512]{1,0:T(8,128)(2,1)}, bf16[256,512]{1,0:T(8,128)(2,1)S(1)}, u32[]{:S(2)}, u32[]{:S(2)}) collective-permute-start(bf16[256,512]{1,0:T(8,128)(2,1)} %refs_2_.3), channel_id=1, source_target_pairs={{0,8},{8,16},{16,24},{24,28},{28,20},{20,12},{12,4},{4,0},{1,9},{9... | collective-permute-start | bytes 786440 | tf_op jit(solution)/shard_map/ppermute | solution.py:294
  3.7 0.9 %constant_dynamic-slice_fusion.8 = (bf16[32,512]{1,0:T(8,128)(2,1)S(1)}, bf16[32,512]{1,0:T(8,128)(2,1)S(1)}, bf16[32,512]{1,0:T(8,128)(2,1)S(1)}, bf16[32,512]{...) fusion(bf16[32,2048]{1,0:T(8,128)(2,1)} %param.10, ...), kind=kLoop, calls=%fused_computation.19 | loop fusion | bytes 524304 | tf_op jit(solution)/shard_map/dynamic_slice | solution.py:47
  4.7 2.0 %collective-permute-start.2 = (bf16[64,512]{1,0:T(8,128)(2,1)S(1)}, bf16[64,512]{1,0:T(8,128)(2,1)S(1)}, u32[]{:S(2)}, u32[]{:S(2)}) collective-permute-start(bf16[64,512]{1,0:T(8,128)(2,1)S(1)} %pad_maximum_fusion.9), channel_id=1, source_target_pairs={{0,2},{1,3},{2,0},{3,1},{4,6},{5,7},{6,4},{7,5},{8,10},{9,11},{10,... | collective-permute-start | bytes 196616 | tf_op jit(solution)/shard_map/ppermute | solution.py:291
  6.8 0.1 collective-permute-start.3
  6.9 1.2 %constant_dynamic-slice_fusion = (bf16[32,2048]{1,0:T(8,128)(2,1)S(1)}, bf16[32,2048]{1,0:T(8,128)(2,1)S(1)}, bf16[32,2048]{1,0:T(8,128)(2,1)S(1)}, bf16[32,2048...) fusion(bf16[32,8192]{1,0:T(8,128)(2,1)S(1)} %copy-done.2, ...), kind=kLoop, calls=%fused_computation.11 | loop fusion | bytes 2097168 | tf_op jit(solution)/shard_map/dynamic_slice | solution.py:47
  8.2 1.2 %collective-permute-done.2 = bf16[64,512]{1,0:T(8,128)(2,1)S(1)} collective-permute-done((bf16[64,512]{1,0:T(8,128)(2,1)S(1)}, bf16[64,512]{1,0:T(8,128)(2,1)S(1)}, u32[]{:S(2)}, u32[]{:S(2)}) %collective-permute-start.2) | collective-permute-done | bytes 65568 | tf_op jit(solution)/shard_map/ppermute | solution.py:291
  9.4 1.4 %collective-permute-done.3 = bf16[64,512]{1,0:T(8,128)(2,1)S(1)} collective-permute-done((bf16[64,512]{1,0:T(8,128)(2,1)S(1)}, bf16[64,512]{1,0:T(8,128)(2,1)S(1)}, u32[]{:S(2)}, u32[]{:S(2)}) %collective-permute-start.3) | collective-permute-done | bytes 65568 | tf_op jit(solution)/shard_map/ppermute | solution.py:291
  10.9 0.8 %collective-permute-done.7.refs_4_ = bf16[256,512]{1,0:T(8,128)(2,1)S(1)} collective-permute-done((bf16[256,512]{1,0:T(8,128)(2,1)}, bf16[256,512]{1,0:T(8,128)(2,1)S(1)}, u32[]{:S(2)}, u32[]{:S(2)}) %collective-permute-start.7) | collective-permute-done | bytes 262176 | tf_op jit(solution)/shard_map/ppermute | solution.py:294
  11.8 1.6 %collective-permute-start.4 = (bf16[384,512]{1,0:T(8,128)(2,1)S(1)}, bf16[384,512]{1,0:T(8,128)(2,1)S(1)}, u32[]{:S(2)}, u32[]{:S(2)}) collective-permute-start(bf16[384,512]{1,0:T(8,128)(2,1)S(1)} %get-tuple-element.63), channel_id=1, source_target_pairs={{0,8},{8,16},{16,24},{24,28},{28,20},{20,12},{12,4},{4,0},{1,9},{9... | collective-permute-start | bytes 1179656 | tf_op jit(solution)/shard_map/ppermute | solution.py:294
  13.4 0.4 collective-permute-start.8
  13.8 1.5 %collective-permute-start.14 = (bf16[64,2048]{1,0:T(8,128)(2,1)S(1)}, bf16[64,2048]{1,0:T(8,128)(2,1)S(1)}, u32[]{:S(2)}, u32[]{:S(2)}) collective-permute-start(bf16[64,2048]{1,0:T(8,128)(2,1)S(1)} %pad_maximum_fusion.4), channel_id=1, source_target_pairs={{0,2},{1,3},{2,0},{3,1},{4,6},{5,7},{6,4},{7,5},{8,10},{9,11},{10,... | collective-permute-start | bytes 786440 | tf_op jit(solution)/shard_map/ppermute | solution.py:291
  15.4 0.3 collective-permute-start.15
  16.3 6.1 %collective-permute-done.4.refs_2_ = bf16[384,512]{1,0:T(8,128)(2,1)S(1)} collective-permute-done((bf16[384,512]{1,0:T(8,128)(2,1)S(1)}, bf16[384,512]{1,0:T(8,128)(2,1)S(1)}, u32[]{:S(2)}, u32[]{:S(2)}) %collective-permute-start.4) | collective-permute-done | bytes 393248 | tf_op jit(solution)/shard_map/ppermute | solution.py:294
  22.5 1.6 %collective-permute-start.5 = (bf16[384,512]{1,0:T(8,128)(2,1)S(1)}, bf16[384,512]{1,0:T(8,128)(2,1)S(1)}, u32[]{:S(2)}, u32[]{:S(2)}) collective-permute-start(bf16[384,512]{1,0:T(8,128)(2,1)S(1)} %collective-permute-done.4.refs_2_), channel_id=1, source_target_pairs={{0,8},{8,16},{16,24},{24,28},{28,20},{20,12},{12,4},{4,0},{1,9},{9... | collective-permute-start | bytes 1179656 | tf_op jit(solution)/shard_map/ppermute | solution.py:294
  24.1 0.5 collective-permute-start.9
  24.5 3.4 %attend.6 = (f32[2,2,128,512]{3,2,1,0:T(8,128)S(1)}, f32[2,2,8,512]{3,2,1,0:T(8,128)S(1)}, bf16[2,2,128,512]{3,2,1,0:T(8,128)(2,1)S(1)}) custom-call(s32[1]{0:T(128)S(6)} %copy.9.refs_0_, s32[1,4]{1,0:T(1,128)S(1)} %copy-done.1, bf16[256,512]{1,0:T(8,128)(2,1)S(1)} %copy-done, bf16[256,512]{1,0:T(8,128)(2,1)S(1)} %collective-permute-done.refs_3_, ...), custom_call_target="tpu_custom_call" | custom-call | flops 2147483648 | bytes 2097152 | tf_op jit(solution)/shard_map/attend/pallas_call | solution.py:242
  28.0 3.4 %attend.7 = (f32[2,2,128,512]{3,2,1,0:T(8,128)S(1)}, f32[2,2,8,512]{3,2,1,0:T(8,128)S(1)}, bf16[2,2,128,512]{3,2,1,0:T(8,128)(2,1)S(1)}) custom-call(s32[1]{0:T(128)S(6)} %copy.9.refs_0_, s32[1,4]{1,0:T(1,128)S(1)} %copy-done.1, bf16[256,512]{1,0:T(8,128)(2,1)S(1)} %copy-done, bf16[256,512]{1,0:T(8,128)(2,1)S(1)} %collective-permute-done.refs_3_, ...), custom_call_target="tpu_custom_call" | custom-call | flops 2147483648 | bytes 2097152 | tf_op jit(solution)/shard_map/attend/pallas_call | solution.py:242
  31.4 0.9 %collective-permute-done.5.refs_2_ = bf16[384,512]{1,0:T(8,128)(2,1)S(1)} collective-permute-done((bf16[384,512]{1,0:T(8,128)(2,1)S(1)}, bf16[384,512]{1,0:T(8,128)(2,1)S(1)}, u32[]{:S(2)}, u32[]{:S(2)}) %collective-permute-start.5) | collective-permute-done | bytes 393248 | tf_op jit(solution)/shard_map/ppermute | solution.py:294
  32.3 1.6 %collective-permute-start.6 = (bf16[256,512]{1,0:T(8,128)(2,1)S(1)}, bf16[256,512]{1,0:T(8,128)(2,1)S(1)}, u32[]{:S(2)}, u32[]{:S(2)}) collective-permute-start(bf16[256,512]{1,0:T(8,128)(2,1)S(1)} %slice.46), channel_id=1, source_target_pairs={{0,8},{8,16},{16,24},{24,28},{28,20},{20,12},{12,4},{4,0},{1,9},{9... | collective-permute-start | bytes 786440 | tf_op jit(solution)/shard_map/ppermute | solution.py:294
  33.9 0.5 collective-permute-start.10
  34.5 4.8 %attend.8 = (f32[2,2,128,512]{3,2,1,0:T(8,128)S(1)}, f32[2,2,8,512]{3,2,1,0:T(8,128)S(1)}, f32[2,2,128,512]{3,2,1,0:T(8,128)S(1)}, f32[2,2,8,512]{3,2,1,0:T(8,128)S(1)}) custom-call(s32[1]{0:T(128)S(6)} %copy.9.refs_0_, s32[1,4]{1,0:T(1,128)S(1)} %copy-done.1, bf16[384,512]{1,0:T(8,128)(2,1)S(1)} %collective-permute-done.4.refs_2_, ...), custom_call_target="tpu_custom_call" | custom-call | flops 3221225472 | bytes 4194304 | tf_op jit(solution)/shard_map/attend/pallas_call | solution.py:242
  39.3 0.7 %collective-permute-done.6.refs_2_ = bf16[256,512]{1,0:T(8,128)(2,1)S(1)} collective-permute-done((bf16[256,512]{1,0:T(8,128)(2,1)S(1)}, bf16[256,512]{1,0:T(8,128)(2,1)S(1)}, u32[]{:S(2)}, u32[]{:S(2)}) %collective-permute-start.6) | collective-permute-done | bytes 262176 | tf_op jit(solution)/shard_map/ppermute | solution.py:294
  40.0 1.6 %collective-permute-start.11 = (bf16[64,512]{1,0:T(8,128)(2,1)S(1)}, bf16[64,512]{1,0:T(8,128)(2,1)S(1)}, u32[]{:S(2)}, u32[]{:S(2)}) collective-permute-start(bf16[64,512]{1,0:T(8,128)(2,1)S(1)} %slice.48), channel_id=1, source_target_pairs={{0,8},{8,16},{16,24},{24,28},{28,20},{20,12},{12,4},{4,0},{1,9},{9... | collective-permute-start | bytes 196616 | tf_op jit(solution)/shard_map/ppermute | solution.py:294
  41.6 0.7 %collective-permute-start.12 = (bf16[64,512]{1,0:T(8,128)(2,1)S(1)}, bf16[64,512]{1,0:T(8,128)(2,1)S(1)}, u32[]{:S(2)}, u32[]{:S(2)}) collective-permute-start(bf16[64,512]{1,0:T(8,128)(2,1)S(1)} %slice.49), channel_id=1, source_target_pairs={{8,0},{16,8},{24,16},{28,24},{20,28},{12,20},{4,12},{0,4},{9,1},{1... | collective-permute-start | bytes 196616 | tf_op jit(solution)/shard_map/ppermute | solution.py:294
  42.3 4.8 %attend.9 = (f32[2,2,128,512]{3,2,1,0:T(8,128)S(1)}, f32[2,2,8,512]{3,2,1,0:T(8,128)S(1)}, f32[2,2,128,512]{3,2,1,0:T(8,128)S(1)}, f32[2,2,8,512]{3,2,1,0:T(8,128)S(1)}) custom-call(s32[1]{0:T(128)S(6)} %copy.9.refs_0_, s32[1,4]{1,0:T(1,128)S(1)} %copy-done.1, bf16[384,512]{1,0:T(8,128)(2,1)S(1)} %collective-permute-done.5.refs_2_, ...), custom_call_target="tpu_custom_call" | custom-call | flops 3221225472 | bytes 4194304 | tf_op jit(solution)/shard_map/attend/pallas_call | solution.py:242
  47.1 2.6 %attend.11 = (bf16[64,2048]{1,0:T(8,128)(2,1)S(1)}, bf16[64,2048]{1,0:T(8,128)(2,1)S(1)}) custom-call(s32[1]{0:T(128)S(6)} %copy.9.refs_0_, s32[1,4]{1,0:T(1,128)S(1)} %copy-done.1, bf16[256,512]{1,0:T(8,128)(2,1)S(1)} %collective-permute-done.6.refs_2_, bf16[256,512]{1,0:T(8,128)(2,1)S(1)} %collective-permute-done.10.refs_3_, ...), custom_call_target="tpu_custom_call" | custom-call | flops 1342177280 | bytes 2097152 | tf_op jit(solution)/shard_map/attend/pallas_call | solution.py:242
  49.8 1.6 %collective-permute-start.17 = (bf16[64,2048]{1,0:T(8,128)(2,1)S(1)}, bf16[64,2048]{1,0:T(8,128)(2,1)S(1)}, u32[]{:S(2)}, u32[]{:S(2)}) collective-permute-start(bf16[64,2048]{1,0:T(8,128)(2,1)S(1)} %get-tuple-element.52), channel_id=1, source_target_pairs={{0,2},{1,3},{2,0},{3,1},{4,6},{5,7},{6,4},{7,5},{8,10},{9,11},{10,... | collective-permute-start | bytes 786440 | tf_op jit(solution)/shard_map/ppermute | solution.py:291
  51.4 2.6 %attend.10 = (bf16[64,2048]{1,0:T(8,128)(2,1)S(1)}, bf16[64,2048]{1,0:T(8,128)(2,1)S(1)}) custom-call(s32[1]{0:T(128)S(6)} %copy.9.refs_0_, s32[1,4]{1,0:T(1,128)S(1)} %copy-done.1, bf16[256,512]{1,0:T(8,128)(2,1)S(1)} %collective-permute-done.6.refs_2_, bf16[256,512]{1,0:T(8,128)(2,1)S(1)} %collective-permute-done.10.refs_3_, ...), custom_call_target="tpu_custom_call" | custom-call | flops 1342177280 | bytes 2097152 | tf_op jit(solution)/shard_map/attend/pallas_call | solution.py:242
  54.0 0.7 %collective-permute-start.16 = (bf16[64,2048]{1,0:T(8,128)(2,1)S(1)}, bf16[64,2048]{1,0:T(8,128)(2,1)S(1)}, u32[]{:S(2)}, u32[]{:S(2)}) collective-permute-start(bf16[64,2048]{1,0:T(8,128)(2,1)S(1)} %get-tuple-element.49), channel_id=1, source_target_pairs={{0,1},{1,0},{2,3},{3,2},{4,5},{5,4},{6,7},{7,6},{8,9},{9,8},{10,11... | collective-permute-start | bytes 786440 | tf_op jit(solution)/shard_map/ppermute | solution.py:291
  54.7 3.4 %collective-permute-done.17.refs_2_ = bf16[64,2048]{1,0:T(8,128)(2,1)S(1)} collective-permute-done((bf16[64,2048]{1,0:T(8,128)(2,1)S(1)}, bf16[64,2048]{1,0:T(8,128)(2,1)S(1)}, u32[]{:S(2)}, u32[]{:S(2)}) %collective-permute-start.17) | collective-permute-done | bytes 262176 | tf_op jit(solution)/shard_map/ppermute | solution.py:291
  58.1 2.7 %collective-permute-done.18.refs_3_ = bf16[64,2048]{1,0:T(8,128)(2,1)S(1)} collective-permute-done((bf16[64,2048]{1,0:T(8,128)(2,1)S(1)}, bf16[64,2048]{1,0:T(8,128)(2,1)S(1)}, u32[]{:S(2)}, u32[]{:S(2)}) %collective-permute-start.18) | collective-permute-done | bytes 262176 | tf_op jit(solution)/shard_map/ppermute | solution.py:291
  60.8 1.0 %join_columns.1 = (bf16[32,8192]{1,0:T(8,128)(2,1)}, bf16[32,8192]{1,0:T(8,128)(2,1)}) custom-call(bf16[64,2048]{1,0:T(8,128)(2,1)S(1)} %get-tuple-element.48.refs_0_, bf16[64,2048]{1,0:T(8,128)(2,1)S(1)} %collective-permute-done.16.refs_1_, bf16[64,2048]{1,0:T(8,128)(2,1)S(1)} %collective-permute-done.17.refs_2_, ...), custom_call_target="tpu_custom_call" | custom-call | tf_op jit(solution)/shard_map/join_columns/pallas_call | solution.py:70
  (38 shorter events, 0.4 us)
Async XLA Ops:
  0.6 6.3 %copy-start.2 = (bf16[32,8192]{1,0:T(8,128)(2,1)S(1)}, bf16[32,8192]{1,0:T(8,128)(2,1)}, u32[]{:S(2)}) copy-start(bf16[32,8192]{1,0:T(8,128)(2,1)} %param.9) | copy-start | bytes 1572868
  0.6 10.2 %collective-permute-start = (bf16[256,512]{1,0:T(8,128)(2,1)}, bf16[256,512]{1,0:T(8,128)(2,1)S(1)}, u32[]{:S(2)}, u32[]{:S(2)}) collective-permute-start(bf16[256,512]{1,0:T(8,128)(2,1)} %refs_2_.3), channel_id=1, source_target_pairs={{0,8},{8,16},{16,24},{24,28},{28,20},{20,12},{12,4},{4,0},{1,9},{9... | collective-permute-start | bytes 786440 | tf_op jit(solution)/shard_map/ppermute | solution.py:294
  3.7 8.0 %collective-permute-start.7 = (bf16[256,512]{1,0:T(8,128)(2,1)}, bf16[256,512]{1,0:T(8,128)(2,1)S(1)}, u32[]{:S(2)}, u32[]{:S(2)}) collective-permute-start(bf16[256,512]{1,0:T(8,128)(2,1)} %refs_2_.3), channel_id=1, source_target_pairs={{8,0},{16,8},{24,16},{28,24},{20,28},{12,20},{4,12},{0,4},{9,1},{1... | collective-permute-start | bytes 786440 | tf_op jit(solution)/shard_map/ppermute | solution.py:294
  4.6 3.5 %collective-permute-start.1 = (bf16[64,512]{1,0:T(8,128)(2,1)S(1)}, bf16[64,512]{1,0:T(8,128)(2,1)S(1)}, u32[]{:S(2)}, u32[]{:S(2)}) collective-permute-start(bf16[64,512]{1,0:T(8,128)(2,1)S(1)} %pad_maximum_fusion.8), channel_id=1, source_target_pairs={{0,1},{1,0},{2,3},{3,2},{4,5},{5,4},{6,7},{7,6},{8,9},{9,8},{10,11... | collective-permute-start | bytes 196616 | tf_op jit(solution)/shard_map/ppermute | solution.py:291
  4.7 4.7 %collective-permute-start.2 = (bf16[64,512]{1,0:T(8,128)(2,1)S(1)}, bf16[64,512]{1,0:T(8,128)(2,1)S(1)}, u32[]{:S(2)}, u32[]{:S(2)}) collective-permute-start(bf16[64,512]{1,0:T(8,128)(2,1)S(1)} %pad_maximum_fusion.9), channel_id=1, source_target_pairs={{0,2},{1,3},{2,0},{3,1},{4,6},{5,7},{6,4},{7,5},{8,10},{9,11},{10,... | collective-permute-start | bytes 196616 | tf_op jit(solution)/shard_map/ppermute | solution.py:291
  6.8 4.1 %collective-permute-start.3 = (bf16[64,512]{1,0:T(8,128)(2,1)S(1)}, bf16[64,512]{1,0:T(8,128)(2,1)S(1)}, u32[]{:S(2)}, u32[]{:S(2)}) collective-permute-start(bf16[64,512]{1,0:T(8,128)(2,1)S(1)} %pad_maximum_fusion.10), channel_id=1, source_target_pairs={{0,3},{1,2},{2,1},{3,0},{4,7},{5,6},{6,5},{7,4},{8,11},{9,10},{10,... | collective-permute-start | bytes 196616 | tf_op jit(solution)/shard_map/ppermute | solution.py:291
  10.9 13.7 %copy-start = (bf16[256,512]{1,0:T(8,128)(2,1)S(1)}, bf16[256,512]{1,0:T(8,128)(2,1)}, u32[]{:S(2)}) copy-start(bf16[256,512]{1,0:T(8,128)(2,1)} %refs_2_.3) | copy-start | bytes 786436
  11.8 10.7 %collective-permute-start.4 = (bf16[384,512]{1,0:T(8,128)(2,1)S(1)}, bf16[384,512]{1,0:T(8,128)(2,1)S(1)}, u32[]{:S(2)}, u32[]{:S(2)}) collective-permute-start(bf16[384,512]{1,0:T(8,128)(2,1)S(1)} %get-tuple-element.63), channel_id=1, source_target_pairs={{0,8},{8,16},{16,24},{24,28},{28,20},{20,12},{12,4},{4,0},{1,9},{9... | collective-permute-start | bytes 1179656 | tf_op jit(solution)/shard_map/ppermute | solution.py:294
  13.4 11.1 %copy-start.1 = (s32[1,4]{1,0:T(1,128)S(1)}, s32[1,4]{1,0:T(1,128)}, u32[]{:S(2)}) copy-start(s32[1,4]{1,0:T(1,128)} %refs_1_.11) | copy-start | bytes 52
  13.4 10.7 %collective-permute-start.8 = (bf16[384,512]{1,0:T(8,128)(2,1)S(1)}, bf16[384,512]{1,0:T(8,128)(2,1)S(1)}, u32[]{:S(2)}, u32[]{:S(2)}) collective-permute-start(bf16[384,512]{1,0:T(8,128)(2,1)S(1)} %get-tuple-element.62), channel_id=1, source_target_pairs={{8,0},{16,8},{24,16},{28,24},{20,28},{12,20},{4,12},{0,4},{9,1},{1... | collective-permute-start | bytes 1179656 | tf_op jit(solution)/shard_map/ppermute | solution.py:294
  13.8 10.7 %collective-permute-start.13 = (bf16[64,2048]{1,0:T(8,128)(2,1)S(1)}, bf16[64,2048]{1,0:T(8,128)(2,1)S(1)}, u32[]{:S(2)}, u32[]{:S(2)}) collective-permute-start(bf16[64,2048]{1,0:T(8,128)(2,1)S(1)} %pad_maximum_fusion.3), channel_id=1, source_target_pairs={{0,1},{1,0},{2,3},{3,2},{4,5},{5,4},{6,7},{7,6},{8,9},{9,8},{10,11... | collective-permute-start | bytes 786440 | tf_op jit(solution)/shard_map/ppermute | solution.py:291
  13.8 14.1 %collective-permute-start.14 = (bf16[64,2048]{1,0:T(8,128)(2,1)S(1)}, bf16[64,2048]{1,0:T(8,128)(2,1)S(1)}, u32[]{:S(2)}, u32[]{:S(2)}) collective-permute-start(bf16[64,2048]{1,0:T(8,128)(2,1)S(1)} %pad_maximum_fusion.4), channel_id=1, source_target_pairs={{0,2},{1,3},{2,0},{3,1},{4,6},{5,7},{6,4},{7,5},{8,10},{9,11},{10,... | collective-permute-start | bytes 786440 | tf_op jit(solution)/shard_map/ppermute | solution.py:291
  15.4 12.6 %collective-permute-start.15 = (bf16[64,2048]{1,0:T(8,128)(2,1)S(1)}, bf16[64,2048]{1,0:T(8,128)(2,1)S(1)}, u32[]{:S(2)}, u32[]{:S(2)}) collective-permute-start(bf16[64,2048]{1,0:T(8,128)(2,1)S(1)} %pad_maximum_fusion.5), channel_id=1, source_target_pairs={{0,3},{1,2},{2,1},{3,0},{4,7},{5,6},{6,5},{7,4},{8,11},{9,10},{10,... | collective-permute-start | bytes 786440 | tf_op jit(solution)/shard_map/ppermute | solution.py:291
  22.5 9.8 %collective-permute-start.5 = (bf16[384,512]{1,0:T(8,128)(2,1)S(1)}, bf16[384,512]{1,0:T(8,128)(2,1)S(1)}, u32[]{:S(2)}, u32[]{:S(2)}) collective-permute-start(bf16[384,512]{1,0:T(8,128)(2,1)S(1)} %collective-permute-done.4.refs_2_), channel_id=1, source_target_pairs={{0,8},{8,16},{16,24},{24,28},{28,20},{20,12},{12,4},{4,0},{1,9},{9... | collective-permute-start | bytes 1179656 | tf_op jit(solution)/shard_map/ppermute | solution.py:294
  24.1 9.8 %collective-permute-start.9 = (bf16[384,512]{1,0:T(8,128)(2,1)S(1)}, bf16[384,512]{1,0:T(8,128)(2,1)S(1)}, u32[]{:S(2)}, u32[]{:S(2)}) collective-permute-start(bf16[384,512]{1,0:T(8,128)(2,1)S(1)} %collective-permute-done.8.refs_3_), channel_id=1, source_target_pairs={{8,0},{16,8},{24,16},{28,24},{20,28},{12,20},{4,12},{0,4},{9,1},{1... | collective-permute-start | bytes 1179656 | tf_op jit(solution)/shard_map/ppermute | solution.py:294
  32.3 7.7 %collective-permute-start.6 = (bf16[256,512]{1,0:T(8,128)(2,1)S(1)}, bf16[256,512]{1,0:T(8,128)(2,1)S(1)}, u32[]{:S(2)}, u32[]{:S(2)}) collective-permute-start(bf16[256,512]{1,0:T(8,128)(2,1)S(1)} %slice.46), channel_id=1, source_target_pairs={{0,8},{8,16},{16,24},{24,28},{28,20},{20,12},{12,4},{4,0},{1,9},{9... | collective-permute-start | bytes 786440 | tf_op jit(solution)/shard_map/ppermute | solution.py:294
  33.9 7.7 %collective-permute-start.10 = (bf16[256,512]{1,0:T(8,128)(2,1)S(1)}, bf16[256,512]{1,0:T(8,128)(2,1)S(1)}, u32[]{:S(2)}, u32[]{:S(2)}) collective-permute-start(bf16[256,512]{1,0:T(8,128)(2,1)S(1)} %slice.47), channel_id=1, source_target_pairs={{8,0},{16,8},{24,16},{28,24},{20,28},{12,20},{4,12},{0,4},{9,1},{1... | collective-permute-start | bytes 786440 | tf_op jit(solution)/shard_map/ppermute | solution.py:294
  40.0 7.1 %collective-permute-start.11 = (bf16[64,512]{1,0:T(8,128)(2,1)S(1)}, bf16[64,512]{1,0:T(8,128)(2,1)S(1)}, u32[]{:S(2)}, u32[]{:S(2)}) collective-permute-start(bf16[64,512]{1,0:T(8,128)(2,1)S(1)} %slice.48), channel_id=1, source_target_pairs={{0,8},{8,16},{16,24},{24,28},{28,20},{20,12},{12,4},{4,0},{1,9},{9... | collective-permute-start | bytes 196616 | tf_op jit(solution)/shard_map/ppermute | solution.py:294
  41.6 5.5 %collective-permute-start.12 = (bf16[64,512]{1,0:T(8,128)(2,1)S(1)}, bf16[64,512]{1,0:T(8,128)(2,1)S(1)}, u32[]{:S(2)}, u32[]{:S(2)}) collective-permute-start(bf16[64,512]{1,0:T(8,128)(2,1)S(1)} %slice.49), channel_id=1, source_target_pairs={{8,0},{16,8},{24,16},{28,24},{20,28},{12,20},{4,12},{0,4},{9,1},{1... | collective-permute-start | bytes 196616 | tf_op jit(solution)/shard_map/ppermute | solution.py:294
  49.8 8.3 %collective-permute-start.17 = (bf16[64,2048]{1,0:T(8,128)(2,1)S(1)}, bf16[64,2048]{1,0:T(8,128)(2,1)S(1)}, u32[]{:S(2)}, u32[]{:S(2)}) collective-permute-start(bf16[64,2048]{1,0:T(8,128)(2,1)S(1)} %get-tuple-element.52), channel_id=1, source_target_pairs={{0,2},{1,3},{2,0},{3,1},{4,6},{5,7},{6,4},{7,5},{8,10},{9,11},{10,... | collective-permute-start | bytes 786440 | tf_op jit(solution)/shard_map/ppermute | solution.py:291
  51.4 9.4 %collective-permute-start.18 = (bf16[64,2048]{1,0:T(8,128)(2,1)S(1)}, bf16[64,2048]{1,0:T(8,128)(2,1)S(1)}, u32[]{:S(2)}, u32[]{:S(2)}) collective-permute-start(bf16[64,2048]{1,0:T(8,128)(2,1)S(1)} %get-tuple-element.53), channel_id=1, source_target_pairs={{0,3},{1,2},{2,1},{3,0},{4,7},{5,6},{6,5},{7,4},{8,11},{9,10},{10,... | collective-permute-start | bytes 786440 | tf_op jit(solution)/shard_map/ppermute | solution.py:291
  54.0 6.8 %collective-permute-start.16 = (bf16[64,2048]{1,0:T(8,128)(2,1)S(1)}, bf16[64,2048]{1,0:T(8,128)(2,1)S(1)}, u32[]{:S(2)}, u32[]{:S(2)}) collective-permute-start(bf16[64,2048]{1,0:T(8,128)(2,1)S(1)} %get-tuple-element.49), channel_id=1, source_target_pairs={{0,1},{1,0},{2,3},{3,2},{4,5},{5,4},{6,7},{7,6},{8,9},{9,8},{10,11... | collective-permute-start | bytes 786440 | tf_op jit(solution)/shard_map/ppermute | solution.py:291

commit v4 on v3

--- a/solution.py
+++ b/solution.py
@@ -324,7 +324,6 @@
         )
     moving = step(moving[0][cut : cut + seat_tokens // 2], moving[1][seat_tokens // 2 : seat_tokens])
     pieces.append([(m, [(0, seat_tokens // 2, seers(half, side))]) for side, m in enumerate(moving)])
-    pieces[-2:] = [pieces[-2] + pieces[-1]]
 
     def update(sets, piece, own=None, last=False):
         return attend(set_length, passage_first_slot, peers, sets, piece, own, last)
@@ -333,10 +332,13 @@
     (near_set,) = update([near_set], pieces[0], own)
     far_set = (far, lax.optimization_barrier((far_set[1], pieces[1][0][0]))[0], None)
     (far_set,) = update([far_set], pieces[0], own)
-    for piece in pieces[1:-1]:
+    late = max(1, len(pieces) - 3)
+    for piece in pieces[1:late]:
         near_set, far_set = update([near_set, far_set], piece)
-    (far_out,) = update([far_set], pieces[-1], last=True)
-    (near_out,) = update([near_set], pieces[-1], last=True)
+    for piece in pieces[late:-2]:
+        (far_set,) = update([far_set], piece)
+    (far_out,) = update([far_set], pieces[-2] + pieces[-1], last=True)
+    (near_out,) = update([near_set], [p for piece in pieces[late:] for p in piece], last=True)
     far_out = [across(c, r) for c, r in zip(far_out, far)]
     near_out = [across(c, r) if r else c for c, r in zip(near_out, near)]
     return tuple(join_columns(near_out + far_out, peers, tokens))

time: 62.6 us -> 61.6 us (0.984)
  waiting for transfers between devices: 17.3 us -> 16.3 us
    ppermute x9, waiting for transfers between devices: 8.74 us -> 6.68 us  [across(): return lax.ppermute(chunk, 'head', [(h, h ^ r) for h in range(peers)])]
    ppermute x5, waiting for transfers between devices: 0.83 us -> 1.83 us  [step(): lax.ppermute(from_right, 'seq', left)]
  transfers between devices with their start and end apart: 19 -> 19, of which waited for: 8 -> 9; matrix products, arithmetic and copies ran while one was open for 4% -> 4% of each run, Pallas kernels for 31% -> 31%
where the time goes in v4:
time: 61.6 us; the launch traced here: 61 us
  Pallas kernels  22.8 us (37%)
  starting transfers between devices  17.9 us (29%)
  waiting for transfers between devices  16.3 us (26%)
  local copies, waits for them, and re-layouts  2.14 us (3%)
  between operations  1.67 us (3%)
    pallas_call x6, Pallas kernels, attend(): pl.pallas_call(kernel, in_specs=[pl.BlockSpec(memory_space=pltpu.SMEM)] *...  21.8 us
    ppermute x5, starting transfers between devices, step(): lax.ppermute(from_left, 'seq', right)  9.45 us
    ppermute x5, waiting for transfers between devices, step(): lax.ppermute(from_left, 'seq', right)  7.75 us
    ppermute x9, waiting for transfers between devices, across(): return lax.ppermute(chunk, 'head', [(h, h ^ r) for h in range(peers)])  6.68 us
    ppermute x9, starting transfers between devices, across(): return lax.ppermute(chunk, 'head', [(h, h ^ r) for h in range(peers)])  6.35 us
    ppermute x5, starting transfers between devices, step(): lax.ppermute(from_right, 'seq', left)  2.12 us
    dynamic_slice x2, local copies, waits for them, and re-layouts, split_columns(): lax.dynamic_slice_in_dim(a, (me ^ r) * cols, cols, 1)  2.06 us
    ppermute x5, waiting for transfers between devices, step(): lax.ppermute(from_right, 'seq', left)  1.83 us
  transfers between devices with their start and end apart: 19, of which 9 were waited for; matrix products, arithmetic and copies ran while one was open for 4% of the time, Pallas kernels for 31%

profile of v4, /device:TPU:0, one launch (start us, length us, event | category | flops | bytes accessed | tf_op | source)
XLA Modules:
  0.0 61.0 jit_solution(18276902792989974582)
XLA Ops:
  0.6 3.1 %collective-permute-start = (bf16[256,512]{1,0:T(8,128)(2,1)}, bf16[256,512]{1,0:T(8,128)(2,1)S(1)}, u32[]{:S(2)}, u32[]{:S(2)}) collective-permute-start(bf16[256,512]{1,0:T(8,128)(2,1)} %refs_2_.3), channel_id=1, source_target_pairs={{0,8},{8,16},{16,24},{24,28},{28,20},{20,12},{12,4},{4,0},{1,9},{9... | collective-permute-start | bytes 786440 | tf_op jit(solution)/shard_map/ppermute | solution.py:294
  3.7 0.9 %constant_dynamic-slice_fusion.8 = (bf16[32,512]{1,0:T(8,128)(2,1)S(1)}, bf16[32,512]{1,0:T(8,128)(2,1)S(1)}, bf16[32,512]{1,0:T(8,128)(2,1)S(1)}, bf16[32,512]{...) fusion(bf16[32,2048]{1,0:T(8,128)(2,1)} %param.10, ...), kind=kLoop, calls=%fused_computation.19 | loop fusion | bytes 524304 | tf_op jit(solution)/shard_map/dynamic_slice | solution.py:47
  4.7 2.0 %collective-permute-start.2 = (bf16[64,512]{1,0:T(8,128)(2,1)S(1)}, bf16[64,512]{1,0:T(8,128)(2,1)S(1)}, u32[]{:S(2)}, u32[]{:S(2)}) collective-permute-start(bf16[64,512]{1,0:T(8,128)(2,1)S(1)} %pad_maximum_fusion.9), channel_id=1, source_target_pairs={{0,2},{1,3},{2,0},{3,1},{4,6},{5,7},{6,4},{7,5},{8,10},{9,11},{10,... | collective-permute-start | bytes 196616 | tf_op jit(solution)/shard_map/ppermute | solution.py:291
  6.9 1.2 %constant_dynamic-slice_fusion = (bf16[32,2048]{1,0:T(8,128)(2,1)S(1)}, bf16[32,2048]{1,0:T(8,128)(2,1)S(1)}, bf16[32,2048]{1,0:T(8,128)(2,1)S(1)}, bf16[32,2048...) fusion(bf16[32,8192]{1,0:T(8,128)(2,1)S(1)} %copy-done.2, ...), kind=kLoop, calls=%fused_computation.11 | loop fusion | bytes 2097168 | tf_op jit(solution)/shard_map/dynamic_slice | solution.py:47
  8.2 1.2 %collective-permute-done.2 = bf16[64,512]{1,0:T(8,128)(2,1)S(1)} collective-permute-done((bf16[64,512]{1,0:T(8,128)(2,1)S(1)}, bf16[64,512]{1,0:T(8,128)(2,1)S(1)}, u32[]{:S(2)}, u32[]{:S(2)}) %collective-permute-start.2) | collective-permute-done | bytes 65568 | tf_op jit(solution)/shard_map/ppermute | solution.py:291
  9.4 1.4 %collective-permute-done.3 = bf16[64,512]{1,0:T(8,128)(2,1)S(1)} collective-permute-done((bf16[64,512]{1,0:T(8,128)(2,1)S(1)}, bf16[64,512]{1,0:T(8,128)(2,1)S(1)}, u32[]{:S(2)}, u32[]{:S(2)}) %collective-permute-start.3) | collective-permute-done | bytes 65568 | tf_op jit(solution)/shard_map/ppermute | solution.py:291
  10.9 0.8 %collective-permute-done.6.refs_4_ = bf16[256,512]{1,0:T(8,128)(2,1)S(1)} collective-permute-done((bf16[256,512]{1,0:T(8,128)(2,1)}, bf16[256,512]{1,0:T(8,128)(2,1)S(1)}, u32[]{:S(2)}, u32[]{:S(2)}) %collective-permute-start.6) | collective-permute-done | bytes 262176 | tf_op jit(solution)/shard_map/ppermute | solution.py:294
  11.8 1.6 %collective-permute-start.4 = (bf16[384,512]{1,0:T(8,128)(2,1)S(1)}, bf16[384,512]{1,0:T(8,128)(2,1)S(1)}, u32[]{:S(2)}, u32[]{:S(2)}) collective-permute-start(bf16[384,512]{1,0:T(8,128)(2,1)S(1)} %get-tuple-element.59), channel_id=1, source_target_pairs={{0,8},{8,16},{16,24},{24,28},{28,20},{20,12},{12,4},{4,0},{1,9},{9... | collective-permute-start | bytes 1179656 | tf_op jit(solution)/shard_map/ppermute | solution.py:294
  13.4 0.4 collective-permute-start.7
  13.8 1.5 %collective-permute-start.14 = (bf16[64,2048]{1,0:T(8,128)(2,1)S(1)}, bf16[64,2048]{1,0:T(8,128)(2,1)S(1)}, u32[]{:S(2)}, u32[]{:S(2)}) collective-permute-start(bf16[64,2048]{1,0:T(8,128)(2,1)S(1)} %pad_maximum_fusion.4), channel_id=1, source_target_pairs={{0,2},{1,3},{2,0},{3,1},{4,6},{5,7},{6,4},{7,5},{8,10},{9,11},{10,... | collective-permute-start | bytes 786440 | tf_op jit(solution)/shard_map/ppermute | solution.py:291
  15.4 0.3 collective-permute-start.15
  16.3 6.1 %collective-permute-done.4.refs_2_ = bf16[384,512]{1,0:T(8,128)(2,1)S(1)} collective-permute-done((bf16[384,512]{1,0:T(8,128)(2,1)S(1)}, bf16[384,512]{1,0:T(8,128)(2,1)S(1)}, u32[]{:S(2)}, u32[]{:S(2)}) %collective-permute-start.4) | collective-permute-done | bytes 393248 | tf_op jit(solution)/shard_map/ppermute | solution.py:294
  22.5 1.6 %collective-permute-start.5 = (bf16[384,512]{1,0:T(8,128)(2,1)S(1)}, bf16[384,512]{1,0:T(8,128)(2,1)S(1)}, u32[]{:S(2)}, u32[]{:S(2)}) collective-permute-start(bf16[384,512]{1,0:T(8,128)(2,1)S(1)} %collective-permute-done.4.refs_2_), channel_id=1, source_target_pairs={{0,8},{8,16},{16,24},{24,28},{28,20},{20,12},{12,4},{4,0},{1,9},{9... | collective-permute-start | bytes 1179656 | tf_op jit(solution)/shard_map/ppermute | solution.py:294
  24.1 0.5 collective-permute-start.8
  24.5 3.4 %attend.6 = (f32[2,2,128,512]{3,2,1,0:T(8,128)S(1)}, f32[2,2,8,512]{3,2,1,0:T(8,128)S(1)}, bf16[2,2,128,512]{3,2,1,0:T(8,128)(2,1)S(1)}) custom-call(s32[1]{0:T(128)S(6)} %copy.9.refs_0_, s32[1,4]{1,0:T(1,128)S(1)} %copy-done.1, bf16[256,512]{1,0:T(8,128)(2,1)S(1)} %copy-done, bf16[256,512]{1,0:T(8,128)(2,1)S(1)} %collective-permute-done.refs_3_, ...), custom_call_target="tpu_custom_call" | custom-call | flops 2147483648 | bytes 2097152 | tf_op jit(solution)/shard_map/attend/pallas_call | solution.py:242
  28.0 3.4 %attend.7 = (f32[2,2,128,512]{3,2,1,0:T(8,128)S(1)}, f32[2,2,8,512]{3,2,1,0:T(8,128)S(1)}, bf16[2,2,128,512]{3,2,1,0:T(8,128)(2,1)S(1)}) custom-call(s32[1]{0:T(128)S(6)} %copy.9.refs_0_, s32[1,4]{1,0:T(1,128)S(1)} %copy-done.1, bf16[256,512]{1,0:T(8,128)(2,1)S(1)} %copy-done, bf16[256,512]{1,0:T(8,128)(2,1)S(1)} %collective-permute-done.refs_3_, ...), custom_call_target="tpu_custom_call" | custom-call | flops 2147483648 | bytes 2097152 | tf_op jit(solution)/shard_map/attend/pallas_call | solution.py:242
  31.4 0.9 %collective-permute-done.5.refs_2_ = bf16[384,512]{1,0:T(8,128)(2,1)S(1)} collective-permute-done((bf16[384,512]{1,0:T(8,128)(2,1)S(1)}, bf16[384,512]{1,0:T(8,128)(2,1)S(1)}, u32[]{:S(2)}, u32[]{:S(2)}) %collective-permute-start.5) | collective-permute-done | bytes 393248 | tf_op jit(solution)/shard_map/ppermute | solution.py:294
  32.3 1.6 %collective-permute-start.9 = (bf16[256,512]{1,0:T(8,128)(2,1)S(1)}, bf16[256,512]{1,0:T(8,128)(2,1)S(1)}, u32[]{:S(2)}, u32[]{:S(2)}) collective-permute-start(bf16[256,512]{1,0:T(8,128)(2,1)S(1)} %slice.46), channel_id=1, source_target_pairs={{0,8},{8,16},{16,24},{24,28},{28,20},{20,12},{12,4},{4,0},{1,9},{9... | collective-permute-start | bytes 786440 | tf_op jit(solution)/shard_map/ppermute | solution.py:294
  33.9 0.5 collective-permute-start.10
  34.5 4.8 %attend.8 = (f32[2,2,128,512]{3,2,1,0:T(8,128)S(1)}, f32[2,2,8,512]{3,2,1,0:T(8,128)S(1)}, f32[2,2,128,512]{3,2,1,0:T(8,128)S(1)}, f32[2,2,8,512]{3,2,1,0:T(8,128)S(1)}) custom-call(s32[1]{0:T(128)S(6)} %copy.9.refs_0_, s32[1,4]{1,0:T(1,128)S(1)} %copy-done.1, bf16[384,512]{1,0:T(8,128)(2,1)S(1)} %collective-permute-done.4.refs_2_, ...), custom_call_target="tpu_custom_call" | custom-call | flops 3221225472 | bytes 4194304 | tf_op jit(solution)/shard_map/attend/pallas_call | solution.py:242
  39.3 0.7 %collective-permute-done.9.refs_4_.refs_2_ = bf16[256,512]{1,0:T(8,128)(2,1)S(1)} collective-permute-done((bf16[256,512]{1,0:T(8,128)(2,1)S(1)}, bf16[256,512]{1,0:T(8,128)(2,1)S(1)}, u32[]{:S(2)}, u32[]{:S(2)}) %collective-permute-start.9) | collective-permute-done | bytes 262176 | tf_op jit(solution)/shard_map/ppermute | solution.py:294
  40.0 1.6 %collective-permute-start.11 = (bf16[64,512]{1,0:T(8,128)(2,1)S(1)}, bf16[64,512]{1,0:T(8,128)(2,1)S(1)}, u32[]{:S(2)}, u32[]{:S(2)}) collective-permute-start(bf16[64,512]{1,0:T(8,128)(2,1)S(1)} %slice.48), channel_id=1, source_target_pairs={{0,8},{8,16},{16,24},{24,28},{28,20},{20,12},{12,4},{4,0},{1,9},{9... | collective-permute-start | bytes 196616 | tf_op jit(solution)/shard_map/ppermute | solution.py:294
  41.6 0.7 %collective-permute-start.12 = (bf16[64,512]{1,0:T(8,128)(2,1)S(1)}, bf16[64,512]{1,0:T(8,128)(2,1)S(1)}, u32[]{:S(2)}, u32[]{:S(2)}) collective-permute-start(bf16[64,512]{1,0:T(8,128)(2,1)S(1)} %slice.49), channel_id=1, source_target_pairs={{8,0},{16,8},{24,16},{28,24},{20,28},{12,20},{4,12},{0,4},{9,1},{1... | collective-permute-start | bytes 196616 | tf_op jit(solution)/shard_map/ppermute | solution.py:294
  42.3 2.8 %attend.10 = (f32[2,2,128,512]{3,2,1,0:T(8,128)S(1)}, f32[2,2,8,512]{3,2,1,0:T(8,128)S(1)}) custom-call(s32[1]{0:T(128)S(6)} %copy.9.refs_0_, s32[1,4]{1,0:T(1,128)S(1)} %copy-done.1, bf16[384,512]{1,0:T(8,128)(2,1)S(1)} %collective-permute-done.5.refs_2_, bf16[384,512]{1,0:T(8,128)(2,1)S(1)} %collective-permute-done.8.refs_3_, ...), custom_call_target="tpu_custom_call" | custom-call | flops 1610612736 | bytes 2097152 | tf_op jit(solution)/shard_map/attend/pallas_call | solution.py:242
  45.1 1.0 %collective-permute-done.12.refs_7_.refs_5_ = bf16[64,512]{1,0:T(8,128)(2,1)S(1)} collective-permute-done((bf16[64,512]{1,0:T(8,128)(2,1)S(1)}, bf16[64,512]{1,0:T(8,128)(2,1)S(1)}, u32[]{:S(2)}, u32[]{:S(2)}) %collective-permute-start.12) | collective-permute-done | bytes 65568 | tf_op jit(solution)/shard_map/ppermute | solution.py:294
  46.1 2.6 %attend.11 = (bf16[64,2048]{1,0:T(8,128)(2,1)S(1)}, bf16[64,2048]{1,0:T(8,128)(2,1)S(1)}) custom-call(s32[1]{0:T(128)S(6)} %copy.9.refs_0_, s32[1,4]{1,0:T(1,128)S(1)} %copy-done.1, bf16[256,512]{1,0:T(8,128)(2,1)S(1)} %collective-permute-done.9.refs_4_.refs_2_, bf16[256,512]{1,0:T(8,128)(2,1)S(1)} %collective-permute-done.10.refs_5_.refs_3_, ...), custom_call_target="tpu_custom_call" | custom-call | flops 1342177280 | bytes 2097152 | tf_op jit(solution)/shard_map/attend/pallas_call | solution.py:242
  48.7 1.6 %collective-permute-start.17 = (bf16[64,2048]{1,0:T(8,128)(2,1)S(1)}, bf16[64,2048]{1,0:T(8,128)(2,1)S(1)}, u32[]{:S(2)}, u32[]{:S(2)}) collective-permute-start(bf16[64,2048]{1,0:T(8,128)(2,1)S(1)} %get-tuple-element.48), channel_id=1, source_target_pairs={{0,2},{1,3},{2,0},{3,1},{4,6},{5,7},{6,4},{7,5},{8,10},{9,11},{10,... | collective-permute-start | bytes 786440 | tf_op jit(solution)/shard_map/ppermute | solution.py:291
  50.3 4.7 %attend.9 = (bf16[64,2048]{1,0:T(8,128)(2,1)S(1)}, bf16[64,2048]{1,0:T(8,128)(2,1)S(1)}) custom-call(s32[1]{0:T(128)S(6)} %copy.9.refs_0_, s32[1,4]{1,0:T(1,128)S(1)} %copy-done.1, bf16[384,512]{1,0:T(8,128)(2,1)S(1)} %collective-permute-done.5.refs_2_, bf16[384,512]{1,0:T(8,128)(2,1)S(1)} %collective-permute-done.8.refs_3_, ...), custom_call_target="tpu_custom_call" | custom-call | flops 2952790016 | bytes 2097152 | tf_op jit(solution)/shard_map/attend/pallas_call | solution.py:242
  55.0 0.7 %collective-permute-start.16 = (bf16[64,2048]{1,0:T(8,128)(2,1)S(1)}, bf16[64,2048]{1,0:T(8,128)(2,1)S(1)}, u32[]{:S(2)}, u32[]{:S(2)}) collective-permute-start(bf16[64,2048]{1,0:T(8,128)(2,1)S(1)} %get-tuple-element.43), channel_id=1, source_target_pairs={{0,1},{1,0},{2,3},{3,2},{4,5},{5,4},{6,7},{7,6},{8,9},{9,8},{10,11... | collective-permute-start | bytes 786440 | tf_op jit(solution)/shard_map/ppermute | solution.py:291
  55.7 1.3 %collective-permute-done.17.refs_2_ = bf16[64,2048]{1,0:T(8,128)(2,1)S(1)} collective-permute-done((bf16[64,2048]{1,0:T(8,128)(2,1)S(1)}, bf16[64,2048]{1,0:T(8,128)(2,1)S(1)}, u32[]{:S(2)}, u32[]{:S(2)}) %collective-permute-start.17) | collective-permute-done | bytes 262176 | tf_op jit(solution)/shard_map/ppermute | solution.py:291
  57.0 2.7 %collective-permute-done.18.refs_3_ = bf16[64,2048]{1,0:T(8,128)(2,1)S(1)} collective-permute-done((bf16[64,2048]{1,0:T(8,128)(2,1)S(1)}, bf16[64,2048]{1,0:T(8,128)(2,1)S(1)}, u32[]{:S(2)}, u32[]{:S(2)}) %collective-permute-start.18) | collective-permute-done | bytes 262176 | tf_op jit(solution)/shard_map/ppermute | solution.py:291
  59.8 1.0 %join_columns.1 = (bf16[32,8192]{1,0:T(8,128)(2,1)}, bf16[32,8192]{1,0:T(8,128)(2,1)}) custom-call(bf16[64,2048]{1,0:T(8,128)(2,1)S(1)} %get-tuple-element.42.refs_0_, bf16[64,2048]{1,0:T(8,128)(2,1)S(1)} %collective-permute-done.16.refs_1_, bf16[64,2048]{1,0:T(8,128)(2,1)S(1)} %collective-permute-done.17.refs_2_, ...), custom_call_target="tpu_custom_call" | custom-call | tf_op jit(solution)/shard_map/join_columns/pallas_call | solution.py:70
  (38 shorter events, 0.5 us)
Async XLA Ops:
  0.6 6.3 %copy-start.2 = (bf16[32,8192]{1,0:T(8,128)(2,1)S(1)}, bf16[32,8192]{1,0:T(8,128)(2,1)}, u32[]{:S(2)}) copy-start(bf16[32,8192]{1,0:T(8,128)(2,1)} %param.9) | copy-start | bytes 1572868
  0.6 10.2 %collective-permute-start = (bf16[256,512]{1,0:T(8,128)(2,1)}, bf16[256,512]{1,0:T(8,128)(2,1)S(1)}, u32[]{:S(2)}, u32[]{:S(2)}) collective-permute-start(bf16[256,512]{1,0:T(8,128)(2,1)} %refs_2_.3), channel_id=1, source_target_pairs={{0,8},{8,16},{16,24},{24,28},{28,20},{20,12},{12,4},{4,0},{1,9},{9... | collective-permute-start | bytes 786440 | tf_op jit(solution)/shard_map/ppermute | solution.py:294
  3.7 8.0 %collective-permute-start.6 = (bf16[256,512]{1,0:T(8,128)(2,1)}, bf16[256,512]{1,0:T(8,128)(2,1)S(1)}, u32[]{:S(2)}, u32[]{:S(2)}) collective-permute-start(bf16[256,512]{1,0:T(8,128)(2,1)} %refs_2_.3), channel_id=1, source_target_pairs={{8,0},{16,8},{24,16},{28,24},{20,28},{12,20},{4,12},{0,4},{9,1},{1... | collective-permute-start | bytes 786440 | tf_op jit(solution)/shard_map/ppermute | solution.py:294
  4.6 3.5 %collective-permute-start.1 = (bf16[64,512]{1,0:T(8,128)(2,1)S(1)}, bf16[64,512]{1,0:T(8,128)(2,1)S(1)}, u32[]{:S(2)}, u32[]{:S(2)}) collective-permute-start(bf16[64,512]{1,0:T(8,128)(2,1)S(1)} %pad_maximum_fusion.8), channel_id=1, source_target_pairs={{0,1},{1,0},{2,3},{3,2},{4,5},{5,4},{6,7},{7,6},{8,9},{9,8},{10,11... | collective-permute-start | bytes 196616 | tf_op jit(solution)/shard_map/ppermute | solution.py:291
  4.7 4.7 %collective-permute-start.2 = (bf16[64,512]{1,0:T(8,128)(2,1)S(1)}, bf16[64,512]{1,0:T(8,128)(2,1)S(1)}, u32[]{:S(2)}, u32[]{:S(2)}) collective-permute-start(bf16[64,512]{1,0:T(8,128)(2,1)S(1)} %pad_maximum_fusion.9), channel_id=1, source_target_pairs={{0,2},{1,3},{2,0},{3,1},{4,6},{5,7},{6,4},{7,5},{8,10},{9,11},{10,... | collective-permute-start | bytes 196616 | tf_op jit(solution)/shard_map/ppermute | solution.py:291
  6.8 4.1 %collective-permute-start.3 = (bf16[64,512]{1,0:T(8,128)(2,1)S(1)}, bf16[64,512]{1,0:T(8,128)(2,1)S(1)}, u32[]{:S(2)}, u32[]{:S(2)}) collective-permute-start(bf16[64,512]{1,0:T(8,128)(2,1)S(1)} %pad_maximum_fusion.10), channel_id=1, source_target_pairs={{0,3},{1,2},{2,1},{3,0},{4,7},{5,6},{6,5},{7,4},{8,11},{9,10},{10,... | collective-permute-start | bytes 196616 | tf_op jit(solution)/shard_map/ppermute | solution.py:291
  10.9 13.7 %copy-start = (bf16[256,512]{1,0:T(8,128)(2,1)S(1)}, bf16[256,512]{1,0:T(8,128)(2,1)}, u32[]{:S(2)}) copy-start(bf16[256,512]{1,0:T(8,128)(2,1)} %refs_2_.3) | copy-start | bytes 786436
  11.8 10.7 %collective-permute-start.4 = (bf16[384,512]{1,0:T(8,128)(2,1)S(1)}, bf16[384,512]{1,0:T(8,128)(2,1)S(1)}, u32[]{:S(2)}, u32[]{:S(2)}) collective-permute-start(bf16[384,512]{1,0:T(8,128)(2,1)S(1)} %get-tuple-element.59), channel_id=1, source_target_pairs={{0,8},{8,16},{16,24},{24,28},{28,20},{20,12},{12,4},{4,0},{1,9},{9... | collective-permute-start | bytes 1179656 | tf_op jit(solution)/shard_map/ppermute | solution.py:294
  13.4 11.1 %copy-start.1 = (s32[1,4]{1,0:T(1,128)S(1)}, s32[1,4]{1,0:T(1,128)}, u32[]{:S(2)}) copy-start(s32[1,4]{1,0:T(1,128)} %refs_1_.11) | copy-start | bytes 52
  13.4 10.7 %collective-permute-start.7 = (bf16[384,512]{1,0:T(8,128)(2,1)S(1)}, bf16[384,512]{1,0:T(8,128)(2,1)S(1)}, u32[]{:S(2)}, u32[]{:S(2)}) collective-permute-start(bf16[384,512]{1,0:T(8,128)(2,1)S(1)} %get-tuple-element.58), channel_id=1, source_target_pairs={{8,0},{16,8},{24,16},{28,24},{20,28},{12,20},{4,12},{0,4},{9,1},{1... | collective-permute-start | bytes 1179656 | tf_op jit(solution)/shard_map/ppermute | solution.py:294
  13.8 10.7 %collective-permute-start.13 = (bf16[64,2048]{1,0:T(8,128)(2,1)S(1)}, bf16[64,2048]{1,0:T(8,128)(2,1)S(1)}, u32[]{:S(2)}, u32[]{:S(2)}) collective-permute-start(bf16[64,2048]{1,0:T(8,128)(2,1)S(1)} %pad_maximum_fusion.3), channel_id=1, source_target_pairs={{0,1},{1,0},{2,3},{3,2},{4,5},{5,4},{6,7},{7,6},{8,9},{9,8},{10,11... | collective-permute-start | bytes 786440 | tf_op jit(solution)/shard_map/ppermute | solution.py:291
  13.8 14.1 %collective-permute-start.14 = (bf16[64,2048]{1,0:T(8,128)(2,1)S(1)}, bf16[64,2048]{1,0:T(8,128)(2,1)S(1)}, u32[]{:S(2)}, u32[]{:S(2)}) collective-permute-start(bf16[64,2048]{1,0:T(8,128)(2,1)S(1)} %pad_maximum_fusion.4), channel_id=1, source_target_pairs={{0,2},{1,3},{2,0},{3,1},{4,6},{5,7},{6,4},{7,5},{8,10},{9,11},{10,... | collective-permute-start | bytes 786440 | tf_op jit(solution)/shard_map/ppermute | solution.py:291
  15.4 12.6 %collective-permute-start.15 = (bf16[64,2048]{1,0:T(8,128)(2,1)S(1)}, bf16[64,2048]{1,0:T(8,128)(2,1)S(1)}, u32[]{:S(2)}, u32[]{:S(2)}) collective-permute-start(bf16[64,2048]{1,0:T(8,128)(2,1)S(1)} %pad_maximum_fusion.5), channel_id=1, source_target_pairs={{0,3},{1,2},{2,1},{3,0},{4,7},{5,6},{6,5},{7,4},{8,11},{9,10},{10,... | collective-permute-start | bytes 786440 | tf_op jit(solution)/shard_map/ppermute | solution.py:291
  22.5 9.8 %collective-permute-start.5 = (bf16[384,512]{1,0:T(8,128)(2,1)S(1)}, bf16[384,512]{1,0:T(8,128)(2,1)S(1)}, u32[]{:S(2)}, u32[]{:S(2)}) collective-permute-start(bf16[384,512]{1,0:T(8,128)(2,1)S(1)} %collective-permute-done.4.refs_2_), channel_id=1, source_target_pairs={{0,8},{8,16},{16,24},{24,28},{28,20},{20,12},{12,4},{4,0},{1,9},{9... | collective-permute-start | bytes 1179656 | tf_op jit(solution)/shard_map/ppermute | solution.py:294
  24.1 9.8 %collective-permute-start.8 = (bf16[384,512]{1,0:T(8,128)(2,1)S(1)}, bf16[384,512]{1,0:T(8,128)(2,1)S(1)}, u32[]{:S(2)}, u32[]{:S(2)}) collective-permute-start(bf16[384,512]{1,0:T(8,128)(2,1)S(1)} %collective-permute-done.7.refs_3_), channel_id=1, source_target_pairs={{8,0},{16,8},{24,16},{28,24},{20,28},{12,20},{4,12},{0,4},{9,1},{1... | collective-permute-start | bytes 1179656 | tf_op jit(solution)/shard_map/ppermute | solution.py:294
  32.3 7.7 %collective-permute-start.9 = (bf16[256,512]{1,0:T(8,128)(2,1)S(1)}, bf16[256,512]{1,0:T(8,128)(2,1)S(1)}, u32[]{:S(2)}, u32[]{:S(2)}) collective-permute-start(bf16[256,512]{1,0:T(8,128)(2,1)S(1)} %slice.46), channel_id=1, source_target_pairs={{0,8},{8,16},{16,24},{24,28},{28,20},{20,12},{12,4},{4,0},{1,9},{9... | collective-permute-start | bytes 786440 | tf_op jit(solution)/shard_map/ppermute | solution.py:294
  33.9 7.7 %collective-permute-start.10 = (bf16[256,512]{1,0:T(8,128)(2,1)S(1)}, bf16[256,512]{1,0:T(8,128)(2,1)S(1)}, u32[]{:S(2)}, u32[]{:S(2)}) collective-permute-start(bf16[256,512]{1,0:T(8,128)(2,1)S(1)} %slice.47), channel_id=1, source_target_pairs={{8,0},{16,8},{24,16},{28,24},{20,28},{12,20},{4,12},{0,4},{9,1},{1... | collective-permute-start | bytes 786440 | tf_op jit(solution)/shard_map/ppermute | solution.py:294
  40.0 5.1 %collective-permute-start.11 = (bf16[64,512]{1,0:T(8,128)(2,1)S(1)}, bf16[64,512]{1,0:T(8,128)(2,1)S(1)}, u32[]{:S(2)}, u32[]{:S(2)}) collective-permute-start(bf16[64,512]{1,0:T(8,128)(2,1)S(1)} %slice.48), channel_id=1, source_target_pairs={{0,8},{8,16},{16,24},{24,28},{28,20},{20,12},{12,4},{4,0},{1,9},{9... | collective-permute-start | bytes 196616 | tf_op jit(solution)/shard_map/ppermute | solution.py:294
  41.6 4.5 %collective-permute-start.12 = (bf16[64,512]{1,0:T(8,128)(2,1)S(1)}, bf16[64,512]{1,0:T(8,128)(2,1)S(1)}, u32[]{:S(2)}, u32[]{:S(2)}) collective-permute-start(bf16[64,512]{1,0:T(8,128)(2,1)S(1)} %slice.49), channel_id=1, source_target_pairs={{8,0},{16,8},{24,16},{28,24},{20,28},{12,20},{4,12},{0,4},{9,1},{1... | collective-permute-start | bytes 196616 | tf_op jit(solution)/shard_map/ppermute | solution.py:294
  48.7 8.3 %collective-permute-start.17 = (bf16[64,2048]{1,0:T(8,128)(2,1)S(1)}, bf16[64,2048]{1,0:T(8,128)(2,1)S(1)}, u32[]{:S(2)}, u32[]{:S(2)}) collective-permute-start(bf16[64,2048]{1,0:T(8,128)(2,1)S(1)} %get-tuple-element.48), channel_id=1, source_target_pairs={{0,2},{1,3},{2,0},{3,1},{4,6},{5,7},{6,4},{7,5},{8,10},{9,11},{10,... | collective-permute-start | bytes 786440 | tf_op jit(solution)/shard_map/ppermute | solution.py:291
  50.3 9.4 %collective-permute-start.18 = (bf16[64,2048]{1,0:T(8,128)(2,1)S(1)}, bf16[64,2048]{1,0:T(8,128)(2,1)S(1)}, u32[]{:S(2)}, u32[]{:S(2)}) collective-permute-start(bf16[64,2048]{1,0:T(8,128)(2,1)S(1)} %get-tuple-element.49), channel_id=1, source_target_pairs={{0,3},{1,2},{2,1},{3,0},{4,7},{5,6},{6,5},{7,4},{8,11},{9,10},{10,... | collective-permute-start | bytes 786440 | tf_op jit(solution)/shard_map/ppermute | solution.py:291
  55.0 4.7 %collective-permute-start.16 = (bf16[64,2048]{1,0:T(8,128)(2,1)S(1)}, bf16[64,2048]{1,0:T(8,128)(2,1)S(1)}, u32[]{:S(2)}, u32[]{:S(2)}) collective-permute-start(bf16[64,2048]{1,0:T(8,128)(2,1)S(1)} %get-tuple-element.43), channel_id=1, source_target_pairs={{0,1},{1,0},{2,3},{3,2},{4,5},{5,4},{6,7},{7,6},{8,9},{9,8},{10,11... | collective-permute-start | bytes 786440 | tf_op jit(solution)/shard_map/ppermute | solution.py:291

commit v5 on v4

--- a/solution.py
+++ b/solution.py
@@ -307,37 +307,36 @@
     own, queries = lax.optimization_barrier((own, queries))
     queries = [queries[0]] + [across(queries[r], r) for r in range(1, peers)]
 
+    near_by = step(own[0], own[0])
     pieces = [[(prefix_key_values, [(0, prefix_tokens, None)])] + [(p, [(0, prefix_tokens, None)]) for p in first]]
-    cut = prefix_tokens // 2
-    moving = jnp.concatenate([first[0], own[0]], axis=0), jnp.concatenate([own[0], first[1]], axis=0)
-    for k in range(2, half + 1):
-        count = prefix_tokens
-        if k == half:
-            count = cut
-            moving = moving[0][cut:], moving[1][: seat_tokens + cut]
-        moving = step(*moving)
-        pieces.append(
-            [
-                (moving[0], [(0, count, None), (count, seat_tokens, seers(k - 1, 0))]),
-                (moving[1], [(0, seat_tokens, seers(k - 1, 1)), (seat_tokens, count, None)]),
-            ]
-        )
-    moving = step(moving[0][cut : cut + seat_tokens // 2], moving[1][seat_tokens // 2 : seat_tokens])
-    pieces.append([(m, [(0, seat_tokens // 2, seers(half, side))]) for side, m in enumerate(moving)])
-
+    pieces[0] += [(p, [(0, seat_tokens, seers(1, side))]) for side, p in enumerate(near_by)]
+    moving = [jnp.concatenate([p, q], axis=0) for p, q in zip(first, near_by)]
     def update(sets, piece, own=None, last=False):
         return attend(set_length, passage_first_slot, peers, sets, piece, own, last)
 
     near_set, far_set = (near, [queries[r] for r in near], None), (far, [queries[r] for r in far], None)
     (near_set,) = update([near_set], pieces[0], own)
+    for k in range(2, half + 1):
+        spans = [[(0, prefix_tokens, None), (prefix_tokens, seat_tokens, seers(k, side))] for side in range(2)]
+        if k == half:
+            cut = prefix_tokens // 2 + seat_tokens // 2
+            moving = moving[0][:cut], moving[1][cut:]
+            spans[0] = [(0, cut, None)]
+            spans[1] = [(0, prefix_tokens - cut, None), (prefix_tokens - cut, seat_tokens, seers(k, 1))]
+        moving = step(*moving)
+        if k == 2:
+            moving, near_queries = lax.optimization_barrier((moving, near_set[1]))
+            near_set = (near, near_queries, near_set[2])
+        pieces.append(list(zip(moving, spans)))
+
     far_set = (far, lax.optimization_barrier((far_set[1], pieces[1][0][0]))[0], None)
     (far_set,) = update([far_set], pieces[0], own)
-    late = max(1, len(pieces) - 3)
+    late = max(1, len(pieces) - 2)
     for piece in pieces[1:late]:
         near_set, far_set = update([near_set, far_set], piece)
-    for piece in pieces[late:-2]:
+    for piece in pieces[late:-1]:
         (far_set,) = update([far_set], piece)
-    (far_out,) = update([far_set], pieces[-2] + pieces[-1], last=True)
+    (far_out,) = update([far_set], pieces[-1], last=True)
     (near_out,) = update([near_set], [p for piece in pieces[late:] for p in piece], last=True)
     far_out = [across(c, r) for c, r in zip(far_out, far)]
     near_out = [across(c, r) if r else c for c, r in zip(near_out, near)]

time: 61.6 us -> 67.9 us (1.10)
  waiting for transfers between devices: 16.3 us -> 23.6 us
    ppermute x9, waiting for transfers between devices: 6.68 us -> 16.6 us  [across(): return lax.ppermute(chunk, 'head', [(h, h ^ r) for h in range(peers)])]
    ppermute x5, starting transfers between devices: 2.12 us -> 9.19 us  [step(): lax.ppermute(from_right, 'seq', left)]
    ppermute x5, starting transfers between devices: 9.45 us -> 2.49 us  [step(): lax.ppermute(from_left, 'seq', right)]
    ppermute x5, waiting for transfers between devices: 7.75 us -> 1.59 us  [step(): lax.ppermute(from_left, 'seq', right)]
    ppermute x5, waiting for transfers between devices: 1.83 us -> 5.44 us  [step(): lax.ppermute(from_right, 'seq', left)]
  transfers between devices with their start and end apart: 19 -> 19, of which waited for: 9 -> 9; matrix products, arithmetic and copies ran while one was open for 4% -> 3% of each run, Pallas kernels for 31% -> 26%
where the time goes in v5:
time: 67.9 us; the launch traced here: 67.6 us
  waiting for transfers between devices  23.6 us (35%)
  Pallas kernels  22.7 us (33%)
  starting transfers between devices  17.4 us (26%)
  local copies, waits for them, and re-layouts  2.12 us (3%)
  between operations  1.66 us (2%)
    pallas_call x6, Pallas kernels, attend(): pl.pallas_call(kernel, in_specs=[pl.BlockSpec(memory_space=pltpu.SMEM)] *...  21.7 us
    ppermute x9, waiting for transfers between devices, across(): return lax.ppermute(chunk, 'head', [(h, h ^ r) for h in range(peers)])  16.6 us
    ppermute x5, starting transfers between devices, step(): lax.ppermute(from_right, 'seq', left)  9.19 us
    ppermute x9, starting transfers between devices, across(): return lax.ppermute(chunk, 'head', [(h, h ^ r) for h in range(peers)])  5.68 us
    ppermute x5, waiting for transfers between devices, step(): lax.ppermute(from_right, 'seq', left)  5.44 us
    ppermute x5, starting transfers between devices, step(): lax.ppermute(from_left, 'seq', right)  2.49 us
    dynamic_slice x2, local copies, waits for them, and re-layouts, split_columns(): lax.dynamic_slice_in_dim(a, (me ^ r) * cols, cols, 1)  2.06 us
    ppermute x5, waiting for transfers between devices, step(): lax.ppermute(from_left, 'seq', right)  1.59 us
  transfers between devices with their start and end apart: 19, of which 9 were waited for; matrix products, arithmetic and copies ran while one was open for 3% of the time, Pallas kernels for 26%

profile of v5, /device:TPU:0, one launch (start us, length us, event | category | flops | bytes accessed | tf_op | source)
XLA Modules:
  0.0 67.6 jit_solution(17264208972014055168)
XLA Ops:
  0.6 3.0 %collective-permute-start.6 = (bf16[256,512]{1,0:T(8,128)(2,1)}, bf16[256,512]{1,0:T(8,128)(2,1)S(1)}, u32[]{:S(2)}, u32[]{:S(2)}) collective-permute-start(bf16[256,512]{1,0:T(8,128)(2,1)} %refs_2_.3), channel_id=1, source_target_pairs={{8,0},{16,8},{24,16},{28,24},{20,28},{12,20},{4,12},{0,4},{9,1},{1... | collective-permute-start | bytes 786440 | tf_op jit(solution)/shard_map/ppermute | solution.py:294
  3.8 0.9 %constant_dynamic-slice_fusion.8 = (bf16[32,512]{1,0:T(8,128)(2,1)S(1)}, bf16[32,512]{1,0:T(8,128)(2,1)S(1)}, bf16[32,512]{1,0:T(8,128)(2,1)S(1)}, bf16[32,512]{...) fusion(bf16[32,2048]{1,0:T(8,128)(2,1)} %param.10, ...), kind=kLoop, calls=%fused_computation.19 | loop fusion | bytes 524304 | tf_op jit(solution)/shard_map/dynamic_slice | solution.py:47
  4.7 0.8 %collective-permute-start.3 = (bf16[64,512]{1,0:T(8,128)(2,1)S(1)}, bf16[64,512]{1,0:T(8,128)(2,1)S(1)}, u32[]{:S(2)}, u32[]{:S(2)}) collective-permute-start(bf16[64,512]{1,0:T(8,128)(2,1)S(1)} %pad_maximum_fusion.10), channel_id=1, source_target_pairs={{0,3},{1,2},{2,1},{3,0},{4,7},{5,6},{6,5},{7,4},{8,11},{9,10},{10,... | collective-permute-start | bytes 196616 | tf_op jit(solution)/shard_map/ppermute | solution.py:291
  5.5 1.2 %collective-permute-start.1 = (bf16[64,512]{1,0:T(8,128)(2,1)S(1)}, bf16[64,512]{1,0:T(8,128)(2,1)S(1)}, u32[]{:S(2)}, u32[]{:S(2)}) collective-permute-start(bf16[64,512]{1,0:T(8,128)(2,1)S(1)} %pad_maximum_fusion.8), channel_id=1, source_target_pairs={{0,1},{1,0},{2,3},{3,2},{4,5},{5,4},{6,7},{7,6},{8,9},{9,8},{10,11... | collective-permute-start | bytes 196616 | tf_op jit(solution)/shard_map/ppermute | solution.py:291
  6.9 1.2 %constant_dynamic-slice_fusion = (bf16[32,2048]{1,0:T(8,128)(2,1)S(1)}, bf16[32,2048]{1,0:T(8,128)(2,1)S(1)}, bf16[32,2048]{1,0:T(8,128)(2,1)S(1)}, bf16[32,2048...) fusion(bf16[32,8192]{1,0:T(8,128)(2,1)S(1)} %copy-done.2, ...), kind=kLoop, calls=%fused_computation.11 | loop fusion | bytes 2097168 | tf_op jit(solution)/shard_map/dynamic_slice | solution.py:47
  8.2 0.6 collective-permute-done.3
  8.8 2.3 %collective-permute-done.2 = bf16[64,512]{1,0:T(8,128)(2,1)S(1)} collective-permute-done((bf16[64,512]{1,0:T(8,128)(2,1)S(1)}, bf16[64,512]{1,0:T(8,128)(2,1)S(1)}, u32[]{:S(2)}, u32[]{:S(2)}) %collective-permute-start.2) | collective-permute-done | bytes 65568 | tf_op jit(solution)/shard_map/ppermute | solution.py:291
  11.1 1.5 %collective-permute-start.7 = (bf16[128,512]{1,0:T(8,128)(2,1)S(1)}, bf16[128,512]{1,0:T(8,128)(2,1)S(1)}, u32[]{:S(2)}, u32[]{:S(2)}) collective-permute-start(bf16[128,512]{1,0:T(8,128)(2,1)S(1)} %pad_maximum_fusion.6.refs_7_), channel_id=1, source_target_pairs={{8,0},{16,8},{24,16},{28,24},{20,28},{12,20},{4,12},{0,4},{9,1},{1... | collective-permute-start | bytes 393224 | tf_op jit(solution)/shard_map/ppermute | solution.py:294
  12.6 0.5 collective-permute-start.4
  13.2 2.9 %collective-permute-done.7.refs_6_ = bf16[128,512]{1,0:T(8,128)(2,1)S(1)} collective-permute-done((bf16[128,512]{1,0:T(8,128)(2,1)S(1)}, bf16[128,512]{1,0:T(8,128)(2,1)S(1)}, u32[]{:S(2)}, u32[]{:S(2)}) %collective-permute-start.7) | collective-permute-done | bytes 131104 | tf_op jit(solution)/shard_map/ppermute | solution.py:294
  16.2 1.5 %collective-permute-start.8 = (bf16[384,512]{1,0:T(8,128)(2,1)S(1)}, bf16[384,512]{1,0:T(8,128)(2,1)S(1)}, u32[]{:S(2)}, u32[]{:S(2)}) collective-permute-start(bf16[384,512]{1,0:T(8,128)(2,1)S(1)} %pad_maximum_fusion.1), channel_id=1, source_target_pairs={{8,0},{16,8},{24,16},{28,24},{20,28},{12,20},{4,12},{0,4},{9,1},{1... | collective-permute-start | bytes 1179656 | tf_op jit(solution)/shard_map/ppermute | solution.py:294
  17.8 0.6 collective-permute-start.5
  19.0 1.5 %collective-permute-start.14 = (bf16[64,2048]{1,0:T(8,128)(2,1)S(1)}, bf16[64,2048]{1,0:T(8,128)(2,1)S(1)}, u32[]{:S(2)}, u32[]{:S(2)}) collective-permute-start(bf16[64,2048]{1,0:T(8,128)(2,1)S(1)} %pad_maximum_fusion.4), channel_id=1, source_target_pairs={{0,2},{1,3},{2,0},{3,1},{4,6},{5,7},{6,4},{7,5},{8,10},{9,11},{10,... | collective-permute-start | bytes 786440 | tf_op jit(solution)/shard_map/ppermute | solution.py:291
  20.5 4.0 %attend.6 = (f32[2,2,128,512]{3,2,1,0:T(8,128)S(1)}, f32[2,2,8,512]{3,2,1,0:T(8,128)S(1)}, bf16[2,2,128,512]{3,2,1,0:T(8,128)(2,1)S(1)}) custom-call(s32[1]{0:T(128)S(6)} %copy.9.refs_0_, s32[1,4]{1,0:T(1,128)S(1)} %copy-done.1, bf16[256,512]{1,0:T(8,128)(2,1)S(1)} %copy-done, bf16[256,512]{1,0:T(8,128)(2,1)S(1)} %collective-permute-done.refs_3_, ...), custom_call_target="tpu_custom_call" | custom-call | flops 2684354560 | bytes 2097152 | tf_op jit(solution)/shard_map/attend/pallas_call | solution.py:242
  24.5 0.8 %collective-permute-done.8.refs_3_ = bf16[384,512]{1,0:T(8,128)(2,1)S(1)} collective-permute-done((bf16[384,512]{1,0:T(8,128)(2,1)S(1)}, bf16[384,512]{1,0:T(8,128)(2,1)S(1)}, u32[]{:S(2)}, u32[]{:S(2)}) %collective-permute-start.8) | collective-permute-done | bytes 393248 | tf_op jit(solution)/shard_map/ppermute | solution.py:294
  25.3 1.6 %collective-permute-done.5.refs_2_ = bf16[384,512]{1,0:T(8,128)(2,1)S(1)} collective-permute-done((bf16[384,512]{1,0:T(8,128)(2,1)S(1)}, bf16[384,512]{1,0:T(8,128)(2,1)S(1)}, u32[]{:S(2)}, u32[]{:S(2)}) %collective-permute-start.5) | collective-permute-done | bytes 393248 | tf_op jit(solution)/shard_map/ppermute | solution.py:294
  26.9 1.6 %collective-permute-start.11 = (bf16[384,512]{1,0:T(8,128)(2,1)S(1)}, bf16[384,512]{1,0:T(8,128)(2,1)S(1)}, u32[]{:S(2)}, u32[]{:S(2)}) collective-permute-start(bf16[384,512]{1,0:T(8,128)(2,1)S(1)} %collective-permute-done.8.refs_3_), channel_id=1, source_target_pairs={{8,0},{16,8},{24,16},{28,24},{20,28},{12,20},{4,12},{0,4},{9,1},{1... | collective-permute-start | bytes 1179656 | tf_op jit(solution)/shard_map/ppermute | solution.py:294
  28.5 0.4 collective-permute-start.10
  28.9 1.7 %collective-permute-done.15.refs_10_ = bf16[64,2048]{1,0:T(8,128)(2,1)S(1)} collective-permute-done((bf16[64,2048]{1,0:T(8,128)(2,1)S(1)}, bf16[64,2048]{1,0:T(8,128)(2,1)S(1)}, u32[]{:S(2)}, u32[]{:S(2)}) %collective-permute-start.15) | collective-permute-done | bytes 262176 | tf_op jit(solution)/shard_map/ppermute | solution.py:291
  30.6 4.0 %attend.7 = (f32[2,2,128,512]{3,2,1,0:T(8,128)S(1)}, f32[2,2,8,512]{3,2,1,0:T(8,128)S(1)}, bf16[2,2,128,512]{3,2,1,0:T(8,128)(2,1)S(1)}) custom-call(s32[1]{0:T(128)S(6)} %copy.9.refs_0_, s32[1,4]{1,0:T(1,128)S(1)} %copy-done.1, bf16[256,512]{1,0:T(8,128)(2,1)S(1)} %copy-done, bf16[256,512]{1,0:T(8,128)(2,1)S(1)} %collective-permute-done.refs_3_, ...), custom_call_target="tpu_custom_call" | custom-call | flops 2684354560 | bytes 2097152 | tf_op jit(solution)/shard_map/attend/pallas_call | solution.py:242
  34.6 1.7 %collective-permute-done.11.refs_3_ = bf16[384,512]{1,0:T(8,128)(2,1)S(1)} collective-permute-done((bf16[384,512]{1,0:T(8,128)(2,1)S(1)}, bf16[384,512]{1,0:T(8,128)(2,1)S(1)}, u32[]{:S(2)}, u32[]{:S(2)}) %collective-permute-start.11) | collective-permute-done | bytes 393248 | tf_op jit(solution)/shard_map/ppermute | solution.py:294
  36.4 1.5 %collective-permute-start.13 = (bf16[192,512]{1,0:T(8,128)(2,1)S(1)}, bf16[192,512]{1,0:T(8,128)(2,1)S(1)}, u32[]{:S(2)}, u32[]{:S(2)}) collective-permute-start(bf16[192,512]{1,0:T(8,128)(2,1)S(1)} %slice.39), channel_id=1, source_target_pairs={{8,0},{16,8},{24,16},{28,24},{20,28},{12,20},{4,12},{0,4},{9,1},{1... | collective-permute-start | bytes 589832 | tf_op jit(solution)/shard_map/ppermute | solution.py:294
  37.9 0.8 %collective-permute-start.12 = (bf16[192,512]{1,0:T(8,128)(2,1)S(1)}, bf16[192,512]{1,0:T(8,128)(2,1)S(1)}, u32[]{:S(2)}, u32[]{:S(2)}) collective-permute-start(bf16[192,512]{1,0:T(8,128)(2,1)S(1)} %slice.38), channel_id=1, source_target_pairs={{0,8},{8,16},{16,24},{24,28},{28,20},{20,12},{12,4},{4,0},{1,9},{9... | collective-permute-start | bytes 589832 | tf_op jit(solution)/shard_map/ppermute | solution.py:294
  38.7 4.8 %attend.8 = (f32[2,2,128,512]{3,2,1,0:T(8,128)S(1)}, f32[2,2,8,512]{3,2,1,0:T(8,128)S(1)}, f32[2,2,128,512]{3,2,1,0:T(8,128)S(1)}, f32[2,2,8,512]{3,2,1,0:T(8,128)S(1)}) custom-call(s32[1]{0:T(128)S(6)} %copy.9.refs_0_, s32[1,4]{1,0:T(1,128)S(1)} %copy-done.1, bf16[384,512]{1,0:T(8,128)(2,1)S(1)} %collective-permute-done.5.refs_2_, ...), custom_call_target="tpu_custom_call" | custom-call | flops 3221225472 | bytes 4194304 | tf_op jit(solution)/shard_map/attend/pallas_call | solution.py:242
  43.5 2.8 %attend.10 = (f32[2,2,128,512]{3,2,1,0:T(8,128)S(1)}, f32[2,2,8,512]{3,2,1,0:T(8,128)S(1)}) custom-call(s32[1]{0:T(128)S(6)} %copy.9.refs_0_, s32[1,4]{1,0:T(1,128)S(1)} %copy-done.1, bf16[384,512]{1,0:T(8,128)(2,1)S(1)} %collective-permute-done.10.refs_2_, bf16[384,512]{1,0:T(8,128)(2,1)S(1)} %collective-permute-done.11.refs_3_, ...), custom_call_target="tpu_custom_call" | custom-call | flops 1610612736 | bytes 2097152 | tf_op jit(solution)/shard_map/attend/pallas_call | solution.py:242
  46.3 4.0 %attend.9 = (bf16[64,2048]{1,0:T(8,128)(2,1)S(1)}, bf16[64,2048]{1,0:T(8,128)(2,1)S(1)}) custom-call(s32[1]{0:T(128)S(6)} %copy.9.refs_0_, s32[1,4]{1,0:T(1,128)S(1)} %copy-done.1, bf16[384,512]{1,0:T(8,128)(2,1)S(1)} %collective-permute-done.10.refs_2_, bf16[384,512]{1,0:T(8,128)(2,1)S(1)} %collective-permute-done.11.refs_3_, ...), custom_call_target="tpu_custom_call" | custom-call | flops 2415919104 | bytes 2097152 | tf_op jit(solution)/shard_map/attend/pallas_call | solution.py:242
  50.4 2.0 %attend.11 = (bf16[64,2048]{1,0:T(8,128)(2,1)S(1)}, bf16[64,2048]{1,0:T(8,128)(2,1)S(1)}) custom-call(s32[1]{0:T(128)S(6)} %copy.9.refs_0_, s32[1,4]{1,0:T(1,128)S(1)} %copy-done.1, bf16[192,512]{1,0:T(8,128)(2,1)S(1)} %collective-permute-done.12.refs_4_.refs_2_, bf16[192,512]{1,0:T(8,128)(2,1)S(1)} %collective-permute-done.13.refs_5_.refs_3_, ...), custom_call_target="tpu_custom_call" | custom-call | flops 805306368 | bytes 2097152 | tf_op jit(solution)/shard_map/attend/pallas_call | solution.py:242
  52.5 1.5 %collective-permute-start.17 = (bf16[64,2048]{1,0:T(8,128)(2,1)S(1)}, bf16[64,2048]{1,0:T(8,128)(2,1)S(1)}, u32[]{:S(2)}, u32[]{:S(2)}) collective-permute-start(bf16[64,2048]{1,0:T(8,128)(2,1)S(1)} %get-tuple-element.54), channel_id=1, source_target_pairs={{0,2},{1,3},{2,0},{3,1},{4,6},{5,7},{6,4},{7,5},{8,10},{9,11},{10,... | collective-permute-start | bytes 786440 | tf_op jit(solution)/shard_map/ppermute | solution.py:291
  53.9 0.4 collective-permute-start.18
  54.4 7.3 %collective-permute-done.17.refs_2_ = bf16[64,2048]{1,0:T(8,128)(2,1)S(1)} collective-permute-done((bf16[64,2048]{1,0:T(8,128)(2,1)S(1)}, bf16[64,2048]{1,0:T(8,128)(2,1)S(1)}, u32[]{:S(2)}, u32[]{:S(2)}) %collective-permute-start.17) | collective-permute-done | bytes 262176 | tf_op jit(solution)/shard_map/ppermute | solution.py:291
  61.6 4.8 %collective-permute-done.18.refs_3_ = bf16[64,2048]{1,0:T(8,128)(2,1)S(1)} collective-permute-done((bf16[64,2048]{1,0:T(8,128)(2,1)S(1)}, bf16[64,2048]{1,0:T(8,128)(2,1)S(1)}, u32[]{:S(2)}, u32[]{:S(2)}) %collective-permute-start.18) | collective-permute-done | bytes 262176 | tf_op jit(solution)/shard_map/ppermute | solution.py:291
  66.5 1.0 %join_columns.1 = (bf16[32,8192]{1,0:T(8,128)(2,1)}, bf16[32,8192]{1,0:T(8,128)(2,1)}) custom-call(bf16[64,2048]{1,0:T(8,128)(2,1)S(1)} %get-tuple-element.48.refs_0_, bf16[64,2048]{1,0:T(8,128)(2,1)S(1)} %collective-permute-done.16.refs_1_, bf16[64,2048]{1,0:T(8,128)(2,1)S(1)} %collective-permute-done.17.refs_2_, ...), custom_call_target="tpu_custom_call" | custom-call | tf_op jit(solution)/shard_map/join_columns/pallas_call | solution.py:70
  (37 shorter events, 0.6 us)
Async XLA Ops:
  0.6 6.3 %copy-start.2 = (bf16[32,8192]{1,0:T(8,128)(2,1)S(1)}, bf16[32,8192]{1,0:T(8,128)(2,1)}, u32[]{:S(2)}) copy-start(bf16[32,8192]{1,0:T(8,128)(2,1)} %param.9) | copy-start | bytes 1572868
  0.6 15.5 %collective-permute-start.6 = (bf16[256,512]{1,0:T(8,128)(2,1)}, bf16[256,512]{1,0:T(8,128)(2,1)S(1)}, u32[]{:S(2)}, u32[]{:S(2)}) collective-permute-start(bf16[256,512]{1,0:T(8,128)(2,1)} %refs_2_.3), channel_id=1, source_target_pairs={{8,0},{16,8},{24,16},{28,24},{20,28},{12,20},{4,12},{0,4},{9,1},{1... | collective-permute-start | bytes 786440 | tf_op jit(solution)/shard_map/ppermute | solution.py:294
  3.6 14.1 %collective-permute-start = (bf16[256,512]{1,0:T(8,128)(2,1)}, bf16[256,512]{1,0:T(8,128)(2,1)S(1)}, u32[]{:S(2)}, u32[]{:S(2)}) collective-permute-start(bf16[256,512]{1,0:T(8,128)(2,1)} %refs_2_.3), channel_id=1, source_target_pairs={{0,8},{8,16},{16,24},{24,28},{28,20},{20,12},{12,4},{4,0},{1,9},{9... | collective-permute-start | bytes 786440 | tf_op jit(solution)/shard_map/ppermute | solution.py:294
  4.7 4.1 %collective-permute-start.3 = (bf16[64,512]{1,0:T(8,128)(2,1)S(1)}, bf16[64,512]{1,0:T(8,128)(2,1)S(1)}, u32[]{:S(2)}, u32[]{:S(2)}) collective-permute-start(bf16[64,512]{1,0:T(8,128)(2,1)S(1)} %pad_maximum_fusion.10), channel_id=1, source_target_pairs={{0,3},{1,2},{2,1},{3,0},{4,7},{5,6},{6,5},{7,4},{8,11},{9,10},{10,... | collective-permute-start | bytes 196616 | tf_op jit(solution)/shard_map/ppermute | solution.py:291
  5.5 3.2 %collective-permute-start.1 = (bf16[64,512]{1,0:T(8,128)(2,1)S(1)}, bf16[64,512]{1,0:T(8,128)(2,1)S(1)}, u32[]{:S(2)}, u32[]{:S(2)}) collective-permute-start(bf16[64,512]{1,0:T(8,128)(2,1)S(1)} %pad_maximum_fusion.8), channel_id=1, source_target_pairs={{0,1},{1,0},{2,3},{3,2},{4,5},{5,4},{6,7},{7,6},{8,9},{9,8},{10,11... | collective-permute-start | bytes 196616 | tf_op jit(solution)/shard_map/ppermute | solution.py:291
  6.8 4.3 %collective-permute-start.2 = (bf16[64,512]{1,0:T(8,128)(2,1)S(1)}, bf16[64,512]{1,0:T(8,128)(2,1)S(1)}, u32[]{:S(2)}, u32[]{:S(2)}) collective-permute-start(bf16[64,512]{1,0:T(8,128)(2,1)S(1)} %pad_maximum_fusion.9), channel_id=1, source_target_pairs={{0,2},{1,3},{2,0},{3,1},{4,6},{5,7},{6,4},{7,5},{8,10},{9,11},{10,... | collective-permute-start | bytes 196616 | tf_op jit(solution)/shard_map/ppermute | solution.py:291
  11.1 5.0 %collective-permute-start.7 = (bf16[128,512]{1,0:T(8,128)(2,1)S(1)}, bf16[128,512]{1,0:T(8,128)(2,1)S(1)}, u32[]{:S(2)}, u32[]{:S(2)}) collective-permute-start(bf16[128,512]{1,0:T(8,128)(2,1)S(1)} %pad_maximum_fusion.6.refs_7_), channel_id=1, source_target_pairs={{8,0},{16,8},{24,16},{28,24},{20,28},{12,20},{4,12},{0,4},{9,1},{1... | collective-permute-start | bytes 393224 | tf_op jit(solution)/shard_map/ppermute | solution.py:294
  12.6 5.1 %collective-permute-start.4 = (bf16[128,512]{1,0:T(8,128)(2,1)S(1)}, bf16[128,512]{1,0:T(8,128)(2,1)S(1)}, u32[]{:S(2)}, u32[]{:S(2)}) collective-permute-start(bf16[128,512]{1,0:T(8,128)(2,1)S(1)} %pad_maximum_fusion.6.refs_7_), channel_id=1, source_target_pairs={{0,8},{8,16},{16,24},{24,28},{28,20},{20,12},{12,4},{4,0},{1,9},{9... | collective-permute-start | bytes 393224 | tf_op jit(solution)/shard_map/ppermute | solution.py:294
  13.2 7.3 %collective-permute-start.9 = (bf16[64,2048]{1,0:T(8,128)(2,1)S(1)}, bf16[64,2048]{1,0:T(8,128)(2,1)S(1)}, u32[]{:S(2)}, u32[]{:S(2)}) collective-permute-start(bf16[64,2048]{1,0:T(8,128)(2,1)S(1)} %pad_maximum_fusion.3), channel_id=1, source_target_pairs={{0,1},{1,0},{2,3},{3,2},{4,5},{5,4},{6,7},{7,6},{8,9},{9,8},{10,11... | collective-permute-start | bytes 786440 | tf_op jit(solution)/shard_map/ppermute | solution.py:291
  16.1 4.3 %copy-start = (bf16[256,512]{1,0:T(8,128)(2,1)S(1)}, bf16[256,512]{1,0:T(8,128)(2,1)}, u32[]{:S(2)}) copy-start(bf16[256,512]{1,0:T(8,128)(2,1)} %refs_2_.3) | copy-start | bytes 786436
  16.2 9.1 %collective-permute-start.8 = (bf16[384,512]{1,0:T(8,128)(2,1)S(1)}, bf16[384,512]{1,0:T(8,128)(2,1)S(1)}, u32[]{:S(2)}, u32[]{:S(2)}) collective-permute-start(bf16[384,512]{1,0:T(8,128)(2,1)S(1)} %pad_maximum_fusion.1), channel_id=1, source_target_pairs={{8,0},{16,8},{24,16},{28,24},{20,28},{12,20},{4,12},{0,4},{9,1},{1... | collective-permute-start | bytes 1179656 | tf_op jit(solution)/shard_map/ppermute | solution.py:294
  17.7 2.7 %copy-start.1 = (s32[1,4]{1,0:T(1,128)S(1)}, s32[1,4]{1,0:T(1,128)}, u32[]{:S(2)}) copy-start(s32[1,4]{1,0:T(1,128)} %refs_1_.11) | copy-start | bytes 52
  17.8 9.1 %collective-permute-start.5 = (bf16[384,512]{1,0:T(8,128)(2,1)S(1)}, bf16[384,512]{1,0:T(8,128)(2,1)S(1)}, u32[]{:S(2)}, u32[]{:S(2)}) collective-permute-start(bf16[384,512]{1,0:T(8,128)(2,1)S(1)} %pad_maximum_fusion), channel_id=1, source_target_pairs={{0,8},{8,16},{16,24},{24,28},{28,20},{20,12},{12,4},{4,0},{1,9},{9... | collective-permute-start | bytes 1179656 | tf_op jit(solution)/shard_map/ppermute | solution.py:294
  19.0 9.9 %collective-permute-start.14 = (bf16[64,2048]{1,0:T(8,128)(2,1)S(1)}, bf16[64,2048]{1,0:T(8,128)(2,1)S(1)}, u32[]{:S(2)}, u32[]{:S(2)}) collective-permute-start(bf16[64,2048]{1,0:T(8,128)(2,1)S(1)} %pad_maximum_fusion.4), channel_id=1, source_target_pairs={{0,2},{1,3},{2,0},{3,1},{4,6},{5,7},{6,4},{7,5},{8,10},{9,11},{10,... | collective-permute-start | bytes 786440 | tf_op jit(solution)/shard_map/ppermute | solution.py:291
  20.5 10.1 %collective-permute-start.15 = (bf16[64,2048]{1,0:T(8,128)(2,1)S(1)}, bf16[64,2048]{1,0:T(8,128)(2,1)S(1)}, u32[]{:S(2)}, u32[]{:S(2)}) collective-permute-start(bf16[64,2048]{1,0:T(8,128)(2,1)S(1)} %pad_maximum_fusion.5), channel_id=1, source_target_pairs={{0,3},{1,2},{2,1},{3,0},{4,7},{5,6},{6,5},{7,4},{8,11},{9,10},{10,... | collective-permute-start | bytes 786440 | tf_op jit(solution)/shard_map/ppermute | solution.py:291
  26.9 9.5 %collective-permute-start.11 = (bf16[384,512]{1,0:T(8,128)(2,1)S(1)}, bf16[384,512]{1,0:T(8,128)(2,1)S(1)}, u32[]{:S(2)}, u32[]{:S(2)}) collective-permute-start(bf16[384,512]{1,0:T(8,128)(2,1)S(1)} %collective-permute-done.8.refs_3_), channel_id=1, source_target_pairs={{8,0},{16,8},{24,16},{28,24},{20,28},{12,20},{4,12},{0,4},{9,1},{1... | collective-permute-start | bytes 1179656 | tf_op jit(solution)/shard_map/ppermute | solution.py:294
  28.5 9.5 %collective-permute-start.10 = (bf16[384,512]{1,0:T(8,128)(2,1)S(1)}, bf16[384,512]{1,0:T(8,128)(2,1)S(1)}, u32[]{:S(2)}, u32[]{:S(2)}) collective-permute-start(bf16[384,512]{1,0:T(8,128)(2,1)S(1)} %collective-permute-done.5.refs_2_), channel_id=1, source_target_pairs={{0,8},{8,16},{16,24},{24,28},{28,20},{20,12},{12,4},{4,0},{1,9},{9... | collective-permute-start | bytes 1179656 | tf_op jit(solution)/shard_map/ppermute | solution.py:294
  36.4 10.0 %collective-permute-start.13 = (bf16[192,512]{1,0:T(8,128)(2,1)S(1)}, bf16[192,512]{1,0:T(8,128)(2,1)S(1)}, u32[]{:S(2)}, u32[]{:S(2)}) collective-permute-start(bf16[192,512]{1,0:T(8,128)(2,1)S(1)} %slice.39), channel_id=1, source_target_pairs={{8,0},{16,8},{24,16},{28,24},{20,28},{12,20},{4,12},{0,4},{9,1},{1... | collective-permute-start | bytes 589832 | tf_op jit(solution)/shard_map/ppermute | solution.py:294
  37.9 8.4 %collective-permute-start.12 = (bf16[192,512]{1,0:T(8,128)(2,1)S(1)}, bf16[192,512]{1,0:T(8,128)(2,1)S(1)}, u32[]{:S(2)}, u32[]{:S(2)}) collective-permute-start(bf16[192,512]{1,0:T(8,128)(2,1)S(1)} %slice.38), channel_id=1, source_target_pairs={{0,8},{8,16},{16,24},{24,28},{28,20},{20,12},{12,4},{4,0},{1,9},{9... | collective-permute-start | bytes 589832 | tf_op jit(solution)/shard_map/ppermute | solution.py:294
  50.4 4.0 %collective-permute-start.16 = (bf16[64,2048]{1,0:T(8,128)(2,1)S(1)}, bf16[64,2048]{1,0:T(8,128)(2,1)S(1)}, u32[]{:S(2)}, u32[]{:S(2)}) collective-permute-start(bf16[64,2048]{1,0:T(8,128)(2,1)S(1)} %get-tuple-element.49), channel_id=1, source_target_pairs={{0,1},{1,0},{2,3},{3,2},{4,5},{5,4},{6,7},{7,6},{8,9},{9,8},{10,11... | collective-permute-start | bytes 786440 | tf_op jit(solution)/shard_map/ppermute | solution.py:291
  52.5 9.2 %collective-permute-start.17 = (bf16[64,2048]{1,0:T(8,128)(2,1)S(1)}, bf16[64,2048]{1,0:T(8,128)(2,1)S(1)}, u32[]{:S(2)}, u32[]{:S(2)}) collective-permute-start(bf16[64,2048]{1,0:T(8,128)(2,1)S(1)} %get-tuple-element.54), channel_id=1, source_target_pairs={{0,2},{1,3},{2,0},{3,1},{4,6},{5,7},{6,4},{7,5},{8,10},{9,11},{10,... | collective-permute-start | bytes 786440 | tf_op jit(solution)/shard_map/ppermute | solution.py:291
  53.9 12.5 %collective-permute-start.18 = (bf16[64,2048]{1,0:T(8,128)(2,1)S(1)}, bf16[64,2048]{1,0:T(8,128)(2,1)S(1)}, u32[]{:S(2)}, u32[]{:S(2)}) collective-permute-start(bf16[64,2048]{1,0:T(8,128)(2,1)S(1)} %get-tuple-element.55), channel_id=1, source_target_pairs={{0,3},{1,2},{2,1},{3,0},{4,7},{5,6},{6,5},{7,4},{8,11},{9,10},{10,... | collective-permute-start | bytes 786440 | tf_op jit(solution)/shard_map/ppermute | solution.py:291
